TPU v7x, 32 devices: a whole 2x2x4 slice. The times are simulated.
32 devices in a mesh: rxn: 4 (over y, core), col: 8 (over z, x).
Axes of the slice: x: 2, y: 2, z: 4, core: 2. Of those that a mesh axis runs over, the one named last changes fastest.
Arguments:
- basis: bfloat16 [12288, 16384], P('rxn', 'col'), may hold values from -8 to 8, as said below
- lower_slack: float32 [12288], P('rxn'), may hold values from 0.5 to 4
- upper_slack: float32 [12288], P('rxn'), may hold values from 0.5 to 4
Outputs:
- panel_factor: float32 [16384, 256], P(('col', 'rxn'))
Inputs may be any that keep to these rules, and one draw needn't show every extreme that they name: `basis`: finite real entries of order one.
All inputs are finite; a program needn't handle non-finite values.
Results may differ from a plain program's by a relative error of at most 0.00045.
Values may be sent and summed in bfloat16 or wider, within the bound.
No kernel may reach another device: no remote copies, remote signals or barrier semaphores. Data moves between devices by JAX's collectives and lax.ppermute only.
A program may use at most 64 MiB of HBM per device.

v0:
```python
import jax
import jax.numpy as jnp
from jax import lax
from jax.sharding import PartitionSpec as P

PANEL = 256


def from_root(value, axis, source):
    kept = jnp.where(lax.axis_index(axis) == source, value, 0).astype(value.dtype)
    return lax.psum(kept, axis)


def on_device(basis, lower_slack, upper_slack):
    width = basis.shape[0]
    total = width * lax.axis_size("rxn")
    weight = 1.0 / (lower_slack * lower_slack) + 1.0 / (upper_slack * upper_slack)
    scaled = weight / jnp.float32(total)
    panel = from_root(basis[:, :PANEL], "col", 0)
    weighted = (panel.astype(jnp.float32) * scaled[:, None]).astype(jnp.bfloat16)
    contract = (((0,), (0,)), ((), ()))
    diag_part = lax.dot_general(panel, weighted, contract, preferred_element_type=jnp.float32)
    diag_block = lax.psum(diag_part, "rxn")
    factor = jnp.linalg.cholesky(diag_block)
    identity = jnp.eye(PANEL, dtype=jnp.float32)
    inverse = lax.linalg.triangular_solve(factor, identity, left_side=True, lower=True)
    share = basis.shape[1] // lax.axis_size("rxn")
    partial_gram = lax.dot_general(basis, weighted, contract, preferred_element_type=jnp.float32)
    summed = lax.psum(partial_gram, "rxn")
    first_row = lax.axis_index("rxn") * share
    mine = lax.dynamic_slice_in_dim(summed, first_row, share, 0)
    return jnp.dot(mine, inverse.T, precision=lax.Precision.HIGHEST)


def solution(mesh):
    return jax.shard_map(
        on_device,
        mesh=mesh,
        in_specs=(P("rxn", "col"), P("rxn"), P("rxn")),
        out_specs=P(("col", "rxn"), None),
        check_vma=False,
    )
```

profile of v0, /device:TPU:0, one launch (start us, length us, event | category | flops | bytes accessed | tf_op | source)
XLA Modules:
  0.0 242.0 jit_solution(16826513850945508790)
XLA Ops:
  6.5 0.0 all-reduce.5.cloned.1.call-start
  6.5 0.0 copy-start.1
  6.5 0.0 copy-start.2
  6.5 2.7 %slice_select_fusion = bf16[3072,256]{1,0:T(8,128)(2,1)} fusion(bf16[3072,2048]{1,0:T(8,128)(2,1)} %param.3, pred[]{:T(512)S(6)} %eq.8), kind=kLoop, calls=%fused_computation.7 | loop fusion | flops 786432 | bytes 3145729 | tf_op jit(solution)/shard_map/jit(_where)/select_n | solution.py:10
  9.2 0.0 all-reduce.5.cloned.1.call-update
  9.2 0.0 all-reduce.7.cloned.1.call-start
  9.3 0.0 copy-done.1
  9.3 0.0 copy-done.2
  9.3 93.2 %all-reduce.5.cloned.1.call-done = bf16[3072,256]{1,0:T(8,128)(2,1)} async-done(((bf16[3072,256]{1,0:T(8,128)(2,1)}), bf16[3072,256]{1,0:T(8,128)(2,1)}) %all-reduce.5.cloned.1.call-update) | async-done | bytes 1572880 | tf_op jit(solution)/shard_map/psum | solution.py:11
  102.5 0.0 copy-start
  102.5 10.0 %convolution_bitcast_fusion = f32[2048,256]{0,1:T(8,128)} fusion(bf16[3072,2048]{1,0:T(8,128)(2,1)} %param.3, bf16[3072,256]{1,0:T(8,128)(2,1)} %all-reduce.5.cloned.1.call-done, f32[3072]{0:T(1024)S(1)} %add_multiply_fusion), kind=kOutput, calls=%fused_computation.3 | convolution fusion | flops 3223584768 | bytes 16265216 | tf_op jit(solution)/shard_map/dot_general | solution.py:28
  112.5 0.0 copy-done
  112.5 1.9 fusion
  114.4 0.0 all-reduce.7.cloned.1.call-update
  114.5 55.3 %all-reduce.7.cloned.1.call-done = (f32[2048,256]{0,1:T(8,128)}, f32[256,256]{0,1:T(8,128)}) async-done(((f32[2048,256]{0,1:T(8,128)}, f32[256,256]{0,1:T(8,128)}), (f32[2048,256]{0,1:T(8,128)}, f32[256,256]{0,1:T(8,128)})) %all-reduce.7.cloned.1.call-update) | async-done | bytes 2359312 | tf_op jit(solution)/shard_map/psum | solution.py:29
  169.8 1.1 copy.5
  170.9 1.0 fusion.8
  171.9 11.7 %cholesky.50 = f32[128,128]{1,0:T(8,128)S(1)} custom-call(f32[128,128]{1,0:T(8,128)S(1)} %cholesky.118), custom_call_target="Cholesky" | custom-call | tf_op jit(solution)/shard_map/jit(cholesky)/cholesky | solution.py:24
  183.6 9.8 %custom-call.14 = f32[1,128,128]{1,2,0:T(8,128)S(1)} custom-call(f32[1,128,128]{2,1,0:T(8,128)S(1)} %get-tuple-element.28), custom_call_target="InvertDiagBlocksLowerTriangular" | custom-call | tf_op jit(solution)/shard_map/jit(cholesky)/cholesky | solution.py:24
  193.5 0.2 constant_dynamic-update-slice_fusion.1
  193.7 0.3 convolution_subtract_fusion.1
  193.9 11.9 %cholesky.105 = f32[128,128]{1,0:T(8,128)S(1)} custom-call(f32[128,128]{1,0:T(8,128)S(1)} %convolution_subtract_fusion.1), custom_call_target="Cholesky" | custom-call | tf_op jit(solution)/shard_map/jit(cholesky)/cholesky | solution.py:24
  205.8 0.7 compare_reduce_fusion
  207.8 0.1 triangular_solve.63
  207.9 3.9 %while.1 = (s32[]{:T(128)}, f32[256,256]{1,0:T(8,128)S(1)}, s32[2,2]{1,0:T(2,128)S(1)}, f32[2,128,128]{2,1,0:T(8,128)S(1)}, s32[]{:T(128)}) while((s32[]{:T(128)}, f32[256,256]{1,0:T(8,128)S(1)}, s32[2,2]{1,0:T(2,128)S(1)}, f32[2,128,128]{2,1,0:T(8,128)S(1)}, s32[]{:T(128)}) %tuple.23), condition=%wide.while_cond, body=%wide.while_body.sunk | while | flops 2 | bytes 131181 | solution.py:26
  207.9 0.6 fusion.26
  208.5 1.4 bitcast_dynamic-update-slice_fusion.2
  209.8 0.6 fusion.26
  210.4 1.4 bitcast_dynamic-update-slice_fusion.2
  211.8 19.7 %custom-call.15 = f32[2,128,128]{1,2,0:T(8,128)S(1)} custom-call(f32[2,128,128]{2,1,0:T(8,128)S(1)} %get-tuple-element.12), custom_call_target="InvertDiagBlocksLowerTriangular" | custom-call | tf_op jit(solution)/shard_map/triangular_solve | solution.py:26
  231.5 0.3 fusion.9
  231.8 0.3 convolution_subtract_fusion
  232.0 0.3 fusion.12
  232.3 2.8 %fusion.3 = f32[512,256]{1,0:T(8,128)} fusion(f32[2048,256]{0,1:T(8,128)} %get-tuple-element.21, s32[]{:T(128)S(6)} %select_n.17, f32[128,256]{1,0:T(8,128)S(1)} %fusion.12, f32[128,256]{1,0:T(8,128)S(1)} %fusion.9), kind=kOutput, calls=%fused_computation.10 | convolution fusion | flops 402718720 | bytes 1310724 | tf_op jit(solution)/shard_map/dot_general | solution.py:32
  (11 shorter events, 0.2 us)
Async XLA Ops:
  6.5 96.0 %all-reduce.5.cloned.1.call-start = ((), (), s32[]{:S(2)}) async-start(), calls=%async_computation | async-start | bytes 3145728 | tf_op jit(solution)/shard_map/psum | solution.py:11
  6.5 2.8 %copy-start.1 = (f32[3072]{0:T(1024)S(1)}, f32[3072]{0:T(1024)}, u32[]{:S(2)}) copy-start(f32[3072]{0:T(1024)} %param.5) | copy-start | bytes 36868
  6.5 2.8 %copy-start.2 = (f32[3072]{0:T(1024)S(1)}, f32[3072]{0:T(1024)}, u32[]{:S(2)}) copy-start(f32[3072]{0:T(1024)} %param.4) | copy-start | bytes 36868
  9.2 160.5 %all-reduce.7.cloned.1.call-start = ((), (), s32[]{:S(2)}) async-start(), calls=%async_computation.1 | async-start | bytes 4718592 | tf_op jit(solution)/shard_map/psum | solution.py:29
  102.5 10.0 %copy-start = (bf16[3072,256]{1,0:T(8,128)(2,1)S(1)}, bf16[3072,256]{1,0:T(8,128)(2,1)}, u32[]{:S(2)}) copy-start(bf16[3072,256]{1,0:T(8,128)(2,1)} %all-reduce.5.cloned.1.call-done) | copy-start | bytes 4718596
Sparse Core Ops, SparseCore 0:
  10.9 91.5 all-reduce.4
  114.6 55.1 all-reduce.6
where the time goes:
time: 242 us
  waiting for transfers between devices  148 us (61%)
  other arithmetic  57.5 us (24%)
  matrix products  16.1 us (7%)
  between operations  14.8 us (6%)
  local copies, waits for them, and re-layouts  5.08 us (2%)
    psum x1, waiting for transfers between devices, from_root(): return lax.psum(kept, axis)  93.2 us
    psum x1, waiting for transfers between devices, on_device(): summed = lax.psum(partial_gram, 'rxn')  55.3 us
    another operation x6, other arithmetic, on_device(): factor = jnp.linalg.cholesky(diag_block)  34.1 us
    another operation x3, other arithmetic, on_device(): lax.linalg.triangular_solve(factor, identity, left_side=True, lower=True)  19.7 us
    dot_general x1, matrix products, on_device(): lax.dot_general(basis, weighted, contract, preferred_element_type=jnp.flo...  9.99 us
  transfers between devices with their start and end apart: 2, of which 2 were waited for; matrix products, arithmetic and copies ran while one was open for 0% of the time, Pallas kernels for 0%

commit v1 on v0

v1 whole, which is shorter than its diff:
```python
import functools

import jax
import jax.numpy as jnp
from jax import lax
from jax.experimental import pallas as pl
from jax.experimental.pallas import tpu as pltpu
from jax.sharding import PartitionSpec as P

PANEL = 256
HALF = PANEL // 2
LANES = 128
BLOCK = 64
STRIP = 8
WIRE_SCALE = 1024.0
COLUMN, CORE, AT, BLOCKS = 0, 1, 2, 3
HIGHEST = lax.Precision.HIGHEST
F32 = jnp.float32
PARAMS = pltpu.CompilerParams(vmem_limit_bytes=16 * 2**20)


def ring_order(columns):
    return list(range(0, columns, 2)) + list(range(columns - 1, 0, -2))


def reverse_bits(value, count):
    out, bit = 0, 1
    while bit < count:
        out = out * 2 + (1 if value & bit else 0)
        bit *= 2
    return out


def to_column(value, pairs):
    return lax.ppermute(value, "col", pairs)


def swap(value, bit):
    size = lax.axis_size("rxn")
    return lax.ppermute(value, "rxn", [(i, i ^ bit) for i in range(size)])


def prepare_kernel(total, count, where_ref, panel_ref, lower_ref, upper_ref, *refs):
    pieces, (keep_ref, send_ref, diag_ref) = refs[:count], refs[count:]
    depth = pieces[0].shape[1]
    low, up = lower_ref[...], upper_ref[...]
    scaled = (1.0 / (low * low) + 1.0 / (up * up)) / total
    diag = jnp.zeros((PANEL, PANEL), F32)
    for line in range(scaled.shape[0]):
        panel = panel_ref[line * LANES : (line + 1) * LANES, :]
        weighted = (panel.astype(F32).T * scaled[line : line + 1, :]).astype(jnp.bfloat16)
        diag += jnp.dot(weighted, panel, preferred_element_type=F32)
        start = line * LANES
        while start < (line + 1) * LANES:
            piece, inside = divmod(start, depth)
            end = min((line + 1) * LANES, (piece + 1) * depth)
            part = weighted[:, start - line * LANES : end - line * LANES]
            if piece == 0:
                part = jnp.where(where_ref[COLUMN] == 0, part.astype(F32), 0.0).astype(jnp.bfloat16)
            pieces[piece][:, inside : inside + end - start] = part
            start = end
    diag_ref[...] = diag
    core = where_ref[CORE]
    keep_ref[...] = diag_ref[pl.ds(pl.multiple_of(core * HALF, HALF), HALF), :]
    send_ref[...] = diag_ref[pl.ds(pl.multiple_of((1 - core) * HALF, HALF), HALF), :]


def prepare(place, basis, lower, upper, total, count):
    rows = basis.shape[0]
    depth = rows // count
    piece = jax.ShapeDtypeStruct((PANEL, depth), jnp.bfloat16)
    half = jax.ShapeDtypeStruct((HALF, PANEL), F32)
    whole = lambda *shape: pl.BlockSpec(shape, lambda i, s: (0, 0))
    lines = rows // LANES
    slacks = [x.reshape(lines, LANES) for x in (lower, upper)]
    return pl.pallas_call(
        functools.partial(prepare_kernel, float(total), count),
        out_shape=[piece] * count + [half, half],
        grid_spec=pltpu.PrefetchScalarGridSpec(
            num_scalar_prefetch=1,
            grid=(1,),
            in_specs=[whole(rows, PANEL), whole(lines, LANES), whole(lines, LANES)],
            out_specs=[whole(PANEL, depth)] * count + [whole(HALF, PANEL)] * 2,
            scratch_shapes=[pltpu.VMEM((PANEL, PANEL), F32)],
        ),
        compiler_params=PARAMS,
        name="prepare",
    )(place, *[pltpu.with_memory_space_constraint(x, pltpu.HBM) for x in (basis, *slacks)])


def eliminate(work):
    done, width = [], work.shape[1]
    for start in range(0, work.shape[0], STRIP):
        rows = work.shape[0]
        row = lax.broadcasted_iota(jnp.int32, (rows, width), 0)
        column = [jnp.broadcast_to(work[:, start + j : start + j + 1], (rows, width)) for j in range(STRIP)]
        for k in range(STRIP):
            root = lax.rsqrt(column[k][k : k + 1, :])
            pivot_row = work[k : k + 1, :] * root
            below = jnp.where(row > k, column[k] * root, 0.0)
            work = jnp.where(row == k, pivot_row, work - below * pivot_row)
            for j in range(k + 1, STRIP):
                column[j] = column[j] - below * (column[j][k : k + 1, :] * root)
        done.append(work[:STRIP])
        work = work[STRIP:]
    return jnp.concatenate(done, 0)


def invert_kernel(where_ref, mine_ref, other_ref, out_ref, work):
    out_ref[...] = jnp.zeros_like(out_ref)

    @pl.when(where_ref[COLUMN] == 0)
    def _():
        invert_diagonal(where_ref[CORE], mine_ref, other_ref, out_ref, work)


def invert_diagonal(core, mine_ref, other_ref, out_ref, work):
    mine = pl.ds(pl.multiple_of(core * HALF, HALF), HALF)
    other = pl.ds(pl.multiple_of((1 - core) * HALF, HALF), HALF)
    work[mine, :PANEL] = mine_ref[...]
    work[other, :PANEL] = other_ref[...]
    row = lax.broadcasted_iota(jnp.int32, (PANEL, PANEL), 0)
    col = lax.broadcasted_iota(jnp.int32, (PANEL, PANEL), 1)
    work[:, PANEL:] = jnp.where(row == col, 1.0, 0.0).astype(F32)
    row = lax.broadcasted_iota(jnp.int32, (BLOCK, 128), 0)
    col = lax.broadcasted_iota(jnp.int32, (BLOCK, 128), 1)
    for low in range(0, PANEL, BLOCK):
        base = low // 128 * 128
        square = work[low : low + BLOCK, base : base + 128]
        if low > base:
            square = pltpu.roll(square, 128 - (low - base), 1)
        square = jnp.where(col < BLOCK, square, jnp.where(col - BLOCK == row, 1.0, 0.0))
        corner = pltpu.roll(eliminate(square), 128 - BLOCK, 1)[:, :BLOCK]
        end = PANEL + (low + BLOCK + 127) // 128 * 128
        scaled = jnp.dot(corner, work[low : low + BLOCK, base:end], precision=HIGHEST, preferred_element_type=F32)
        work[low : low + BLOCK, base:end] = scaled
        rest = low + BLOCK
        if rest < PANEL:
            left = rest // 128 * 128
            update = lax.dot_general(
                scaled[:, left - base : PANEL - base],
                scaled[:, left - base :],
                (((0,), (0,)), ((), ())),
                precision=HIGHEST,
                preferred_element_type=F32,
            )
            work[rest:PANEL, left:end] = work[rest:PANEL, left:end] - update[rest - left :]
    row = lax.broadcasted_iota(jnp.int32, (HALF, PANEL), 0) + core * HALF
    col = lax.broadcasted_iota(jnp.int32, (HALF, PANEL), 1)
    out_ref[...] = jnp.where(row >= col, work[mine, PANEL:], 0.0)


def invert(place, mine, other):
    half = pl.BlockSpec((HALF, PANEL), lambda i, s: (0, 0))
    return pl.pallas_call(
        invert_kernel,
        out_shape=jax.ShapeDtypeStruct((HALF, PANEL), F32),
        grid_spec=pltpu.PrefetchScalarGridSpec(
            num_scalar_prefetch=1,
            grid=(1,),
            in_specs=[half, half],
            out_specs=half,
            scratch_shapes=[pltpu.VMEM((PANEL, 2 * PANEL), F32)],
        ),
        compiler_params=PARAMS,
        cost_estimate=pl.CostEstimate(flops=8 * 10**9, bytes_accessed=2**19, transcendentals=0),
        name="invert",
    )(place, mine, other)


def gram_kernel(count, has_total, where_ref, *refs):
    pieces, tiles, rest = refs[:count], refs[count : 2 * count], refs[2 * count :]
    total = rest[0][0] if has_total else None
    for piece, tile in zip(pieces, tiles):
        term = jnp.dot(piece[...], tile[...], preferred_element_type=F32)
        total = term if total is None else total + term
    rest[-1][0] = total


def add_gram(place, basis, total, pieces, offsets, shares, columns, first, count):
    rows, cols = basis.shape
    depth, share, number = rows // columns, cols // shares, len(pieces)
    tile = lambda offset: pl.BlockSpec(
        (depth, share), lambda j, s: (lax.rem(s[AT] + (offset + columns), columns), s[BLOCKS + first + j])
    )
    piece = pl.BlockSpec((PANEL, depth), lambda j, s: (0, 0))
    in_specs = [piece] * number + [tile(offset) for offset in offsets]
    operands = [*pieces, *([basis] * number)]
    if total is not None:
        in_specs.append(pl.BlockSpec((1, PANEL, share), lambda j, s: (first + j, 0, 0)))
        operands.append(total)
    return pl.pallas_call(
        functools.partial(gram_kernel, number, total is not None),
        out_shape=jax.ShapeDtypeStruct((count, PANEL, share), F32),
        grid_spec=pltpu.PrefetchScalarGridSpec(
            num_scalar_prefetch=1,
            grid=(count,),
            in_specs=in_specs,
            out_specs=pl.BlockSpec((1, PANEL, share), lambda j, s: (j, 0, 0)),
        ),
        compiler_params=PARAMS,
        input_output_aliases={2 * number + 1: 0} if total is not None and count == shares else {},
        cost_estimate=pl.CostEstimate(
            flops=2 * number * depth * PANEL * share * count,
            bytes_accessed=count * (number * depth * share * 2 + 8 * PANEL * share),
            transcendentals=0,
        ),
        name="gram",
    )(place, *operands)


def transform_kernel(where_ref, mine_ref, other_ref, kept_ref, came_ref, out_ref, inverse):
    core = where_ref[CORE]
    inverse[pl.ds(pl.multiple_of(core * HALF, HALF), HALF), :] = mine_ref[...]
    inverse[pl.ds(pl.multiple_of((1 - core) * HALF, HALF), HALF), :] = other_ref[...]
    gram = (kept_ref[0] + came_ref[0]).T
    out_ref[0] = lax.dot_general(
        gram, inverse[...], (((1,), (1,)), ((), ())), precision=HIGHEST, preferred_element_type=F32
    )


def transform(place, mine, other, kept, came):
    count, _, share = kept.shape
    half = pl.BlockSpec((HALF, PANEL), lambda j, s: (0, 0))
    gram = pl.BlockSpec((1, PANEL, share), lambda j, s: (j, 0, 0))
    return pl.pallas_call(
        transform_kernel,
        out_shape=jax.ShapeDtypeStruct((count, share, PANEL), F32),
        grid_spec=pltpu.PrefetchScalarGridSpec(
            num_scalar_prefetch=1,
            grid=(count,),
            in_specs=[half, half, gram, gram],
            out_specs=pl.BlockSpec((1, share, PANEL), lambda j, s: (j, 0, 0)),
            scratch_shapes=[pltpu.VMEM((PANEL, PANEL), F32)],
        ),
        compiler_params=PARAMS,
        name="transform",
    )(place, mine, other, kept, came)


def on_device(basis, lower_slack, upper_slack):
    rows = basis.shape[0]
    shares, columns = lax.axis_size("rxn"), lax.axis_size("col")
    me, column = lax.axis_index("rxn"), lax.axis_index("col")
    order = ring_order(columns)
    relay, middle = order[-1], columns // 2
    at = sum(jnp.where(column == c, p, 0) for p, c in enumerate(order))
    blocks = [me ^ reverse_bits(j, shares) for j in range(shares)]
    place = jnp.stack([column, me % 2, at, *blocks]).astype(jnp.int32)
    *pieces, keep, send = prepare(place, basis, lower_slack, upper_slack, rows * shares, columns)
    basis = pltpu.with_memory_space_constraint(basis, pltpu.VMEM)

    half = keep + swap(send, 1)
    half, *pieces[1:] = lax.optimization_barrier((half, *pieces[1:]))
    bit = 2
    while bit < shares:
        half = half + swap(half, bit)
        bit *= 2

    through = list(range(middle + 1, columns - 1))
    near = list(range(1, middle + 1))
    to_relay = lambda p: to_column(pieces[p], [(0, relay)])
    direct = lambda p: to_column(pieces[p], [(0, order[p])])
    far = [to_relay(p) for p in through]
    parts = [pieces[0]] + [direct(p) for p in near[:-2]]
    late = [*near[-2:], columns - 1]
    half, *moved = lax.optimization_barrier((half, *[pieces[p] for p in late]))
    for p, x in zip(late, moved):
        pieces[p] = x
    other = swap(half, 1)
    parts += [direct(near[-2]), to_relay(columns - 1), direct(near[-1])]
    inverse = invert(place, half, other)
    inverse, *far = lax.optimization_barrier((inverse, *far))
    parts += [to_column(x, [(relay, order[p])]) for x, p in zip(far, through)]
    held = functools.reduce(lambda a, b: a + b, parts)

    forward = [(order[i], order[(i + 1) % columns]) for i in range(columns)]
    backward = [(b, a) for a, b in forward]
    holders, strides = [0], [1] + [columns >> i for i in range(1, columns.bit_length() - 1)]
    gram = lambda total, pending, first, count: add_gram(
        place, basis, total, *zip(*pending), shares, columns, first, count
    )
    pending, total = [(held, 0)], None
    ahead = back = held
    for step in range(1, middle + 1):
        ahead = to_column(ahead, forward)
        came = [(ahead, -step)]
        if step < middle:
            back = to_column(back, backward)
            came.append((back, step))
        if strides:
            stride = strides.pop(0)
            inverse = inverse + to_column(inverse, [(i, i + stride) for i in holders])
            holders += [i + stride for i in holders]
        total, pending = gram(total, pending, 0, shares), came
        if step < middle:
            ahead, back, inverse, total = lax.optimization_barrier((ahead, back, inverse, total))
    inverse_other = swap(inverse, 1)

    quarter = shares // 4
    finish = lambda q: gram(total, pending, q * quarter, quarter)
    came = swap(finish(3), 1)
    away = transform(place, inverse, inverse_other, finish(1), came)
    came = swap(finish(2), 1)
    mine = transform(place, inverse, inverse_other, finish(0), came)
    bit = 2
    while True:
        mine = mine + swap((away * WIRE_SCALE).astype(jnp.float16), bit).astype(F32) * (1.0 / WIRE_SCALE)
        if mine.shape[0] == 1:
            return mine[0]
        half = mine.shape[0] // 2
        mine, away = mine[:half], mine[half:]
        bit *= 2


def solution(mesh):
    return jax.shard_map(
        on_device,
        mesh=mesh,
        in_specs=(P("rxn", "col"), P("rxn"), P("rxn")),
        out_specs=P(("col", "rxn"), None),
        check_vma=False,
    )
```

time: 242 us -> 86.3 us (0.36)
  waiting for transfers between devices: 148 us -> 19.4 us
  other arithmetic: 57.5 us -> 1.07 us
  starting transfers between devices: 0.04 us -> 36.9 us
  Pallas kernels: 0 us -> 28 us
  matrix products: 16.1 us -> 0 us
  between operations: 14.8 us -> 0.43 us
  local copies, waits for them, and re-layouts: 5.08 us -> 0.1 us
    psum x2 -> x0, waiting for transfers between devices: 148 us -> none  [the longest x1 93.2 us: from_root(): return lax.psum(kept, axis)]
    another operation x9 -> x0, other arithmetic: 53.8 us -> none  [the longest x6 34.1 us: on_device(): factor = jnp.linalg.cholesky(diag_block)]
    ppermute x0 -> x26, starting transfers between devices: none -> 36.9 us  [the longest x19 31.1 us: to_column(): return lax.ppermute(value, 'col', pairs)]
    pallas_call x0 -> x12, Pallas kernels: none -> 28 us  [the longest x8 13.2 us: add_gram(): pl.pallas_call(functools.partial(gram_kernel, number, total is not None),...]
    ppermute x0 -> x26, waiting for transfers between devices: none -> 19.4 us  [the longest x7 9.86 us: swap(): return lax.ppermute(value, 'rxn', [(i, i ^ bit) for i in range(size)])]
    dot_general x3 -> x0, matrix products: 14.7 us -> none  [the longest x1 9.99 us: on_device(): lax.dot_general(basis, weighted, contract, preferred_element_type=jnp.flo...]
    another operation x9 -> x1, local copies, waits for them, and re-layouts: 3.99 us -> 0.08 us  [on_device(): place = jnp.stack([column, me % 2, at, *blocks]).astype(jnp.int32)]
    select_n x1 -> x0, other arithmetic: 2.68 us -> none  [from_root(): jnp.where(lax.axis_index(axis) == source, value, 0).astype(value.dtype)]
  transfers between devices with their start and end apart: 2 -> 26, of which waited for: 2 -> 9; matrix products, arithmetic and copies ran while one was open for 0% -> 0% of each run, Pallas kernels for 0% -> 28%
where the time goes in v1:
time: 86.3 us; the launch traced here: 85.9 us
  starting transfers between devices  36.9 us (43%)
  Pallas kernels  28 us (32%)
  waiting for transfers between devices  19.4 us (22%)
  other arithmetic  1.07 us (1%)
    ppermute x19, starting transfers between devices, to_column(): return lax.ppermute(value, 'col', pairs)  31.1 us
    pallas_call x8, Pallas kernels, add_gram(): pl.pallas_call(functools.partial(gram_kernel, number, total is not None),...  13.2 us
    ppermute x7, waiting for transfers between devices, swap(): return lax.ppermute(value, 'rxn', [(i, i ^ bit) for i in range(size)])  9.86 us
    ppermute x19, waiting for transfers between devices, to_column(): return lax.ppermute(value, 'col', pairs)  9.57 us
    pallas_call x1, Pallas kernels, invert(): pl.pallas_call(invert_kernel, out_shape=jax.ShapeDtypeStruct((HALF, PANEL...  9.35 us
    ppermute x7, starting transfers between devices, swap(): return lax.ppermute(value, 'rxn', [(i, i ^ bit) for i in range(size)])  5.84 us
    pallas_call x1, Pallas kernels, prepare(): pl.pallas_call(functools.partial(prepare_kernel, float(total), count), ou...  3.03 us
    pallas_call x2, Pallas kernels, transform(): pl.pallas_call(transform_kernel, out_shape=jax.ShapeDtypeStruct((count, s...  2.39 us
  transfers between devices with their start and end apart: 26, of which 9 were waited for; matrix products, arithmetic and copies ran while one was open for 0% of the time, Pallas kernels for 28%

profile of v1, /device:TPU:0, one launch (start us, length us, event | category | flops | bytes accessed | tf_op | source)
XLA Modules:
  0.0 85.9 jit_solution(8100889585815585630)
XLA Ops:
  0.0 0.1 stack.31.where_ref
  0.1 3.0 %prepare.1 = (bf16[256,384]{1,0:T(8,128)(2,1)S(1)}, bf16[256,384]{1,0:T(8,128)(2,1)S(1)}, bf16[256,384]{1,0:T(8,128)(2,1)S(1)}, bf16[256,384]{1,0:T(8,128)(2,1)S...) custom-call(s32[7]{0:T(128)S(1)} %stack.31.where_ref, ...), custom_call_target="tpu_custom_call" | custom-call | tf_op jit(solution)/shard_map/prepare/pallas_call | solution.py:76
  3.1 0.5 collective-permute-start
  3.6 1.0 %collective-permute-done = f32[128,256]{1,0:T(8,128)S(1)} collective-permute-done((f32[128,256]{1,0:T(8,128)S(1)}, f32[128,256]{1,0:T(8,128)S(1)}, u32[]{:S(2)}, u32[]{:S(2)}) %collective-permute-start) | collective-permute-done | bytes 131104 | tf_op jit(solution)/shard_map/ppermute | solution.py:40
  4.6 2.9 %collective-permute-start.3 = (f32[128,256]{1,0:T(8,128)S(1)}, f32[128,256]{1,0:T(8,128)S(1)}, u32[]{:S(2)}, u32[]{:S(2)}) collective-permute-start(f32[128,256]{1,0:T(8,128)S(1)} %add.69), channel_id=1, source_target_pairs={{0,16},{8,24},{16,0},{24,8},{1,17},{9,25},{17,1},{25,9},{2,18},{10... | collective-permute-start | bytes 393224 | tf_op jit(solution)/shard_map/ppermute | solution.py:40
  7.6 3.8 %collective-permute-done.3 = f32[128,256]{1,0:T(8,128)S(1)} collective-permute-done((f32[128,256]{1,0:T(8,128)S(1)}, f32[128,256]{1,0:T(8,128)S(1)}, u32[]{:S(2)}, u32[]{:S(2)}) %collective-permute-start.3) | collective-permute-done | bytes 131104 | tf_op jit(solution)/shard_map/ppermute | solution.py:40
  11.4 0.0 slice-start.1
  11.4 0.1 collective-permute-start.7
  11.5 4.0 %collective-permute-start.8 = (bf16[256,384]{1,0:T(8,128)(2,1)S(1)}, bf16[256,384]{1,0:T(8,128)(2,1)S(1)}, u32[]{:S(2)}, u32[]{:S(2)}) collective-permute-start(bf16[256,384]{1,0:T(8,128)(2,1)S(1)} %get-tuple-element.61), channel_id=1, source_target_pairs={{0,1},{8,9},{16,17},{24,25}} | collective-permute-start | bytes 589832 | tf_op jit(solution)/shard_map/ppermute | solution.py:35
  15.6 1.4 %collective-permute-start.9 = (bf16[256,384]{1,0:T(8,128)(2,1)S(1)}, bf16[256,384]{1,0:T(8,128)(2,1)S(1)}, u32[]{:S(2)}, u32[]{:S(2)}) collective-permute-start(bf16[256,384]{1,0:T(8,128)(2,1)S(1)} %get-tuple-element.62), channel_id=1, source_target_pairs={{0,1},{8,9},{16,17},{24,25}} | collective-permute-start | bytes 589832 | tf_op jit(solution)/shard_map/ppermute | solution.py:35
  17.0 1.3 %collective-permute-start.1 = (bf16[256,384]{1,0:T(8,128)(2,1)S(1)}, bf16[256,384]{1,0:T(8,128)(2,1)S(1)}, u32[]{:S(2)}, u32[]{:S(2)}) collective-permute-start(bf16[256,384]{1,0:T(8,128)(2,1)S(1)} %get-tuple-element.51), channel_id=1, source_target_pairs={{0,2},{8,10},{16,18},{24,26}} | collective-permute-start | bytes 589832 | tf_op jit(solution)/shard_map/ppermute | solution.py:35
  18.3 1.3 %collective-permute-start.2 = (bf16[256,384]{1,0:T(8,128)(2,1)S(1)}, bf16[256,384]{1,0:T(8,128)(2,1)S(1)}, u32[]{:S(2)}, u32[]{:S(2)}) collective-permute-start(bf16[256,384]{1,0:T(8,128)(2,1)S(1)} %get-tuple-element.52), channel_id=1, source_target_pairs={{0,4},{8,12},{16,20},{24,28}} | collective-permute-start | bytes 589832 | tf_op jit(solution)/shard_map/ppermute | solution.py:35
  19.6 1.3 %collective-permute-start.4 = (bf16[256,384]{1,0:T(8,128)(2,1)S(1)}, bf16[256,384]{1,0:T(8,128)(2,1)S(1)}, u32[]{:S(2)}, u32[]{:S(2)}) collective-permute-start(bf16[256,384]{1,0:T(8,128)(2,1)S(1)} %get-tuple-element.57), channel_id=1, source_target_pairs={{0,6},{8,14},{16,22},{24,30}} | collective-permute-start | bytes 589832 | tf_op jit(solution)/shard_map/ppermute | solution.py:35
  20.9 9.3 %invert.1 = f32[128,256]{1,0:T(8,128)S(1)} custom-call(s32[7]{0:T(128)S(1)} %stack.31.where_ref, f32[128,256]{1,0:T(8,128)S(1)} %add.72.mine_ref, f32[128,256]{1,0:T(8,128)S(1)} %collective-permute-done.7.other_ref), custom_call_target="tpu_custom_call" | custom-call | flops 8000000000 | bytes 524288 | tf_op jit(solution)/shard_map/invert/pallas_call | solution.py:155
  30.3 0.0 collective-permute-done.8
  30.3 1.3 %collective-permute-start.5 = (bf16[256,384]{1,0:T(8,128)(2,1)S(1)}, bf16[256,384]{1,0:T(8,128)(2,1)S(1)}, u32[]{:S(2)}, u32[]{:S(2)}) collective-permute-start(bf16[256,384]{1,0:T(8,128)(2,1)S(1)} %get-tuple-element.58), channel_id=1, source_target_pairs={{0,1},{8,9},{16,17},{24,25}} | collective-permute-start | bytes 589832 | tf_op jit(solution)/shard_map/ppermute | solution.py:35
  31.6 0.0 collective-permute-done.9
  31.6 1.3 %collective-permute-start.6 = (bf16[256,384]{1,0:T(8,128)(2,1)S(1)}, bf16[256,384]{1,0:T(8,128)(2,1)S(1)}, u32[]{:S(2)}, u32[]{:S(2)}) collective-permute-start(bf16[256,384]{1,0:T(8,128)(2,1)S(1)} %get-tuple-element.59), channel_id=1, source_target_pairs={{0,7},{8,15},{16,23},{24,31}} | collective-permute-start | bytes 589832 | tf_op jit(solution)/shard_map/ppermute | solution.py:35
  32.9 0.0 collective-permute-done.1
  32.9 0.7 collective-permute-start.10
  33.6 0.0 collective-permute-done.2
  33.6 0.7 collective-permute-start.11
  34.3 0.0 collective-permute-done.4
  34.3 2.1 %collective-permute-done.5 = bf16[256,384]{1,0:T(8,128)(2,1)S(1)} collective-permute-done((bf16[256,384]{1,0:T(8,128)(2,1)S(1)}, bf16[256,384]{1,0:T(8,128)(2,1)S(1)}, u32[]{:S(2)}, u32[]{:S(2)}) %collective-permute-start.5) | collective-permute-done | bytes 196640 | tf_op jit(solution)/shard_map/ppermute | solution.py:35
  36.4 1.4 %collective-permute-done.6 = bf16[256,384]{1,0:T(8,128)(2,1)S(1)} collective-permute-done((bf16[256,384]{1,0:T(8,128)(2,1)S(1)}, bf16[256,384]{1,0:T(8,128)(2,1)S(1)}, u32[]{:S(2)}, u32[]{:S(2)}) %collective-permute-start.6) | collective-permute-done | bytes 196640 | tf_op jit(solution)/shard_map/ppermute | solution.py:35
  37.8 0.0 collective-permute-done.10
  37.8 0.0 collective-permute-done.11
  37.8 0.1 add_add_fusion.refs_0_
  37.9 0.1 collective-permute-start.12
  37.9 2.0 %collective-permute-start.13 = (bf16[256,384]{1,0:T(8,128)(2,1)S(1)}, bf16[256,384]{1,0:T(8,128)(2,1)S(1)}, u32[]{:S(2)}, u32[]{:S(2)}) collective-permute-start(bf16[256,384]{1,0:T(8,128)(2,1)S(1)} %add_add_fusion.refs_0_), channel_id=1, source_target_pairs={{2,0},{4,2},{6,4},{7,6},{5,7},{3,5},{1,3},{0,1},{10,8},{12,10},{14... | collective-permute-start | bytes 589832 | tf_op jit(solution)/shard_map/ppermute | solution.py:35
  40.0 3.0 %collective-permute-start.14 = (f32[128,256]{1,0:T(8,128)S(1)}, f32[128,256]{1,0:T(8,128)S(1)}, u32[]{:S(2)}, u32[]{:S(2)}) collective-permute-start(f32[128,256]{1,0:T(8,128)S(1)} %invert.1), channel_id=1, source_target_pairs={{0,1},{8,9},{16,17},{24,25}} | collective-permute-start | bytes 393224 | tf_op jit(solution)/shard_map/ppermute | solution.py:35
  42.9 3.6 %collective-permute-done.14 = f32[128,256]{1,0:T(8,128)S(1)} collective-permute-done((f32[128,256]{1,0:T(8,128)S(1)}, f32[128,256]{1,0:T(8,128)S(1)}, u32[]{:S(2)}, u32[]{:S(2)}) %collective-permute-start.14) | collective-permute-done | bytes 131104 | tf_op jit(solution)/shard_map/ppermute | solution.py:35
  46.6 1.9 %gram.8.refs_4_ = f32[4,256,512]{2,1,0:T(8,128)S(1)} custom-call(s32[7]{0:T(128)S(1)} %stack.31.where_ref, bf16[256,384]{1,0:T(8,128)(2,1)S(1)} %add_add_fusion.refs_0_, bf16[3072,2048]{1,0:T(8,128)(2,1)S(1)} %bitcast.12), custom_call_target="tpu_custom_call" | custom-call | flops 402653184 | bytes 5767168 | tf_op jit(solution)/shard_map/gram/pallas_call | solution.py:192
  48.5 0.0 collective-permute-done.12.refs_0_
  48.5 0.1 collective-permute-start.15
  48.6 2.5 %collective-permute-start.16 = (bf16[256,384]{1,0:T(8,128)(2,1)S(1)}, bf16[256,384]{1,0:T(8,128)(2,1)S(1)}, u32[]{:S(2)}, u32[]{:S(2)}) collective-permute-start(bf16[256,384]{1,0:T(8,128)(2,1)S(1)} %collective-permute-done.13.refs_1_), channel_id=1, source_target_pairs={{2,0},{4,2},{6,4},{7,6},{5,7},{3,5},{1,3},{0,1},{10,8},{12,10},{14... | collective-permute-start | bytes 589832 | tf_op jit(solution)/shard_map/ppermute | solution.py:35
  51.1 1.5 %collective-permute-start.17 = (f32[128,256]{1,0:T(8,128)S(1)}, f32[128,256]{1,0:T(8,128)S(1)}, u32[]{:S(2)}, u32[]{:S(2)}) collective-permute-start(f32[128,256]{1,0:T(8,128)S(1)} %add.78), channel_id=1, source_target_pairs={{0,4},{1,5},{8,12},{9,13},{16,20},{17,21},{24,28},{25,29}} | collective-permute-start | bytes 393224 | tf_op jit(solution)/shard_map/ppermute | solution.py:35
  52.7 2.6 %gram.9.refs_4_ = f32[4,256,512]{2,1,0:T(8,128)S(1)} custom-call(s32[7]{0:T(128)S(1)} %stack.31.where_ref, bf16[256,384]{1,0:T(8,128)(2,1)S(1)} %collective-permute-done.12.refs_0_, bf16[256,384]{1,0:T(8,128)(2,1)S(1)} %collective-permute-done.13.refs_1_, bf16[3072,2048]{1,0:T(8,128)(2,1)S(1)} %bitcast.12, ...), custom_call_target="tpu_custom_call", output_to_operand_aliasing={{}: (5, {})} | custom-call | flops 805306368 | bytes 7340032 | tf_op jit(solution)/shard_map/gram/pallas_call | solution.py:192
  55.3 1.0 %collective-permute-done.17 = f32[128,256]{1,0:T(8,128)S(1)} collective-permute-done((f32[128,256]{1,0:T(8,128)S(1)}, f32[128,256]{1,0:T(8,128)S(1)}, u32[]{:S(2)}, u32[]{:S(2)}) %collective-permute-start.17) | collective-permute-done | bytes 131104 | tf_op jit(solution)/shard_map/ppermute | solution.py:35
  56.4 0.0 collective-permute-done.16.refs_1_
  56.4 0.1 collective-permute-start.18
  56.4 2.9 %collective-permute-start.19 = (bf16[256,384]{1,0:T(8,128)(2,1)S(1)}, bf16[256,384]{1,0:T(8,128)(2,1)S(1)}, u32[]{:S(2)}, u32[]{:S(2)}) collective-permute-start(bf16[256,384]{1,0:T(8,128)(2,1)S(1)} %collective-permute-done.16.refs_1_), channel_id=1, source_target_pairs={{2,0},{4,2},{6,4},{7,6},{5,7},{3,5},{1,3},{0,1},{10,8},{12,10},{14... | collective-permute-start | bytes 589832 | tf_op jit(solution)/shard_map/ppermute | solution.py:35
  59.3 3.0 %collective-permute-start.20 = (f32[128,256]{1,0:T(8,128)S(1)}, f32[128,256]{1,0:T(8,128)S(1)}, u32[]{:S(2)}, u32[]{:S(2)}) collective-permute-start(f32[128,256]{1,0:T(8,128)S(1)} %add.79), channel_id=1, source_target_pairs={{0,2},{1,3},{4,6},{5,7},{8,10},{9,11},{12,14},{13,15},{16,18},{17,... | collective-permute-start | bytes 393224 | tf_op jit(solution)/shard_map/ppermute | solution.py:35
  62.3 2.6 %gram.10.refs_4_ = f32[4,256,512]{2,1,0:T(8,128)S(1)} custom-call(s32[7]{0:T(128)S(1)} %stack.31.where_ref, bf16[256,384]{1,0:T(8,128)(2,1)S(1)} %collective-permute-done.15.refs_0_, bf16[256,384]{1,0:T(8,128)(2,1)S(1)} %collective-permute-done.16.refs_1_, bf16[3072,2048]{1,0:T(8,128)(2,1)S(1)} %bitcast.12, ...), custom_call_target="tpu_custom_call", output_to_operand_aliasing={{}: (5, {})} | custom-call | flops 805306368 | bytes 7340032 | tf_op jit(solution)/shard_map/gram/pallas_call | solution.py:192
  64.9 0.9 %collective-permute-done.20 = f32[128,256]{1,0:T(8,128)S(1)} collective-permute-done((f32[128,256]{1,0:T(8,128)S(1)}, f32[128,256]{1,0:T(8,128)S(1)}, u32[]{:S(2)}, u32[]{:S(2)}) %collective-permute-start.20) | collective-permute-done | bytes 131104 | tf_op jit(solution)/shard_map/ppermute | solution.py:35
  65.9 0.0 collective-permute-done.18.refs_0_
  65.9 0.0 collective-permute-done.19.refs_1_
  65.9 2.7 %collective-permute-start.22 = (bf16[256,384]{1,0:T(8,128)(2,1)S(1)}, bf16[256,384]{1,0:T(8,128)(2,1)S(1)}, u32[]{:S(2)}, u32[]{:S(2)}) collective-permute-start(bf16[256,384]{1,0:T(8,128)(2,1)S(1)} %collective-permute-done.18.refs_0_), channel_id=1, source_target_pairs={{0,2},{2,4},{4,6},{6,7},{7,5},{5,3},{3,1},{1,0},{8,10},{10,12},{12... | collective-permute-start | bytes 589832 | tf_op jit(solution)/shard_map/ppermute | solution.py:35
  68.6 2.6 %gram.11.refs_2_ = f32[4,256,512]{2,1,0:T(8,128)S(1)} custom-call(s32[7]{0:T(128)S(1)} %stack.31.where_ref, bf16[256,384]{1,0:T(8,128)(2,1)S(1)} %collective-permute-done.18.refs_0_, bf16[256,384]{1,0:T(8,128)(2,1)S(1)} %collective-permute-done.19.refs_1_, bf16[3072,2048]{1,0:T(8,128)(2,1)S(1)} %bitcast.12, ...), custom_call_target="tpu_custom_call", output_to_operand_aliasing={{}: (5, {})} | custom-call | flops 805306368 | bytes 7340032 | tf_op jit(solution)/shard_map/gram/pallas_call | solution.py:192
  71.2 0.5 collective-permute-done.22.refs_0_
  71.8 0.8 gram.15
  72.6 0.1 collective-permute-start.24
  72.7 0.5 collective-permute-start.21
  73.2 0.8 gram.13
  74.1 0.1 collective-permute-start.23
  74.2 0.8 gram.14.kept_ref
  75.1 0.0 collective-permute-done.24.came_ref
  75.1 1.2 %transform.3 = f32[1,512,256]{2,1,0:T(8,128)S(1)} custom-call(s32[7]{0:T(128)S(1)} %stack.31.where_ref, f32[128,256]{1,0:T(8,128)S(1)} %add.80.mine_ref, f32[128,256]{1,0:T(8,128)S(1)} %collective-permute-done.21.other_ref, f32[1,256,512]{2,1,0:T(8,128)S(1)} %gram.14.kept_ref, f32[1,256,512]{2,1,0:T(8,128)S(1)} %collective-permute-done.24.came_ref), custom_call_target="tpu_custom_call" | custom-call | tf_op jit(solution)/shard_map/transform/pallas_call | solution.py:226
  76.3 0.1 multiply_convert_fusion
  76.3 1.6 %collective-permute-start.25 = (f16[1,512,256]{2,1,0:T(8,128)(2,1)S(1)}, f16[1,512,256]{2,1,0:T(8,128)(2,1)S(1)}, u32[]{:S(2)}, u32[]{:S(2)}) collective-permute-start(f16[1,512,256]{2,1,0:T(8,128)(2,1)S(1)} %multiply_convert_fusion), channel_id=1, source_target_pairs={{0,16},{8,24},{16,0},{24,8},{1,17},{9,25},{17,1},{25,9},{2,18},{10... | collective-permute-start | bytes 786440 | tf_op jit(solution)/shard_map/ppermute | solution.py:40
  77.9 0.8 gram.12.kept_ref
  78.8 1.2 %transform.2 = f32[1,512,256]{2,1,0:T(8,128)S(1)} custom-call(s32[7]{0:T(128)S(1)} %stack.31.where_ref, f32[128,256]{1,0:T(8,128)S(1)} %add.80.mine_ref, f32[128,256]{1,0:T(8,128)S(1)} %collective-permute-done.21.other_ref, f32[1,256,512]{2,1,0:T(8,128)S(1)} %gram.12.kept_ref, f32[1,256,512]{2,1,0:T(8,128)S(1)} %collective-permute-done.23.came_ref), custom_call_target="tpu_custom_call" | custom-call | tf_op jit(solution)/shard_map/transform/pallas_call | solution.py:226
  80.0 5.1 %collective-permute-done.25 = f16[1,512,256]{2,1,0:T(8,128)(2,1)S(1)} collective-permute-done((f16[1,512,256]{2,1,0:T(8,128)(2,1)S(1)}, f16[1,512,256]{2,1,0:T(8,128)(2,1)S(1)}, u32[]{:S(2)}, u32[]{:S(2)}) %collective-permute-start.25) | collective-permute-done | bytes 262176 | tf_op jit(solution)/shard_map/ppermute | solution.py:40
  85.1 0.9 add_bitcast_fusion
  (16 shorter events, 0.1 us)
Async XLA Ops:
  3.1 1.5 %collective-permute-start = (f32[128,256]{1,0:T(8,128)S(1)}, f32[128,256]{1,0:T(8,128)S(1)}, u32[]{:S(2)}, u32[]{:S(2)}) collective-permute-start(f32[128,256]{1,0:T(8,128)S(1)} %get-tuple-element.43), channel_id=1, source_target_pairs={{0,8},{8,0},{16,24},{24,16},{1,9},{9,1},{17,25},{25,17},{2,10},{10... | collective-permute-start | bytes 393224 | tf_op jit(solution)/shard_map/ppermute | solution.py:40
  4.6 6.8 %collective-permute-start.3 = (f32[128,256]{1,0:T(8,128)S(1)}, f32[128,256]{1,0:T(8,128)S(1)}, u32[]{:S(2)}, u32[]{:S(2)}) collective-permute-start(f32[128,256]{1,0:T(8,128)S(1)} %add.69), channel_id=1, source_target_pairs={{0,16},{8,24},{16,0},{24,8},{1,17},{9,25},{17,1},{25,9},{2,18},{10... | collective-permute-start | bytes 393224 | tf_op jit(solution)/shard_map/ppermute | solution.py:40
  11.4 35.1 %slice-start = ((s8[12582912]{0:T(1024)(128)(4,1)}), s8[4194304]{0:T(1024)(128)(4,1)S(1)}, s32[]{:S(2)}) async-start(s8[12582912]{0:T(1024)(128)(4,1)} %bitcast.11), calls=%async_computation | async-start | bytes 8388608
  11.4 35.1 %slice-start.1 = ((s8[12582912]{0:T(1024)(128)(4,1)}), s8[4194304]{0:T(1024)(128)(4,1)S(1)}, s32[]{:S(2)}) async-start(s8[12582912]{0:T(1024)(128)(4,1)} %bitcast.11), calls=%async_computation.1 | async-start | bytes 8388608
  11.4 35.1 %slice-start.2 = ((s8[12582912]{0:T(1024)(128)(4,1)}), s8[4194304]{0:T(1024)(128)(4,1)S(1)}, s32[]{:S(2)}) async-start(s8[12582912]{0:T(1024)(128)(4,1)} %bitcast.11), calls=%async_computation.2 | async-start | bytes 8388608
  11.4 8.2 %collective-permute-start.7 = (f32[128,256]{1,0:T(8,128)S(1)}, f32[128,256]{1,0:T(8,128)S(1)}, u32[]{:S(2)}, u32[]{:S(2)}) collective-permute-start(f32[128,256]{1,0:T(8,128)S(1)} %add.72.mine_ref), channel_id=1, source_target_pairs={{0,8},{8,0},{16,24},{24,16},{1,9},{9,1},{17,25},{25,17},{2,10},{10... | collective-permute-start | bytes 393224 | tf_op jit(solution)/shard_map/ppermute | solution.py:40
  11.5 18.8 %collective-permute-start.8 = (bf16[256,384]{1,0:T(8,128)(2,1)S(1)}, bf16[256,384]{1,0:T(8,128)(2,1)S(1)}, u32[]{:S(2)}, u32[]{:S(2)}) collective-permute-start(bf16[256,384]{1,0:T(8,128)(2,1)S(1)} %get-tuple-element.61), channel_id=1, source_target_pairs={{0,1},{8,9},{16,17},{24,25}} | collective-permute-start | bytes 589832 | tf_op jit(solution)/shard_map/ppermute | solution.py:35
  15.6 16.0 %collective-permute-start.9 = (bf16[256,384]{1,0:T(8,128)(2,1)S(1)}, bf16[256,384]{1,0:T(8,128)(2,1)S(1)}, u32[]{:S(2)}, u32[]{:S(2)}) collective-permute-start(bf16[256,384]{1,0:T(8,128)(2,1)S(1)} %get-tuple-element.62), channel_id=1, source_target_pairs={{0,1},{8,9},{16,17},{24,25}} | collective-permute-start | bytes 589832 | tf_op jit(solution)/shard_map/ppermute | solution.py:35
  17.0 15.9 %collective-permute-start.1 = (bf16[256,384]{1,0:T(8,128)(2,1)S(1)}, bf16[256,384]{1,0:T(8,128)(2,1)S(1)}, u32[]{:S(2)}, u32[]{:S(2)}) collective-permute-start(bf16[256,384]{1,0:T(8,128)(2,1)S(1)} %get-tuple-element.51), channel_id=1, source_target_pairs={{0,2},{8,10},{16,18},{24,26}} | collective-permute-start | bytes 589832 | tf_op jit(solution)/shard_map/ppermute | solution.py:35
  18.3 15.3 %collective-permute-start.2 = (bf16[256,384]{1,0:T(8,128)(2,1)S(1)}, bf16[256,384]{1,0:T(8,128)(2,1)S(1)}, u32[]{:S(2)}, u32[]{:S(2)}) collective-permute-start(bf16[256,384]{1,0:T(8,128)(2,1)S(1)} %get-tuple-element.52), channel_id=1, source_target_pairs={{0,4},{8,12},{16,20},{24,28}} | collective-permute-start | bytes 589832 | tf_op jit(solution)/shard_map/ppermute | solution.py:35
  19.6 14.7 %collective-permute-start.4 = (bf16[256,384]{1,0:T(8,128)(2,1)S(1)}, bf16[256,384]{1,0:T(8,128)(2,1)S(1)}, u32[]{:S(2)}, u32[]{:S(2)}) collective-permute-start(bf16[256,384]{1,0:T(8,128)(2,1)S(1)} %get-tuple-element.57), channel_id=1, source_target_pairs={{0,6},{8,14},{16,22},{24,30}} | collective-permute-start | bytes 589832 | tf_op jit(solution)/shard_map/ppermute | solution.py:35
  30.3 6.1 %collective-permute-start.5 = (bf16[256,384]{1,0:T(8,128)(2,1)S(1)}, bf16[256,384]{1,0:T(8,128)(2,1)S(1)}, u32[]{:S(2)}, u32[]{:S(2)}) collective-permute-start(bf16[256,384]{1,0:T(8,128)(2,1)S(1)} %get-tuple-element.58), channel_id=1, source_target_pairs={{0,1},{8,9},{16,17},{24,25}} | collective-permute-start | bytes 589832 | tf_op jit(solution)/shard_map/ppermute | solution.py:35
  31.6 6.2 %collective-permute-start.6 = (bf16[256,384]{1,0:T(8,128)(2,1)S(1)}, bf16[256,384]{1,0:T(8,128)(2,1)S(1)}, u32[]{:S(2)}, u32[]{:S(2)}) collective-permute-start(bf16[256,384]{1,0:T(8,128)(2,1)S(1)} %get-tuple-element.59), channel_id=1, source_target_pairs={{0,7},{8,15},{16,23},{24,31}} | collective-permute-start | bytes 589832 | tf_op jit(solution)/shard_map/ppermute | solution.py:35
  32.9 4.9 %collective-permute-start.10 = (bf16[256,384]{1,0:T(8,128)(2,1)S(1)}, bf16[256,384]{1,0:T(8,128)(2,1)S(1)}, u32[]{:S(2)}, u32[]{:S(2)}) collective-permute-start(bf16[256,384]{1,0:T(8,128)(2,1)S(1)} %collective-permute-done.8), channel_id=1, source_target_pairs={{1,5},{9,13},{17,21},{25,29}} | collective-permute-start | bytes 589832 | tf_op jit(solution)/shard_map/ppermute | solution.py:35
  33.6 4.2 %collective-permute-start.11 = (bf16[256,384]{1,0:T(8,128)(2,1)S(1)}, bf16[256,384]{1,0:T(8,128)(2,1)S(1)}, u32[]{:S(2)}, u32[]{:S(2)}) collective-permute-start(bf16[256,384]{1,0:T(8,128)(2,1)S(1)} %collective-permute-done.9), channel_id=1, source_target_pairs={{1,3},{9,11},{17,19},{25,27}} | collective-permute-start | bytes 589832 | tf_op jit(solution)/shard_map/ppermute | solution.py:35
  37.9 10.6 %collective-permute-start.12 = (bf16[256,384]{1,0:T(8,128)(2,1)S(1)}, bf16[256,384]{1,0:T(8,128)(2,1)S(1)}, u32[]{:S(2)}, u32[]{:S(2)}) collective-permute-start(bf16[256,384]{1,0:T(8,128)(2,1)S(1)} %add_add_fusion.refs_0_), channel_id=1, source_target_pairs={{0,2},{2,4},{4,6},{6,7},{7,5},{5,3},{3,1},{1,0},{8,10},{10,12},{12... | collective-permute-start | bytes 589832 | tf_op jit(solution)/shard_map/ppermute | solution.py:35
  37.9 10.6 %collective-permute-start.13 = (bf16[256,384]{1,0:T(8,128)(2,1)S(1)}, bf16[256,384]{1,0:T(8,128)(2,1)S(1)}, u32[]{:S(2)}, u32[]{:S(2)}) collective-permute-start(bf16[256,384]{1,0:T(8,128)(2,1)S(1)} %add_add_fusion.refs_0_), channel_id=1, source_target_pairs={{2,0},{4,2},{6,4},{7,6},{5,7},{3,5},{1,3},{0,1},{10,8},{12,10},{14... | collective-permute-start | bytes 589832 | tf_op jit(solution)/shard_map/ppermute | solution.py:35
  40.0 6.6 %collective-permute-start.14 = (f32[128,256]{1,0:T(8,128)S(1)}, f32[128,256]{1,0:T(8,128)S(1)}, u32[]{:S(2)}, u32[]{:S(2)}) collective-permute-start(f32[128,256]{1,0:T(8,128)S(1)} %invert.1), channel_id=1, source_target_pairs={{0,1},{8,9},{16,17},{24,25}} | collective-permute-start | bytes 393224 | tf_op jit(solution)/shard_map/ppermute | solution.py:35
  48.5 7.8 %collective-permute-start.15 = (bf16[256,384]{1,0:T(8,128)(2,1)S(1)}, bf16[256,384]{1,0:T(8,128)(2,1)S(1)}, u32[]{:S(2)}, u32[]{:S(2)}) collective-permute-start(bf16[256,384]{1,0:T(8,128)(2,1)S(1)} %collective-permute-done.12.refs_0_), channel_id=1, source_target_pairs={{0,2},{2,4},{4,6},{6,7},{7,5},{5,3},{3,1},{1,0},{8,10},{10,12},{12... | collective-permute-start | bytes 589832 | tf_op jit(solution)/shard_map/ppermute | solution.py:35
  48.6 7.8 %collective-permute-start.16 = (bf16[256,384]{1,0:T(8,128)(2,1)S(1)}, bf16[256,384]{1,0:T(8,128)(2,1)S(1)}, u32[]{:S(2)}, u32[]{:S(2)}) collective-permute-start(bf16[256,384]{1,0:T(8,128)(2,1)S(1)} %collective-permute-done.13.refs_1_), channel_id=1, source_target_pairs={{2,0},{4,2},{6,4},{7,6},{5,7},{3,5},{1,3},{0,1},{10,8},{12,10},{14... | collective-permute-start | bytes 589832 | tf_op jit(solution)/shard_map/ppermute | solution.py:35
  51.1 5.2 %collective-permute-start.17 = (f32[128,256]{1,0:T(8,128)S(1)}, f32[128,256]{1,0:T(8,128)S(1)}, u32[]{:S(2)}, u32[]{:S(2)}) collective-permute-start(f32[128,256]{1,0:T(8,128)S(1)} %add.78), channel_id=1, source_target_pairs={{0,4},{1,5},{8,12},{9,13},{16,20},{17,21},{24,28},{25,29}} | collective-permute-start | bytes 393224 | tf_op jit(solution)/shard_map/ppermute | solution.py:35
  56.4 9.5 %collective-permute-start.18 = (bf16[256,384]{1,0:T(8,128)(2,1)S(1)}, bf16[256,384]{1,0:T(8,128)(2,1)S(1)}, u32[]{:S(2)}, u32[]{:S(2)}) collective-permute-start(bf16[256,384]{1,0:T(8,128)(2,1)S(1)} %collective-permute-done.15.refs_0_), channel_id=1, source_target_pairs={{0,2},{2,4},{4,6},{6,7},{7,5},{5,3},{3,1},{1,0},{8,10},{10,12},{12... | collective-permute-start | bytes 589832 | tf_op jit(solution)/shard_map/ppermute | solution.py:35
  56.4 9.5 %collective-permute-start.19 = (bf16[256,384]{1,0:T(8,128)(2,1)S(1)}, bf16[256,384]{1,0:T(8,128)(2,1)S(1)}, u32[]{:S(2)}, u32[]{:S(2)}) collective-permute-start(bf16[256,384]{1,0:T(8,128)(2,1)S(1)} %collective-permute-done.16.refs_1_), channel_id=1, source_target_pairs={{2,0},{4,2},{6,4},{7,6},{5,7},{3,5},{1,3},{0,1},{10,8},{12,10},{14... | collective-permute-start | bytes 589832 | tf_op jit(solution)/shard_map/ppermute | solution.py:35
  59.3 6.6 %collective-permute-start.20 = (f32[128,256]{1,0:T(8,128)S(1)}, f32[128,256]{1,0:T(8,128)S(1)}, u32[]{:S(2)}, u32[]{:S(2)}) collective-permute-start(f32[128,256]{1,0:T(8,128)S(1)} %add.79), channel_id=1, source_target_pairs={{0,2},{1,3},{4,6},{5,7},{8,10},{9,11},{12,14},{13,15},{16,18},{17,... | collective-permute-start | bytes 393224 | tf_op jit(solution)/shard_map/ppermute | solution.py:35
  65.9 5.9 %collective-permute-start.22 = (bf16[256,384]{1,0:T(8,128)(2,1)S(1)}, bf16[256,384]{1,0:T(8,128)(2,1)S(1)}, u32[]{:S(2)}, u32[]{:S(2)}) collective-permute-start(bf16[256,384]{1,0:T(8,128)(2,1)S(1)} %collective-permute-done.18.refs_0_), channel_id=1, source_target_pairs={{0,2},{2,4},{4,6},{6,7},{7,5},{5,3},{3,1},{1,0},{8,10},{10,12},{12... | collective-permute-start | bytes 589832 | tf_op jit(solution)/shard_map/ppermute | solution.py:35
  72.6 2.4 %collective-permute-start.24 = (f32[1,256,512]{2,1,0:T(8,128)S(1)}, f32[1,256,512]{2,1,0:T(8,128)S(1)}, u32[]{:S(2)}, u32[]{:S(2)}) collective-permute-start(f32[1,256,512]{2,1,0:T(8,128)S(1)} %gram.15), channel_id=1, source_target_pairs={{0,8},{8,0},{16,24},{24,16},{1,9},{9,1},{17,25},{25,17},{2,10},{10... | collective-permute-start | bytes 1572872 | tf_op jit(solution)/shard_map/ppermute | solution.py:40
  72.7 2.3 %collective-permute-start.21 = (f32[128,256]{1,0:T(8,128)S(1)}, f32[128,256]{1,0:T(8,128)S(1)}, u32[]{:S(2)}, u32[]{:S(2)}) collective-permute-start(f32[128,256]{1,0:T(8,128)S(1)} %add.80.mine_ref), channel_id=1, source_target_pairs={{0,8},{8,0},{16,24},{24,16},{1,9},{9,1},{17,25},{25,17},{2,10},{10... | collective-permute-start | bytes 393224 | tf_op jit(solution)/shard_map/ppermute | solution.py:40
  74.1 4.7 %collective-permute-start.23 = (f32[1,256,512]{2,1,0:T(8,128)S(1)}, f32[1,256,512]{2,1,0:T(8,128)S(1)}, u32[]{:S(2)}, u32[]{:S(2)}) collective-permute-start(f32[1,256,512]{2,1,0:T(8,128)S(1)} %gram.13), channel_id=1, source_target_pairs={{0,8},{8,0},{16,24},{24,16},{1,9},{9,1},{17,25},{25,17},{2,10},{10... | collective-permute-start | bytes 1572872 | tf_op jit(solution)/shard_map/ppermute | solution.py:40
  76.3 8.7 %collective-permute-start.25 = (f16[1,512,256]{2,1,0:T(8,128)(2,1)S(1)}, f16[1,512,256]{2,1,0:T(8,128)(2,1)S(1)}, u32[]{:S(2)}, u32[]{:S(2)}) collective-permute-start(f16[1,512,256]{2,1,0:T(8,128)(2,1)S(1)} %multiply_convert_fusion), channel_id=1, source_target_pairs={{0,16},{8,24},{16,0},{24,8},{1,17},{9,25},{17,1},{25,9},{2,18},{10... | collective-permute-start | bytes 786440 | tf_op jit(solution)/shard_map/ppermute | solution.py:40

commit v2 on v0

v2 whole, which is shorter than its diff:
```python
import functools

import jax
import jax.numpy as jnp
from jax import lax
from jax.experimental import pallas as pl
from jax.experimental.pallas import tpu as pltpu
from jax.sharding import PartitionSpec as P

PANEL = 256
HALF = PANEL // 2
LANES = 128
BLOCK = 64
STRIP = 8
COLUMN, CORE, AT, BLOCKS = 0, 1, 2, 3
SMEM, VMEM, HBM = (pl.BlockSpec(memory_space=space) for space in (pltpu.SMEM, pltpu.VMEM, pltpu.HBM))
HIGHEST = lax.Precision.HIGHEST
F32 = jnp.float32
PARAMS = pltpu.CompilerParams(vmem_limit_bytes=16 * 2**20)


def ring_order(columns):
    return list(range(0, columns, 2)) + list(range(columns - 1, 0, -2))


def reverse_bits(value, count):
    out, bit = 0, 1
    while bit < count:
        out = out * 2 + (1 if value & bit else 0)
        bit *= 2
    return out


def to_column(value, pairs):
    return lax.ppermute(value, "col", pairs)


def swap(value, bit, column=None):
    shares, columns = lax.axis_size("rxn"), lax.axis_size("col")
    on = range(columns) if column is None else [column]
    pairs = [(i * columns + c, (i ^ bit) * columns + c) for i in range(shares) for c in on]
    return lax.ppermute(value, ("rxn", "col"), pairs)


def cut_kernel(place_ref, basis_ref, *refs):
    pieces, sems = refs[:-1], refs[-1]
    pieces[0][...] = jnp.zeros_like(pieces[0])

    @pl.when(place_ref[COLUMN] == 0)
    def _():
        depth = pieces[0].shape[0]
        copies = [
            pltpu.make_async_copy(basis_ref.at[pl.ds(p * depth, depth), pl.ds(0, PANEL)], piece, sems.at[p])
            for p, piece in enumerate(pieces)
        ]
        for copy in copies:
            copy.start()
        for copy in copies:
            copy.wait()


def cut_panel(place, basis, count):
    depth = basis.shape[0] // count
    return pl.pallas_call(
        cut_kernel,
        out_shape=[jax.ShapeDtypeStruct((depth, PANEL), jnp.bfloat16)] * count,
        in_specs=[SMEM, HBM],
        out_specs=[VMEM] * count,
        scratch_shapes=[pltpu.SemaphoreType.DMA((count,))],
        compiler_params=PARAMS,
        name="cut_panel",
    )(place, basis)


def eliminate(work):
    done, width = [], work.shape[1]
    for start in range(0, work.shape[0], STRIP):
        rows = work.shape[0]
        row = lax.broadcasted_iota(jnp.int32, (rows, width), 0)
        column = [jnp.broadcast_to(work[:, start + j : start + j + 1], (rows, width)) for j in range(STRIP)]
        for k in range(STRIP):
            root = lax.rsqrt(column[k][k : k + 1, :])
            pivot_row = work[k : k + 1, :] * root
            below = jnp.where(row > k, column[k] * root, 0.0)
            work = jnp.where(row == k, pivot_row, work - below * pivot_row)
            for j in range(k + 1, STRIP):
                column[j] = column[j] - below * (column[j][k : k + 1, :] * root)
        done.append(work[:STRIP])
        work = work[STRIP:]
    return jnp.concatenate(done, 0)


def invert_kernel(place_ref, mine_ref, other_ref, out_ref, work):
    core = place_ref[CORE]
    mine = pl.ds(pl.multiple_of(core * HALF, HALF), HALF)
    other = pl.ds(pl.multiple_of((1 - core) * HALF, HALF), HALF)
    work[mine, :PANEL] = mine_ref[...]
    work[other, :PANEL] = other_ref[...]
    gram = work[:, :PANEL]
    work[:, :PANEL] = 0.5 * (gram + gram.T)
    row = lax.broadcasted_iota(jnp.int32, (PANEL, PANEL), 0)
    col = lax.broadcasted_iota(jnp.int32, (PANEL, PANEL), 1)
    work[:, PANEL:] = jnp.where(row == col, 1.0, 0.0).astype(F32)
    row = lax.broadcasted_iota(jnp.int32, (BLOCK, 128), 0)
    col = lax.broadcasted_iota(jnp.int32, (BLOCK, 128), 1)
    for low in range(0, PANEL, BLOCK):
        base = low // 128 * 128
        square = work[low : low + BLOCK, base : base + 128]
        if low > base:
            square = pltpu.roll(square, 128 - (low - base), 1)
        square = jnp.where(col < BLOCK, square, jnp.where(col - BLOCK == row, 1.0, 0.0))
        corner = pltpu.roll(eliminate(square), 128 - BLOCK, 1)[:, :BLOCK]
        end = PANEL + (low + BLOCK + 127) // 128 * 128
        scaled = jnp.dot(corner, work[low : low + BLOCK, base:end], precision=HIGHEST, preferred_element_type=F32)
        work[low : low + BLOCK, base:end] = scaled
        rest = low + BLOCK
        if rest < PANEL:
            left = rest // 128 * 128
            update = lax.dot_general(
                scaled[:, left - base : PANEL - base],
                scaled[:, left - base :],
                (((0,), (0,)), ((), ())),
                precision=HIGHEST,
                preferred_element_type=F32,
            )
            work[rest:PANEL, left:end] = work[rest:PANEL, left:end] - update[rest - left :]
    row = lax.broadcasted_iota(jnp.int32, (PANEL, PANEL), 0)
    col = lax.broadcasted_iota(jnp.int32, (PANEL, PANEL), 1)
    out_ref[...] = jnp.where(row >= col, work[:, PANEL:], 0.0)


def invert(place, mine, other):
    return pl.pallas_call(
        invert_kernel,
        out_shape=jax.ShapeDtypeStruct((PANEL, PANEL), F32),
        in_specs=[SMEM, VMEM, VMEM],
        out_specs=VMEM,
        scratch_shapes=[pltpu.VMEM((PANEL, 2 * PANEL), F32)],
        compiler_params=PARAMS,
        cost_estimate=pl.CostEstimate(flops=3*10**9, bytes_accessed=2**19, transcendentals=0),
        name="invert",
    )(place, mine, other)


def weigh(total, at, lower_ref, upper_ref, piece):
    low, up = lower_ref[pl.ds(at, 1), :], upper_ref[pl.ds(at, 1), :]
    scaled = (1.0 / (low * low) + 1.0 / (up * up)) / total
    return (piece.astype(F32).T * scaled).astype(jnp.bfloat16)


def piece_at(place_ref, offset, columns):
    return lax.rem(place_ref[AT] + (offset + columns), columns)


def block_lanes(place_ref, block, share):
    return pl.ds(pl.multiple_of(place_ref[BLOCKS + block] * share, share), share)


def fetches(place_ref, basis_ref, columns, offsets, tiles, sems):
    depth = basis_ref.shape[0] // columns
    copies = []
    for i, (offset, tile) in enumerate(zip(offsets, tiles)):
        rows = pl.ds(pl.multiple_of(piece_at(place_ref, offset, columns) * depth, depth), depth)
        copies.append(pltpu.make_async_copy(basis_ref.at[rows, :], tile, sems.at[i]))
    return copies


def gram_kernel(offsets, later, total, fresh, place_ref, lower_ref, upper_ref, basis_ref, *refs):
    number, columns = len(offsets), lower_ref.shape[0]
    pieces, weighted, sems = refs[:number], refs[-number - 1 : -1], refs[-1]
    if fresh:
        outs, tiles = refs[number : -2 * number - 1], refs[-2 * number - 1 : -number - 1]
    else:
        tiles, adds, outs = refs[number : 2 * number], refs[2 * number :], refs[2 * number + 2 : -number - 1]
    copies = fetches(place_ref, basis_ref, columns, later, outs[2:], sems)
    own = fetches(place_ref, basis_ref, columns, offsets, tiles, sems.at[pl.ds(len(later), number)]) if fresh else []
    for copy in own + copies:
        copy.start()
    diagonal = jnp.zeros((PANEL, PANEL), F32) if fresh else adds[1][...]
    for offset, piece, held in zip(offsets, pieces, weighted):
        at = piece_at(place_ref, offset, columns)
        held[...] = weigh(total, at, lower_ref, upper_ref, piece[...])
        diagonal += jnp.dot(held[...], piece[...], preferred_element_type=F32)
    outs[1][...] = diagonal
    for copy in own:
        copy.wait()
    count, _, share = outs[0].shape

    def block(j, carry):
        lanes = block_lanes(place_ref, j, share)
        gram = jnp.zeros((PANEL, share), F32) if fresh else adds[0][j]
        for held, tile in zip(weighted, tiles):
            gram += jnp.dot(held[...], tile[:, lanes], preferred_element_type=F32)
        outs[0][j] = gram
        return carry

    lax.fori_loop(0, count, block, 0)
    for copy in copies:
        copy.wait()


def add_gram(total, shares, shared, sums, pieces, offsets, tiles, later):
    basis, number, depth = shared[-1], len(pieces), pieces[0].shape[0]
    cols = basis.shape[1]
    share = cols // shares
    tile = (depth, cols)
    base = len(shared) + 2 * number
    return pl.pallas_call(
        functools.partial(gram_kernel, offsets, later, float(total), not sums),
        out_shape=[
            jax.ShapeDtypeStruct((shares, PANEL, share), F32),
            jax.ShapeDtypeStruct((PANEL, PANEL), F32),
            *[jax.ShapeDtypeStruct(tile, jnp.bfloat16)] * len(later),
        ],
        in_specs=[SMEM, VMEM, VMEM, HBM] + [VMEM] * (number + len(tiles) + len(sums)),
        out_specs=[VMEM] * (2 + len(later)),
        scratch_shapes=[pltpu.VMEM(tile, jnp.bfloat16)] * (0 if sums else number)
        + [pltpu.VMEM((PANEL, depth), jnp.bfloat16)] * number
        + [pltpu.SemaphoreType.DMA((number + len(later),))],
        compiler_params=PARAMS,
        input_output_aliases={base: 0, base + 1: 1} if sums else {},
        cost_estimate=pl.CostEstimate(
            flops=2 * number * depth * PANEL * cols,
            bytes_accessed=number * depth * cols * 2 + 8 * PANEL * cols,
            transcendentals=0,
        ),
        name="gram",
    )(*shared, *pieces, *tiles, *sums)


def last_kernel(offset, total, place_ref, lower_ref, upper_ref, tile_ref, top_ref, bottom_ref, *refs):
    gram_ref, diagonal_ref, sent_ref, away_ref, mine_ref, other_ref, weighted_ref, sum_ref = refs
    piece = jnp.concatenate([top_ref[...], bottom_ref[...]], 0)
    at = piece_at(place_ref, offset, lower_ref.shape[0])
    weighted_ref[...] = weigh(total, at, lower_ref, upper_ref, piece)
    sum_ref[...] = diagonal_ref[...] + jnp.dot(weighted_ref[...], piece, preferred_element_type=F32)
    core = place_ref[CORE]
    mine_ref[...] = sum_ref[pl.ds(pl.multiple_of(core * HALF, HALF), HALF), :]
    other_ref[...] = sum_ref[pl.ds(pl.multiple_of((1 - core) * HALF, HALF), HALF), :]
    add_blocks(place_ref, gram_ref, weighted_ref, tile_ref, [(3, sent_ref), (1, away_ref)])


def add_blocks(place_ref, gram_ref, weighted_ref, tile_ref, quarters):
    for number, out_ref in quarters:
        count, _, share = out_ref.shape
        for j in range(count):
            block = number * count + j
            lanes = block_lanes(place_ref, block, share)
            term = jnp.dot(weighted_ref[...], tile_ref[:, lanes], preferred_element_type=F32)
            out_ref[j] = gram_ref[block] + term


def rest_kernel(place_ref, weighted_ref, tile_ref, gram_ref, sent_ref, kept_ref):
    add_blocks(place_ref, gram_ref, weighted_ref, tile_ref, [(2, sent_ref), (0, kept_ref)])


def finish_gram(total, shared, sums, tile, top, bottom, offset):
    place, lower, upper, _ = shared
    gram, diagonal = sums
    shares, _, share = gram.shape
    depth = tile.shape[0]
    quarter = jax.ShapeDtypeStruct((shares // 4, PANEL, share), F32)
    half = jax.ShapeDtypeStruct((HALF, PANEL), F32)
    cost = pl.CostEstimate(flops=depth * PANEL * share * shares, bytes_accessed=2**21, transcendentals=0)
    third, first, mine, other, weighted = pl.pallas_call(
        functools.partial(last_kernel, offset, float(total)),
        out_shape=[quarter, quarter, half, half, jax.ShapeDtypeStruct((PANEL, depth), jnp.bfloat16)],
        in_specs=[SMEM] + [VMEM] * 7,
        out_specs=[VMEM] * 5,
        scratch_shapes=[pltpu.VMEM((PANEL, PANEL), F32)],
        compiler_params=PARAMS,
        cost_estimate=cost,
        name="last",
    )(place, lower, upper, tile, top, bottom, gram, diagonal)
    second, zeroth = pl.pallas_call(
        rest_kernel,
        out_shape=[quarter, quarter],
        in_specs=[SMEM] + [VMEM] * 3,
        out_specs=[VMEM] * 2,
        compiler_params=PARAMS,
        cost_estimate=cost,
        name="rest",
    )(place, weighted, tile, gram)
    return zeroth, first, second, third, mine, other


def transform_kernel(inverse_ref, *refs):
    gram = refs[0][0]
    for ref in refs[1:-1]:
        gram = gram + ref[0]
    refs[-1][...] = lax.dot_general(
        gram.T, inverse_ref[...], (((1,), (1,)), ((), ())), precision=HIGHEST, preferred_element_type=F32
    )


def transform(inverse, terms):
    share = terms[0].shape[2]
    return pl.pallas_call(
        transform_kernel,
        out_shape=jax.ShapeDtypeStruct((share, PANEL), F32),
        in_specs=[VMEM] * (1 + len(terms)),
        out_specs=VMEM,
        compiler_params=PARAMS,
        cost_estimate=pl.CostEstimate(
            flops=12 * share * PANEL * PANEL, bytes_accessed=12 * share * PANEL, transcendentals=0
        ),
        name="transform",
    )(inverse, *terms)


def on_device(basis, lower_slack, upper_slack):
    rows = basis.shape[0]
    shares, columns = lax.axis_size("rxn"), lax.axis_size("col")
    me, column = lax.axis_index("rxn"), lax.axis_index("col")
    order = ring_order(columns)
    relay, middle = order[-1], columns // 2
    at = sum(jnp.where(column == c, p, 0) for p, c in enumerate(order))
    blocks = [me ^ reverse_bits(j, shares) for j in range(shares)]
    place = jnp.stack([column, me % 2, at, *blocks]).astype(jnp.int32)
    basis = pltpu.with_memory_space_constraint(basis, pltpu.HBM)
    pieces = cut_panel(place, basis, columns)
    slacks = [x.reshape(columns, rows // columns) for x in (lower_slack, upper_slack)]
    shared = (place, *slacks, basis)

    through, near = range(middle + 1, columns - 1), range(1, middle + 1)
    to_relay = lambda p: to_column(pieces[p], [(0, relay)])
    parts = [to_column(pieces[p], [(0, order[p])]) for p in near]
    far = [to_relay(p) for p in through]
    parts.append(to_relay(columns - 1))
    parts += [to_column(x, [(relay, order[p])]) for x, p in zip(far, through)]
    held = functools.reduce(lambda a, b: a + b, parts, pieces[0])

    forward = [(order[i], order[(i + 1) % columns]) for i in range(columns)]
    backward = [(b, a) for a, b in forward]
    gram = functools.partial(add_gram, rows * shares, shares, shared)
    pieces, offsets, sums, tiles = [held], [0], [], []
    ahead = back = held
    for step in range(1, middle):
        ahead, back = to_column(ahead, forward), to_column(back, backward)
        later = [-step, step]
        *sums, left, right = gram(sums, pieces, offsets, tiles, later)
        ahead, back, left, right, *sums = lax.optimization_barrier((ahead, back, left, right, *sums))
        pieces, offsets, tiles = [ahead, back], later, [left, right]
    cut = rows // columns // 2
    top, bottom = to_column(ahead[:cut], forward), to_column(back[cut:], backward)
    *sums, tile = gram(sums, pieces, offsets, tiles, [middle])
    zeroth, first, second, third, mine, other = finish_gram(rows * shares, shared, sums, tile, top, bottom, middle)

    mine, third = mine + swap(other, 1), swap(third, 1)
    away, second = first + third, swap(second, 1)
    mine, away = lax.optimization_barrier((mine, away))
    part, came = swap(mine, 2), swap(away, 2)
    mine, bit = mine + part, 4
    while bit < shares:
        mine = mine + swap(mine, bit)
        bit *= 2
    other = swap(mine, 1)
    inverse = invert(place, mine, other)
    terms, bit = [zeroth, second, came], 4
    while bit < shares:
        mine = functools.reduce(lambda a, b: a + b, terms)
        middle = mine.shape[0] // 2
        terms = [mine[:middle], swap(mine[middle:], bit)]
        bit *= 2
    return transform(inverse, terms)


def solution(mesh):
    return jax.shard_map(
        on_device,
        mesh=mesh,
        in_specs=(P("rxn", "col"), P("rxn"), P("rxn")),
        out_specs=P(("col", "rxn"), None),
        check_vma=False,
    )
```

time: 242 us -> 73.5 us (0.30)
  waiting for transfers between devices: 148 us -> 20.6 us
  other arithmetic: 57.5 us -> 0.23 us
  Pallas kernels: 0 us -> 26.6 us
  starting transfers between devices: 0.04 us -> 25.2 us
  matrix products: 16.1 us -> 0 us
  between operations: 14.8 us -> 0.28 us
  local copies, waits for them, and re-layouts: 5.08 us -> 0.12 us
    psum x2 -> x0, waiting for transfers between devices: 148 us -> none  [the longest x1 93.2 us: from_root(): return lax.psum(kept, axis)]
    another operation x9 -> x0, other arithmetic: 53.8 us -> none  [the longest x6 34.1 us: on_device(): factor = jnp.linalg.cholesky(diag_block)]
    pallas_call x0 -> x9, Pallas kernels: none -> 26.6 us  [the longest x4 11.5 us: add_gram(): pl.pallas_call(functools.partial(gram_kernel, offsets, later, float(total...]
    ppermute x0 -> x23, starting transfers between devices: none -> 25.2 us  [the longest x17 22.3 us: to_column(): return lax.ppermute(value, 'col', pairs)]
    ppermute x0 -> x23, waiting for transfers between devices: none -> 20.6 us  [the longest x17 14.7 us: to_column(): return lax.ppermute(value, 'col', pairs)]
    dot_general x3 -> x0, matrix products: 14.7 us -> none  [the longest x1 9.99 us: on_device(): lax.dot_general(basis, weighted, contract, preferred_element_type=jnp.flo...]
    another operation x9 -> x1, local copies, waits for them, and re-layouts: 3.99 us -> 0.08 us  [on_device(): place = jnp.stack([column, me % 2, at, *blocks]).astype(jnp.int32)]
    select_n x1 -> x0, other arithmetic: 2.68 us -> none  [from_root(): jnp.where(lax.axis_index(axis) == source, value, 0).astype(value.dtype)]
  transfers between devices with their start and end apart: 2 -> 23, of which waited for: 2 -> 12; matrix products, arithmetic and copies ran while one was open for 0% -> 0% of each run, Pallas kernels for 0% -> 30%
where the time goes in v2:
time: 73.5 us; the launch traced here: 73.1 us
  Pallas kernels  26.6 us (36%)
  starting transfers between devices  25.2 us (34%)
  waiting for transfers between devices  20.6 us (28%)
    ppermute x17, starting transfers between devices, to_column(): return lax.ppermute(value, 'col', pairs)  22.3 us
    ppermute x17, waiting for transfers between devices, to_column(): return lax.ppermute(value, 'col', pairs)  14.7 us
    pallas_call x4, Pallas kernels, add_gram(): pl.pallas_call(functools.partial(gram_kernel, offsets, later, float(total...  11.5 us
    pallas_call x1, Pallas kernels, invert(): pl.pallas_call(invert_kernel, out_shape=jax.ShapeDtypeStruct((PANEL, PANE...  9.39 us
    ppermute x6, waiting for transfers between devices, swap(): return lax.ppermute(value, ('rxn', 'col'), pairs)  5.85 us
    ppermute x6, starting transfers between devices, swap(): return lax.ppermute(value, ('rxn', 'col'), pairs)  2.87 us
    pallas_call x1, Pallas kernels, cut_panel(): pl.pallas_call(cut_kernel, out_shape=[jax.ShapeDtypeStruct((depth, PANEL)...  2.1 us
    pallas_call x1, Pallas kernels, transform(): pl.pallas_call(transform_kernel, out_shape=jax.ShapeDtypeStruct((share, P...  1.51 us
  transfers between devices with their start and end apart: 23, of which 12 were waited for; matrix products, arithmetic and copies ran while one was open for 0% of the time, Pallas kernels for 30%

profile of v2, /device:TPU:0, one launch (start us, length us, event | category | flops | bytes accessed | tf_op | source)
XLA Modules:
  0.0 73.1 jit_solution(11306317940075317480)
XLA Ops:
  0.0 0.1 stack.31.place_ref
  0.1 2.1 %cut_panel.1 = (bf16[384,256]{1,0:T(8,128)(2,1)S(1)}, bf16[384,256]{1,0:T(8,128)(2,1)S(1)}, bf16[384,256]{1,0:T(8,128)(2,1)S(1)}, bf16[384,256]{1,0:T(8,128)(2,1...) custom-call(s32[7]{0:T(128)S(1)} %stack.31.place_ref, ...), custom_call_target="tpu_custom_call" | custom-call | tf_op jit(solution)/shard_map/cut_panel/pallas_call | solution.py:64
  2.2 0.0 copy-start
  2.2 0.0 copy-start.1
  2.2 3.5 %collective-permute-start = (bf16[384,256]{1,0:T(8,128)(2,1)S(1)}, bf16[384,256]{1,0:T(8,128)(2,1)S(1)}, u32[]{:S(2)}, u32[]{:S(2)}) collective-permute-start(bf16[384,256]{1,0:T(8,128)(2,1)S(1)} %get-tuple-element.56), channel_id=1, source_target_pairs={{0,2},{8,10},{16,18},{24,26}} | collective-permute-start | bytes 589832 | tf_op jit(solution)/shard_map/ppermute | solution.py:35
  5.7 1.7 %collective-permute-start.1 = (bf16[384,256]{1,0:T(8,128)(2,1)S(1)}, bf16[384,256]{1,0:T(8,128)(2,1)S(1)}, u32[]{:S(2)}, u32[]{:S(2)}) collective-permute-start(bf16[384,256]{1,0:T(8,128)(2,1)S(1)} %get-tuple-element.57), channel_id=1, source_target_pairs={{0,4},{8,12},{16,20},{24,28}} | collective-permute-start | bytes 589832 | tf_op jit(solution)/shard_map/ppermute | solution.py:35
  7.4 1.3 %collective-permute-start.5 = (bf16[384,256]{1,0:T(8,128)(2,1)S(1)}, bf16[384,256]{1,0:T(8,128)(2,1)S(1)}, u32[]{:S(2)}, u32[]{:S(2)}) collective-permute-start(bf16[384,256]{1,0:T(8,128)(2,1)S(1)} %get-tuple-element.61), channel_id=1, source_target_pairs={{0,1},{8,9},{16,17},{24,25}} | collective-permute-start | bytes 589832 | tf_op jit(solution)/shard_map/ppermute | solution.py:35
  8.7 1.3 %collective-permute-start.7 = (bf16[384,256]{1,0:T(8,128)(2,1)S(1)}, bf16[384,256]{1,0:T(8,128)(2,1)S(1)}, u32[]{:S(2)}, u32[]{:S(2)}) collective-permute-start(bf16[384,256]{1,0:T(8,128)(2,1)S(1)} %get-tuple-element.62), channel_id=1, source_target_pairs={{0,1},{8,9},{16,17},{24,25}} | collective-permute-start | bytes 589832 | tf_op jit(solution)/shard_map/ppermute | solution.py:35
  10.0 1.3 %collective-permute-start.2 = (bf16[384,256]{1,0:T(8,128)(2,1)S(1)}, bf16[384,256]{1,0:T(8,128)(2,1)S(1)}, u32[]{:S(2)}, u32[]{:S(2)}) collective-permute-start(bf16[384,256]{1,0:T(8,128)(2,1)S(1)} %get-tuple-element.58), channel_id=1, source_target_pairs={{0,6},{8,14},{16,22},{24,30}} | collective-permute-start | bytes 589832 | tf_op jit(solution)/shard_map/ppermute | solution.py:35
  11.3 0.0 collective-permute-done
  11.3 1.3 %collective-permute-start.3 = (bf16[384,256]{1,0:T(8,128)(2,1)S(1)}, bf16[384,256]{1,0:T(8,128)(2,1)S(1)}, u32[]{:S(2)}, u32[]{:S(2)}) collective-permute-start(bf16[384,256]{1,0:T(8,128)(2,1)S(1)} %get-tuple-element.59), channel_id=1, source_target_pairs={{0,7},{8,15},{16,23},{24,31}} | collective-permute-start | bytes 589832 | tf_op jit(solution)/shard_map/ppermute | solution.py:35
  12.6 2.5 %collective-permute-done.1 = bf16[384,256]{1,0:T(8,128)(2,1)S(1)} collective-permute-done((bf16[384,256]{1,0:T(8,128)(2,1)S(1)}, bf16[384,256]{1,0:T(8,128)(2,1)S(1)}, u32[]{:S(2)}, u32[]{:S(2)}) %collective-permute-start.1) | collective-permute-done | bytes 196640 | tf_op jit(solution)/shard_map/ppermute | solution.py:35
  15.2 1.3 %collective-permute-start.4 = (bf16[384,256]{1,0:T(8,128)(2,1)S(1)}, bf16[384,256]{1,0:T(8,128)(2,1)S(1)}, u32[]{:S(2)}, u32[]{:S(2)}) collective-permute-start(bf16[384,256]{1,0:T(8,128)(2,1)S(1)} %get-tuple-element.60), channel_id=1, source_target_pairs={{0,1},{8,9},{16,17},{24,25}} | collective-permute-start | bytes 589832 | tf_op jit(solution)/shard_map/ppermute | solution.py:35
  16.5 0.0 collective-permute-done.5
  16.5 0.7 collective-permute-start.6
  17.2 1.0 %collective-permute-done.7 = bf16[384,256]{1,0:T(8,128)(2,1)S(1)} collective-permute-done((bf16[384,256]{1,0:T(8,128)(2,1)S(1)}, bf16[384,256]{1,0:T(8,128)(2,1)S(1)}, u32[]{:S(2)}, u32[]{:S(2)}) %collective-permute-start.7) | collective-permute-done | bytes 196640 | tf_op jit(solution)/shard_map/ppermute | solution.py:35
  18.2 0.7 collective-permute-start.8
  18.9 0.5 collective-permute-done.2
  19.4 3.1 %collective-permute-done.3 = bf16[384,256]{1,0:T(8,128)(2,1)S(1)} collective-permute-done((bf16[384,256]{1,0:T(8,128)(2,1)S(1)}, bf16[384,256]{1,0:T(8,128)(2,1)S(1)}, u32[]{:S(2)}, u32[]{:S(2)}) %collective-permute-start.3) | collective-permute-done | bytes 196640 | tf_op jit(solution)/shard_map/ppermute | solution.py:35
  22.5 0.0 collective-permute-done.4
  22.5 0.0 collective-permute-done.6
  22.5 0.0 collective-permute-done.8
  22.5 0.1 add_add_fusion.refs_0_
  22.6 2.7 %collective-permute-start.10 = (bf16[384,256]{1,0:T(8,128)(2,1)S(1)}, bf16[384,256]{1,0:T(8,128)(2,1)S(1)}, u32[]{:S(2)}, u32[]{:S(2)}) collective-permute-start(bf16[384,256]{1,0:T(8,128)(2,1)S(1)} %add_add_fusion.refs_0_), channel_id=1, source_target_pairs={{2,0},{4,2},{6,4},{7,6},{5,7},{3,5},{1,3},{0,1},{10,8},{12,10},{14... | collective-permute-start | bytes 589832 | tf_op jit(solution)/shard_map/ppermute | solution.py:35
  25.3 0.0 collective-permute-start.9
  25.3 0.0 copy-done
  25.3 0.0 copy-done.1
  25.3 3.2 %gram.4 = (f32[4,256,512]{2,1,0:T(8,128)S(1)}, f32[256,256]{1,0:T(8,128)S(1)}, bf16[384,2048]{1,0:T(8,128)(2,1)S(1)}, bf16[384,2048]{1,0:T(8,128)(2,1)S(1)}) custom-call(s32[7]{0:T(128)S(1)} %stack.31.place_ref, f32[8,384]{1,0:T(8,128)S(1)} %reshape.6.lower_ref, f32[8,384]{1,0:T(8,128)S(1)} %reshape.7.upper_ref, bf16[3072,2048]{1,0:T(8,128)(2,1)} %basis_ref.9, ...), custom_call_target="tpu_custom_call" | custom-call | flops 402653184 | bytes 5767168 | tf_op jit(solution)/shard_map/gram/pallas_call | solution.py:208
  28.6 0.0 collective-permute-done.10.refs_1_
  28.6 3.3 %collective-permute-done.9.refs_0_ = bf16[384,256]{1,0:T(8,128)(2,1)S(1)} collective-permute-done((bf16[384,256]{1,0:T(8,128)(2,1)S(1)}, bf16[384,256]{1,0:T(8,128)(2,1)S(1)}, u32[]{:S(2)}, u32[]{:S(2)}) %collective-permute-start.9) | collective-permute-done | bytes 196640 | tf_op jit(solution)/shard_map/ppermute | solution.py:35
  31.9 0.0 collective-permute-start.11
  31.9 2.3 %collective-permute-start.12 = (bf16[384,256]{1,0:T(8,128)(2,1)S(1)}, bf16[384,256]{1,0:T(8,128)(2,1)S(1)}, u32[]{:S(2)}, u32[]{:S(2)}) collective-permute-start(bf16[384,256]{1,0:T(8,128)(2,1)S(1)} %collective-permute-done.10.refs_1_), channel_id=1, source_target_pairs={{2,0},{4,2},{6,4},{7,6},{5,7},{3,5},{1,3},{0,1},{10,8},{12,10},{14... | collective-permute-start | bytes 589832 | tf_op jit(solution)/shard_map/ppermute | solution.py:35
  34.2 2.8 %gram.5 = (f32[4,256,512]{2,1,0:T(8,128)S(1)}, f32[256,256]{1,0:T(8,128)S(1)}, bf16[384,2048]{1,0:T(8,128)(2,1)S(1)}, bf16[384,2048]{1,0:T(8,128)(2,1)S(1)}) custom-call(s32[7]{0:T(128)S(1)} %stack.31.place_ref, f32[8,384]{1,0:T(8,128)S(1)} %reshape.6.lower_ref, f32[8,384]{1,0:T(8,128)S(1)} %reshape.7.upper_ref, ...), custom_call_target="tpu_custom_call", output_to_operand_aliasing={{0}: (8, {}), {1}: (9, {})} | custom-call | flops 805306368 | bytes 7340032 | tf_op jit(solution)/shard_map/gram/pallas_call | solution.py:208
  37.0 2.6 %collective-permute-done.11.refs_0_ = bf16[384,256]{1,0:T(8,128)(2,1)S(1)} collective-permute-done((bf16[384,256]{1,0:T(8,128)(2,1)S(1)}, bf16[384,256]{1,0:T(8,128)(2,1)S(1)}, u32[]{:S(2)}, u32[]{:S(2)}) %collective-permute-start.11) | collective-permute-done | bytes 196640 | tf_op jit(solution)/shard_map/ppermute | solution.py:35
  39.6 0.0 collective-permute-done.12.refs_1_
  39.6 0.0 collective-permute-start.13
  39.6 2.2 %collective-permute-start.14 = (bf16[384,256]{1,0:T(8,128)(2,1)S(1)}, bf16[384,256]{1,0:T(8,128)(2,1)S(1)}, u32[]{:S(2)}, u32[]{:S(2)}) collective-permute-start(bf16[384,256]{1,0:T(8,128)(2,1)S(1)} %collective-permute-done.12.refs_1_), channel_id=1, source_target_pairs={{2,0},{4,2},{6,4},{7,6},{5,7},{3,5},{1,3},{0,1},{10,8},{12,10},{14... | collective-permute-start | bytes 589832 | tf_op jit(solution)/shard_map/ppermute | solution.py:35
  41.8 2.8 %gram.6 = (f32[4,256,512]{2,1,0:T(8,128)S(1)}, f32[256,256]{1,0:T(8,128)S(1)}, bf16[384,2048]{1,0:T(8,128)(2,1)S(1)}, bf16[384,2048]{1,0:T(8,128)(2,1)S(1)}) custom-call(s32[7]{0:T(128)S(1)} %stack.31.place_ref, f32[8,384]{1,0:T(8,128)S(1)} %reshape.6.lower_ref, f32[8,384]{1,0:T(8,128)S(1)} %reshape.7.upper_ref, ...), custom_call_target="tpu_custom_call", output_to_operand_aliasing={{0}: (8, {}), {1}: (9, {})} | custom-call | flops 805306368 | bytes 7340032 | tf_op jit(solution)/shard_map/gram/pallas_call | solution.py:208
  44.6 1.4 %collective-permute-done.13.refs_0_ = bf16[384,256]{1,0:T(8,128)(2,1)S(1)} collective-permute-done((bf16[384,256]{1,0:T(8,128)(2,1)S(1)}, bf16[384,256]{1,0:T(8,128)(2,1)S(1)}, u32[]{:S(2)}, u32[]{:S(2)}) %collective-permute-start.13) | collective-permute-done | bytes 196640 | tf_op jit(solution)/shard_map/ppermute | solution.py:35
  46.0 0.0 collective-permute-done.14.refs_1_
  46.1 0.3 collective-permute-start.15
  46.4 1.8 %collective-permute-start.16 = (bf16[192,256]{1,0:T(8,128)(2,1)S(1)}, bf16[192,256]{1,0:T(8,128)(2,1)S(1)}, u32[]{:S(2)}, u32[]{:S(2)}) collective-permute-start(bf16[192,256]{1,0:T(8,128)(2,1)S(1)} %slice.7), channel_id=1, source_target_pairs={{2,0},{4,2},{6,4},{7,6},{5,7},{3,5},{1,3},{0,1},{10,8},{12,10},{14... | collective-permute-start | bytes 294920 | tf_op jit(solution)/shard_map/ppermute | solution.py:35
  48.2 2.8 %gram.7 = (f32[4,256,512]{2,1,0:T(8,128)S(1)}, f32[256,256]{1,0:T(8,128)S(1)}, bf16[384,2048]{1,0:T(8,128)(2,1)S(1)}) custom-call(s32[7]{0:T(128)S(1)} %stack.31.place_ref, f32[8,384]{1,0:T(8,128)S(1)} %reshape.6.lower_ref, f32[8,384]{1,0:T(8,128)S(1)} %reshape.7.upper_ref, ...), custom_call_target="tpu_custom_call", output_to_operand_aliasing={{0}: (8, {}), {1}: (9, {})} | custom-call | flops 805306368 | bytes 7340032 | tf_op jit(solution)/shard_map/gram/pallas_call | solution.py:208
  51.0 0.0 collective-permute-done.15.top_ref
  51.0 0.2 collective-permute-done.16.bottom_ref
  51.2 1.1 %last.1 = (f32[1,256,512]{2,1,0:T(8,128)S(1)}, f32[1,256,512]{2,1,0:T(8,128)S(1)}, f32[128,256]{1,0:T(8,128)S(1)}, f32[128,256]{1,0:T(8,128)S(1)}, bf16[256,384]{1,0:T(8,128)(2,1)S(1)}) custom-call(s32[7]{0:T(128)S(1)} %stack.31.place_ref, f32[8,384]{1,0:T(8,128)S(1)} %reshape.6.lower_ref, f32[8,384]{1,0:T(8,128)S(1)} %reshape.7.upper_ref, ...), custom_call_target="tpu_custom_call" | custom-call | flops 201326592 | bytes 2097152 | tf_op jit(solution)/shard_map/last/pallas_call | solution.py:265
  52.3 0.1 collective-permute-start.18
  52.4 0.5 collective-permute-start.17
  52.9 1.6 %collective-permute-done.17 = f32[128,256]{1,0:T(8,128)S(1)} collective-permute-done((f32[128,256]{1,0:T(8,128)S(1)}, f32[128,256]{1,0:T(8,128)S(1)}, u32[]{:S(2)}, u32[]{:S(2)}) %collective-permute-start.17) | collective-permute-done | bytes 131104 | tf_op jit(solution)/shard_map/ppermute | solution.py:42
  54.5 0.0 collective-permute-done.18
  54.5 0.1 add.68
  54.6 1.6 %collective-permute-start.19 = (f32[128,256]{1,0:T(8,128)S(1)}, f32[128,256]{1,0:T(8,128)S(1)}, u32[]{:S(2)}, u32[]{:S(2)}) collective-permute-start(f32[128,256]{1,0:T(8,128)S(1)} %add.67), channel_id=1, source_target_pairs={{0,16},{1,17},{2,18},{3,19},{4,20},{5,21},{6,22},{7,23},{8,24},{9,... | collective-permute-start | bytes 393224 | tf_op jit(solution)/shard_map/ppermute | solution.py:42
  56.2 1.0 %rest.1 = (f32[1,256,512]{2,1,0:T(8,128)S(1)}, f32[1,256,512]{2,1,0:T(8,128)S(1)}) custom-call(s32[7]{0:T(128)S(1)} %stack.31.place_ref, bf16[256,384]{1,0:T(8,128)(2,1)S(1)} %get-tuple-element.101.weighted_ref, bf16[384,2048]{1,0:T(8,128)(2,1)S(1)} %get-tuple-element.93.tile_ref, f32[4,256,512]{2,1,0:T(8,128)S(1)} %get-tuple-element.94.refs_0_.gram_ref), custom_call_target="tpu_custom_call" | custom-call | flops 201326592 | bytes 2097152 | tf_op jit(solution)/shard_map/rest/pallas_call | solution.py:275
  57.1 0.1 collective-permute-start.21
  57.2 0.6 collective-permute-start.22
  57.8 2.4 %collective-permute-done.19 = f32[128,256]{1,0:T(8,128)S(1)} collective-permute-done((f32[128,256]{1,0:T(8,128)S(1)}, f32[128,256]{1,0:T(8,128)S(1)}, u32[]{:S(2)}, u32[]{:S(2)}) %collective-permute-start.19) | collective-permute-done | bytes 131104 | tf_op jit(solution)/shard_map/ppermute | solution.py:42
  60.2 0.1 collective-permute-start.20
  60.3 1.3 %collective-permute-done.20.other_ref = f32[128,256]{1,0:T(8,128)S(1)} collective-permute-done((f32[128,256]{1,0:T(8,128)S(1)}, f32[128,256]{1,0:T(8,128)S(1)}, u32[]{:S(2)}, u32[]{:S(2)}) %collective-permute-start.20) | collective-permute-done | bytes 131104 | tf_op jit(solution)/shard_map/ppermute | solution.py:42
  61.6 9.4 %invert.1.inverse_ref = f32[256,256]{1,0:T(8,128)S(1)} custom-call(s32[7]{0:T(128)S(1)} %stack.31.place_ref, f32[128,256]{1,0:T(8,128)S(1)} %add.69.mine_ref, f32[128,256]{1,0:T(8,128)S(1)} %collective-permute-done.20.other_ref), custom_call_target="tpu_custom_call" | custom-call | flops 3000000000 | bytes 524288 | tf_op jit(solution)/shard_map/invert/pallas_call | solution.py:133
  71.0 0.0 collective-permute-done.21.refs_1_
  71.0 0.5 collective-permute-done.22.refs_2_
  71.6 1.5 %transform.1 = f32[512,256]{1,0:T(8,128)} custom-call(f32[256,256]{1,0:T(8,128)S(1)} %invert.1.inverse_ref, f32[1,256,512]{2,1,0:T(8,128)S(1)} %get-tuple-element.102.refs_0_, f32[1,256,512]{2,1,0:T(8,128)S(1)} %collective-permute-done.21.refs_1_, f32[1,256,512]{2,1,0:T(8,128)S(1)} %collective-permute-done.22.refs_2_), custom_call_target="tpu_custom_call" | custom-call | flops 402653184 | bytes 1572864 | tf_op jit(solution)/shard_map/transform/pallas_call | solution.py:298
  (6 shorter events, 0.1 us)
Async XLA Ops:
  2.2 23.1 %copy-start = (f32[3072]{0:T(1024)S(1)}, f32[3072]{0:T(1024)}, u32[]{:S(2)}) copy-start(f32[3072]{0:T(1024)} %param.4) | copy-start | bytes 36868
  2.2 23.1 %copy-start.1 = (f32[3072]{0:T(1024)S(1)}, f32[3072]{0:T(1024)}, u32[]{:S(2)}) copy-start(f32[3072]{0:T(1024)} %param.5) | copy-start | bytes 36868
  2.2 9.1 %collective-permute-start = (bf16[384,256]{1,0:T(8,128)(2,1)S(1)}, bf16[384,256]{1,0:T(8,128)(2,1)S(1)}, u32[]{:S(2)}, u32[]{:S(2)}) collective-permute-start(bf16[384,256]{1,0:T(8,128)(2,1)S(1)} %get-tuple-element.56), channel_id=1, source_target_pairs={{0,2},{8,10},{16,18},{24,26}} | collective-permute-start | bytes 589832 | tf_op jit(solution)/shard_map/ppermute | solution.py:35
  5.7 9.5 %collective-permute-start.1 = (bf16[384,256]{1,0:T(8,128)(2,1)S(1)}, bf16[384,256]{1,0:T(8,128)(2,1)S(1)}, u32[]{:S(2)}, u32[]{:S(2)}) collective-permute-start(bf16[384,256]{1,0:T(8,128)(2,1)S(1)} %get-tuple-element.57), channel_id=1, source_target_pairs={{0,4},{8,12},{16,20},{24,28}} | collective-permute-start | bytes 589832 | tf_op jit(solution)/shard_map/ppermute | solution.py:35
  7.4 9.1 %collective-permute-start.5 = (bf16[384,256]{1,0:T(8,128)(2,1)S(1)}, bf16[384,256]{1,0:T(8,128)(2,1)S(1)}, u32[]{:S(2)}, u32[]{:S(2)}) collective-permute-start(bf16[384,256]{1,0:T(8,128)(2,1)S(1)} %get-tuple-element.61), channel_id=1, source_target_pairs={{0,1},{8,9},{16,17},{24,25}} | collective-permute-start | bytes 589832 | tf_op jit(solution)/shard_map/ppermute | solution.py:35
  8.7 9.5 %collective-permute-start.7 = (bf16[384,256]{1,0:T(8,128)(2,1)S(1)}, bf16[384,256]{1,0:T(8,128)(2,1)S(1)}, u32[]{:S(2)}, u32[]{:S(2)}) collective-permute-start(bf16[384,256]{1,0:T(8,128)(2,1)S(1)} %get-tuple-element.62), channel_id=1, source_target_pairs={{0,1},{8,9},{16,17},{24,25}} | collective-permute-start | bytes 589832 | tf_op jit(solution)/shard_map/ppermute | solution.py:35
  10.0 9.4 %collective-permute-start.2 = (bf16[384,256]{1,0:T(8,128)(2,1)S(1)}, bf16[384,256]{1,0:T(8,128)(2,1)S(1)}, u32[]{:S(2)}, u32[]{:S(2)}) collective-permute-start(bf16[384,256]{1,0:T(8,128)(2,1)S(1)} %get-tuple-element.58), channel_id=1, source_target_pairs={{0,6},{8,14},{16,22},{24,30}} | collective-permute-start | bytes 589832 | tf_op jit(solution)/shard_map/ppermute | solution.py:35
  11.3 11.1 %collective-permute-start.3 = (bf16[384,256]{1,0:T(8,128)(2,1)S(1)}, bf16[384,256]{1,0:T(8,128)(2,1)S(1)}, u32[]{:S(2)}, u32[]{:S(2)}) collective-permute-start(bf16[384,256]{1,0:T(8,128)(2,1)S(1)} %get-tuple-element.59), channel_id=1, source_target_pairs={{0,7},{8,15},{16,23},{24,31}} | collective-permute-start | bytes 589832 | tf_op jit(solution)/shard_map/ppermute | solution.py:35
  15.2 7.3 %collective-permute-start.4 = (bf16[384,256]{1,0:T(8,128)(2,1)S(1)}, bf16[384,256]{1,0:T(8,128)(2,1)S(1)}, u32[]{:S(2)}, u32[]{:S(2)}) collective-permute-start(bf16[384,256]{1,0:T(8,128)(2,1)S(1)} %get-tuple-element.60), channel_id=1, source_target_pairs={{0,1},{8,9},{16,17},{24,25}} | collective-permute-start | bytes 589832 | tf_op jit(solution)/shard_map/ppermute | solution.py:35
  16.5 6.0 %collective-permute-start.6 = (bf16[384,256]{1,0:T(8,128)(2,1)S(1)}, bf16[384,256]{1,0:T(8,128)(2,1)S(1)}, u32[]{:S(2)}, u32[]{:S(2)}) collective-permute-start(bf16[384,256]{1,0:T(8,128)(2,1)S(1)} %collective-permute-done.5), channel_id=1, source_target_pairs={{1,5},{9,13},{17,21},{25,29}} | collective-permute-start | bytes 589832 | tf_op jit(solution)/shard_map/ppermute | solution.py:35
  18.2 4.3 %collective-permute-start.8 = (bf16[384,256]{1,0:T(8,128)(2,1)S(1)}, bf16[384,256]{1,0:T(8,128)(2,1)S(1)}, u32[]{:S(2)}, u32[]{:S(2)}) collective-permute-start(bf16[384,256]{1,0:T(8,128)(2,1)S(1)} %collective-permute-done.7), channel_id=1, source_target_pairs={{1,3},{9,11},{17,19},{25,27}} | collective-permute-start | bytes 589832 | tf_op jit(solution)/shard_map/ppermute | solution.py:35
  22.6 6.0 %collective-permute-start.10 = (bf16[384,256]{1,0:T(8,128)(2,1)S(1)}, bf16[384,256]{1,0:T(8,128)(2,1)S(1)}, u32[]{:S(2)}, u32[]{:S(2)}) collective-permute-start(bf16[384,256]{1,0:T(8,128)(2,1)S(1)} %add_add_fusion.refs_0_), channel_id=1, source_target_pairs={{2,0},{4,2},{6,4},{7,6},{5,7},{3,5},{1,3},{0,1},{10,8},{12,10},{14... | collective-permute-start | bytes 589832 | tf_op jit(solution)/shard_map/ppermute | solution.py:35
  25.3 6.6 %collective-permute-start.9 = (bf16[384,256]{1,0:T(8,128)(2,1)S(1)}, bf16[384,256]{1,0:T(8,128)(2,1)S(1)}, u32[]{:S(2)}, u32[]{:S(2)}) collective-permute-start(bf16[384,256]{1,0:T(8,128)(2,1)S(1)} %add_add_fusion.refs_0_), channel_id=1, source_target_pairs={{0,2},{2,4},{4,6},{6,7},{7,5},{5,3},{3,1},{1,0},{8,10},{10,12},{12... | collective-permute-start | bytes 589832 | tf_op jit(solution)/shard_map/ppermute | solution.py:35
  31.9 7.7 %collective-permute-start.11 = (bf16[384,256]{1,0:T(8,128)(2,1)S(1)}, bf16[384,256]{1,0:T(8,128)(2,1)S(1)}, u32[]{:S(2)}, u32[]{:S(2)}) collective-permute-start(bf16[384,256]{1,0:T(8,128)(2,1)S(1)} %collective-permute-done.9.refs_0_), channel_id=1, source_target_pairs={{0,2},{2,4},{4,6},{6,7},{7,5},{5,3},{3,1},{1,0},{8,10},{10,12},{12... | collective-permute-start | bytes 589832 | tf_op jit(solution)/shard_map/ppermute | solution.py:35
  31.9 7.7 %collective-permute-start.12 = (bf16[384,256]{1,0:T(8,128)(2,1)S(1)}, bf16[384,256]{1,0:T(8,128)(2,1)S(1)}, u32[]{:S(2)}, u32[]{:S(2)}) collective-permute-start(bf16[384,256]{1,0:T(8,128)(2,1)S(1)} %collective-permute-done.10.refs_1_), channel_id=1, source_target_pairs={{2,0},{4,2},{6,4},{7,6},{5,7},{3,5},{1,3},{0,1},{10,8},{12,10},{14... | collective-permute-start | bytes 589832 | tf_op jit(solution)/shard_map/ppermute | solution.py:35
  39.6 6.4 %collective-permute-start.13 = (bf16[384,256]{1,0:T(8,128)(2,1)S(1)}, bf16[384,256]{1,0:T(8,128)(2,1)S(1)}, u32[]{:S(2)}, u32[]{:S(2)}) collective-permute-start(bf16[384,256]{1,0:T(8,128)(2,1)S(1)} %collective-permute-done.11.refs_0_), channel_id=1, source_target_pairs={{0,2},{2,4},{4,6},{6,7},{7,5},{5,3},{3,1},{1,0},{8,10},{10,12},{12... | collective-permute-start | bytes 589832 | tf_op jit(solution)/shard_map/ppermute | solution.py:35
  39.6 6.5 %collective-permute-start.14 = (bf16[384,256]{1,0:T(8,128)(2,1)S(1)}, bf16[384,256]{1,0:T(8,128)(2,1)S(1)}, u32[]{:S(2)}, u32[]{:S(2)}) collective-permute-start(bf16[384,256]{1,0:T(8,128)(2,1)S(1)} %collective-permute-done.12.refs_1_), channel_id=1, source_target_pairs={{2,0},{4,2},{6,4},{7,6},{5,7},{3,5},{1,3},{0,1},{10,8},{12,10},{14... | collective-permute-start | bytes 589832 | tf_op jit(solution)/shard_map/ppermute | solution.py:35
  46.1 4.9 %collective-permute-start.15 = (bf16[192,256]{1,0:T(8,128)(2,1)S(1)}, bf16[192,256]{1,0:T(8,128)(2,1)S(1)}, u32[]{:S(2)}, u32[]{:S(2)}) collective-permute-start(bf16[192,256]{1,0:T(8,128)(2,1)S(1)} %slice.6), channel_id=1, source_target_pairs={{0,2},{2,4},{4,6},{6,7},{7,5},{5,3},{3,1},{1,0},{8,10},{10,12},{12... | collective-permute-start | bytes 294920 | tf_op jit(solution)/shard_map/ppermute | solution.py:35
  46.4 4.7 %collective-permute-start.16 = (bf16[192,256]{1,0:T(8,128)(2,1)S(1)}, bf16[192,256]{1,0:T(8,128)(2,1)S(1)}, u32[]{:S(2)}, u32[]{:S(2)}) collective-permute-start(bf16[192,256]{1,0:T(8,128)(2,1)S(1)} %slice.7), channel_id=1, source_target_pairs={{2,0},{4,2},{6,4},{7,6},{5,7},{3,5},{1,3},{0,1},{10,8},{12,10},{14... | collective-permute-start | bytes 294920 | tf_op jit(solution)/shard_map/ppermute | solution.py:35
  52.3 2.2 %collective-permute-start.18 = (f32[1,256,512]{2,1,0:T(8,128)S(1)}, f32[1,256,512]{2,1,0:T(8,128)S(1)}, u32[]{:S(2)}, u32[]{:S(2)}) collective-permute-start(f32[1,256,512]{2,1,0:T(8,128)S(1)} %get-tuple-element.99), channel_id=1, source_target_pairs={{0,8},{1,9},{2,10},{3,11},{4,12},{5,13},{6,14},{7,15},{8,0},{9,1},... | collective-permute-start | bytes 1572872 | tf_op jit(solution)/shard_map/ppermute | solution.py:42
  52.4 2.1 %collective-permute-start.17 = (f32[128,256]{1,0:T(8,128)S(1)}, f32[128,256]{1,0:T(8,128)S(1)}, u32[]{:S(2)}, u32[]{:S(2)}) collective-permute-start(f32[128,256]{1,0:T(8,128)S(1)} %get-tuple-element.97), channel_id=1, source_target_pairs={{0,8},{1,9},{2,10},{3,11},{4,12},{5,13},{6,14},{7,15},{8,0},{9,1},... | collective-permute-start | bytes 393224 | tf_op jit(solution)/shard_map/ppermute | solution.py:42
  54.6 5.6 %collective-permute-start.19 = (f32[128,256]{1,0:T(8,128)S(1)}, f32[128,256]{1,0:T(8,128)S(1)}, u32[]{:S(2)}, u32[]{:S(2)}) collective-permute-start(f32[128,256]{1,0:T(8,128)S(1)} %add.67), channel_id=1, source_target_pairs={{0,16},{1,17},{2,18},{3,19},{4,20},{5,21},{6,22},{7,23},{8,24},{9,... | collective-permute-start | bytes 393224 | tf_op jit(solution)/shard_map/ppermute | solution.py:42
  57.1 13.9 %collective-permute-start.21 = (f32[1,256,512]{2,1,0:T(8,128)S(1)}, f32[1,256,512]{2,1,0:T(8,128)S(1)}, u32[]{:S(2)}, u32[]{:S(2)}) collective-permute-start(f32[1,256,512]{2,1,0:T(8,128)S(1)} %get-tuple-element.103), channel_id=1, source_target_pairs={{0,8},{1,9},{2,10},{3,11},{4,12},{5,13},{6,14},{7,15},{8,0},{9,1},... | collective-permute-start | bytes 1572872 | tf_op jit(solution)/shard_map/ppermute | solution.py:42
  57.2 14.3 %collective-permute-start.22 = (f32[1,256,512]{2,1,0:T(8,128)S(1)}, f32[1,256,512]{2,1,0:T(8,128)S(1)}, u32[]{:S(2)}, u32[]{:S(2)}) collective-permute-start(f32[1,256,512]{2,1,0:T(8,128)S(1)} %add.68), channel_id=1, source_target_pairs={{0,16},{1,17},{2,18},{3,19},{4,20},{5,21},{6,22},{7,23},{8,24},{9,... | collective-permute-start | bytes 1572872 | tf_op jit(solution)/shard_map/ppermute | solution.py:42
  60.2 1.4 %collective-permute-start.20 = (f32[128,256]{1,0:T(8,128)S(1)}, f32[128,256]{1,0:T(8,128)S(1)}, u32[]{:S(2)}, u32[]{:S(2)}) collective-permute-start(f32[128,256]{1,0:T(8,128)S(1)} %add.69.mine_ref), channel_id=1, source_target_pairs={{0,8},{1,9},{2,10},{3,11},{4,12},{5,13},{6,14},{7,15},{8,0},{9,1},... | collective-permute-start | bytes 393224 | tf_op jit(solution)/shard_map/ppermute | solution.py:42

commit v3 on v2

--- a/solution.py
+++ b/solution.py
@@ -42,31 +42,33 @@
     return lax.ppermute(value, ("rxn", "col"), pairs)
 
 
-def cut_kernel(place_ref, basis_ref, *refs):
+def cut_kernel(choices, place_ref, basis_ref, *refs):
     pieces, sems = refs[:-1], refs[-1]
     pieces[0][...] = jnp.zeros_like(pieces[0])
 
     @pl.when(place_ref[COLUMN] == 0)
     def _():
         depth = pieces[0].shape[0]
-        copies = [
-            pltpu.make_async_copy(basis_ref.at[pl.ds(p * depth, depth), pl.ds(0, PANEL)], piece, sems.at[p])
-            for p, piece in enumerate(pieces)
-        ]
+        copies = []
+        for i, (piece, choice) in enumerate(zip(pieces, choices)):
+            row = pl.multiple_of(jnp.where(place_ref[CORE] == 0, choice[0], choice[1]) * depth, depth)
+            copies.append(
+                pltpu.make_async_copy(basis_ref.at[pl.ds(row, depth), pl.ds(0, PANEL)], piece, sems.at[i])
+            )
         for copy in copies:
             copy.start()
         for copy in copies:
             copy.wait()
 
 
-def cut_panel(place, basis, count):
+def cut_panel(place, basis, choices, count):
     depth = basis.shape[0] // count
     return pl.pallas_call(
-        cut_kernel,
-        out_shape=[jax.ShapeDtypeStruct((depth, PANEL), jnp.bfloat16)] * count,
+        functools.partial(cut_kernel, choices),
+        out_shape=[jax.ShapeDtypeStruct((depth, PANEL), jnp.bfloat16)] * len(choices),
         in_specs=[SMEM, HBM],
-        out_specs=[VMEM] * count,
-        scratch_shapes=[pltpu.SemaphoreType.DMA((count,))],
+        out_specs=[VMEM] * len(choices),
+        scratch_shapes=[pltpu.SemaphoreType.DMA((len(choices),))],
         compiler_params=PARAMS,
         name="cut_panel",
     )(place, basis)
@@ -90,14 +92,13 @@
     return jnp.concatenate(done, 0)
 
 
-def invert_kernel(place_ref, mine_ref, other_ref, out_ref, work):
-    core = place_ref[CORE]
-    mine = pl.ds(pl.multiple_of(core * HALF, HALF), HALF)
-    other = pl.ds(pl.multiple_of((1 - core) * HALF, HALF), HALF)
-    work[mine, :PANEL] = mine_ref[...]
-    work[other, :PANEL] = other_ref[...]
-    gram = work[:, :PANEL]
-    work[:, :PANEL] = 0.5 * (gram + gram.T)
+def invert_kernel(place_ref, mine_ref, other_ref, out_ref, work, lower):
+    core, part = place_ref[CORE], mine_ref.shape[0]
+    lower[pl.ds(pl.multiple_of(core * part, part), part), :] = mine_ref[...]
+    lower[pl.ds(pl.multiple_of((1 - core) * part, part), part), :] = other_ref[...]
+    work[:, :HALF] = lower[:PANEL, :]
+    work[:HALF, HALF:PANEL] = lower[HALF:PANEL, :].T
+    work[HALF:, HALF:PANEL] = lower[PANEL:, :]
     row = lax.broadcasted_iota(jnp.int32, (PANEL, PANEL), 0)
     col = lax.broadcasted_iota(jnp.int32, (PANEL, PANEL), 1)
     work[:, PANEL:] = jnp.where(row == col, 1.0, 0.0).astype(F32)
@@ -135,9 +136,9 @@
         out_shape=jax.ShapeDtypeStruct((PANEL, PANEL), F32),
         in_specs=[SMEM, VMEM, VMEM],
         out_specs=VMEM,
-        scratch_shapes=[pltpu.VMEM((PANEL, 2 * PANEL), F32)],
-        compiler_params=PARAMS,
-        cost_estimate=pl.CostEstimate(flops=3*10**9, bytes_accessed=2**19, transcendentals=0),
+        scratch_shapes=[pltpu.VMEM((PANEL, 2 * PANEL), F32), pltpu.VMEM((3 * HALF, HALF), F32)],
+        compiler_params=PARAMS,
+        cost_estimate=pl.CostEstimate(flops=4*10**9, bytes_accessed=2**19, transcendentals=0),
         name="invert",
     )(place, mine, other)
 
@@ -233,10 +234,13 @@
     piece = jnp.concatenate([top_ref[...], bottom_ref[...]], 0)
     at = piece_at(place_ref, offset, lower_ref.shape[0])
     weighted_ref[...] = weigh(total, at, lower_ref, upper_ref, piece)
-    sum_ref[...] = diagonal_ref[...] + jnp.dot(weighted_ref[...], piece, preferred_element_type=F32)
-    core = place_ref[CORE]
-    mine_ref[...] = sum_ref[pl.ds(pl.multiple_of(core * HALF, HALF), HALF), :]
-    other_ref[...] = sum_ref[pl.ds(pl.multiple_of((1 - core) * HALF, HALF), HALF), :]
+    diagonal = diagonal_ref[...] + jnp.dot(weighted_ref[...], piece, preferred_element_type=F32)
+    diagonal = 0.5 * (diagonal + diagonal.T)
+    sum_ref[:PANEL, :] = diagonal[:, :HALF]
+    sum_ref[PANEL:, :] = diagonal[HALF:, HALF:]
+    core, part = place_ref[CORE], mine_ref.shape[0]
+    mine_ref[...] = sum_ref[pl.ds(pl.multiple_of(core * part, part), part), :]
+    other_ref[...] = sum_ref[pl.ds(pl.multiple_of((1 - core) * part, part), part), :]
     add_blocks(place_ref, gram_ref, weighted_ref, tile_ref, [(3, sent_ref), (1, away_ref)])
 
 
@@ -260,14 +264,14 @@
     shares, _, share = gram.shape
     depth = tile.shape[0]
     quarter = jax.ShapeDtypeStruct((shares // 4, PANEL, share), F32)
-    half = jax.ShapeDtypeStruct((HALF, PANEL), F32)
+    half = jax.ShapeDtypeStruct((3 * HALF // 2, HALF), F32)
     cost = pl.CostEstimate(flops=depth * PANEL * share * shares, bytes_accessed=2**21, transcendentals=0)
     third, first, mine, other, weighted = pl.pallas_call(
         functools.partial(last_kernel, offset, float(total)),
         out_shape=[quarter, quarter, half, half, jax.ShapeDtypeStruct((PANEL, depth), jnp.bfloat16)],
         in_specs=[SMEM] + [VMEM] * 7,
         out_specs=[VMEM] * 5,
-        scratch_shapes=[pltpu.VMEM((PANEL, PANEL), F32)],
+        scratch_shapes=[pltpu.VMEM((3 * HALF, HALF), F32)],
         compiler_params=PARAMS,
         cost_estimate=cost,
         name="last",
@@ -318,17 +322,29 @@
     blocks = [me ^ reverse_bits(j, shares) for j in range(shares)]
     place = jnp.stack([column, me % 2, at, *blocks]).astype(jnp.int32)
     basis = pltpu.with_memory_space_constraint(basis, pltpu.HBM)
-    pieces = cut_panel(place, basis, columns)
     slacks = [x.reshape(columns, rows // columns) for x in (lower_slack, upper_slack)]
     shared = (place, *slacks, basis)
 
-    through, near = range(middle + 1, columns - 1), range(1, middle + 1)
-    to_relay = lambda p: to_column(pieces[p], [(0, relay)])
-    parts = [to_column(pieces[p], [(0, order[p])]) for p in near]
-    far = [to_relay(p) for p in through]
-    parts.append(to_relay(columns - 1))
-    parts += [to_column(x, [(relay, order[p])]) for x, p in zip(far, through)]
-    held = functools.reduce(lambda a, b: a + b, parts, pieces[0])
+    near, far = range(1, middle), range(middle + 1, columns)
+    choices = [(0, 0), (middle, middle)]
+    for pair in zip(near, far):
+        choices += [pair, pair[::-1]]
+    first, alone, *pieces = cut_panel(place, basis, choices, columns)
+    held = first + to_column(alone, [(0, order[middle])])
+    for i, (p, q) in enumerate(zip(near, far)):
+        came = [
+            lax.ppermute(
+                pieces[2 * i + k],
+                ("rxn", "col"),
+                [(r * columns, r * columns + (order[p] if r % 2 == k else relay)) for r in range(shares)],
+            )
+            for k in range(2)
+        ]
+        pair = came[0] + came[1]
+        if order[q] != relay:
+            held = held + to_column(pair, [(relay, order[q])])
+            pair = jnp.where(column == relay, 0, pair)
+        held = held + pair
 
     forward = [(order[i], order[(i + 1) % columns]) for i in range(columns)]
     backward = [(b, a) for a, b in forward]
@@ -339,7 +355,7 @@
         ahead, back = to_column(ahead, forward), to_column(back, backward)
         later = [-step, step]
         *sums, left, right = gram(sums, pieces, offsets, tiles, later)
-        ahead, back, left, right, *sums = lax.optimization_barrier((ahead, back, left, right, *sums))
+        ahead, left, right, *sums = lax.optimization_barrier((ahead, left, right, *sums))
         pieces, offsets, tiles = [ahead, back], later, [left, right]
     cut = rows // columns // 2
     top, bottom = to_column(ahead[:cut], forward), to_column(back[cut:], backward)
@@ -347,9 +363,8 @@
     zeroth, first, second, third, mine, other = finish_gram(rows * shares, shared, sums, tile, top, bottom, middle)
 
     mine, third = mine + swap(other, 1), swap(third, 1)
-    away, second = first + third, swap(second, 1)
-    mine, away = lax.optimization_barrier((mine, away))
-    part, came = swap(mine, 2), swap(away, 2)
+    mine, away, second = lax.optimization_barrier((mine, first + third, second))
+    part, came, second = swap(mine, 2), swap(away, 2), swap(second, 1)
     mine, bit = mine + part, 4
     while bit < shares:
         mine = mine + swap(mine, bit)

time: 73.5 us -> 70 us (0.952)
  waiting for transfers between devices: 20.6 us -> 16.7 us
    ppermute x0 -> x6, starting transfers between devices: none -> 12.6 us  [on_device(): lax.ppermute(pieces[2 * i + k], ('rxn', 'col'), [(r * columns, r * column...]
    ppermute x17 -> x11, starting transfers between devices: 22.3 us -> 10.3 us  [to_column(): return lax.ppermute(value, 'col', pairs)]
    ppermute x17 -> x11, waiting for transfers between devices: 14.7 us -> 7.34 us  [to_column(): return lax.ppermute(value, 'col', pairs)]
    ppermute x0 -> x6, waiting for transfers between devices: none -> 4.27 us  [on_device(): lax.ppermute(pieces[2 * i + k], ('rxn', 'col'), [(r * columns, r * column...]
  transfers between devices with their start and end apart: 23 -> 23, of which waited for: 12 -> 12; matrix products, arithmetic and copies ran while one was open for 0% -> 0% of each run, Pallas kernels for 30% -> 31%
where the time goes in v3:
time: 70 us; the launch traced here: 69.6 us
  Pallas kernels  26.6 us (38%)
  starting transfers between devices  25.6 us (37%)
  waiting for transfers between devices  16.7 us (24%)
    ppermute x6, starting transfers between devices, on_device(): lax.ppermute(pieces[2 * i + k], ('rxn', 'col'), [(r * columns, r * column...  12.6 us
    pallas_call x4, Pallas kernels, add_gram(): pl.pallas_call(functools.partial(gram_kernel, offsets, later, float(total...  11.5 us
    ppermute x11, starting transfers between devices, to_column(): return lax.ppermute(value, 'col', pairs)  10.3 us
    pallas_call x1, Pallas kernels, invert(): pl.pallas_call(invert_kernel, out_shape=jax.ShapeDtypeStruct((PANEL, PANE...  9.36 us
    ppermute x11, waiting for transfers between devices, to_column(): return lax.ppermute(value, 'col', pairs)  7.34 us
    ppermute x6, waiting for transfers between devices, swap(): return lax.ppermute(value, ('rxn', 'col'), pairs)  5.13 us
    ppermute x6, waiting for transfers between devices, on_device(): lax.ppermute(pieces[2 * i + k], ('rxn', 'col'), [(r * columns, r * column...  4.27 us
    ppermute x6, starting transfers between devices, swap(): return lax.ppermute(value, ('rxn', 'col'), pairs)  2.73 us
  transfers between devices with their start and end apart: 23, of which 12 were waited for; matrix products, arithmetic and copies ran while one was open for 0% of the time, Pallas kernels for 31%

profile of v3, /device:TPU:0, one launch (start us, length us, event | category | flops | bytes accessed | tf_op | source)
XLA Modules:
  0.0 69.6 jit_solution(6876448345583230270)
XLA Ops:
  0.0 0.1 stack.31.place_ref
  0.1 2.1 %cut_panel.1 = (bf16[384,256]{1,0:T(8,128)(2,1)S(1)}, bf16[384,256]{1,0:T(8,128)(2,1)S(1)}, bf16[384,256]{1,0:T(8,128)(2,1)S(1)}, bf16[384,256]{1,0:T(8,128)(2,1...) custom-call(s32[7]{0:T(128)S(1)} %stack.31.place_ref, ...), custom_call_target="tpu_custom_call" | custom-call | tf_op jit(solution)/shard_map/cut_panel/pallas_call | solution.py:66
  2.2 0.0 copy-start
  2.2 0.0 copy-start.1
  2.2 3.5 %collective-permute-start.1 = (bf16[384,256]{1,0:T(8,128)(2,1)S(1)}, bf16[384,256]{1,0:T(8,128)(2,1)S(1)}, u32[]{:S(2)}, u32[]{:S(2)}) collective-permute-start(bf16[384,256]{1,0:T(8,128)(2,1)S(1)} %get-tuple-element.55), channel_id=1, source_target_pairs={{0,2},{8,9},{16,18},{24,25}} | collective-permute-start | bytes 589832 | tf_op jit(solution)/shard_map/ppermute | solution.py:336
  5.7 1.3 %collective-permute-start.2 = (bf16[384,256]{1,0:T(8,128)(2,1)S(1)}, bf16[384,256]{1,0:T(8,128)(2,1)S(1)}, u32[]{:S(2)}, u32[]{:S(2)}) collective-permute-start(bf16[384,256]{1,0:T(8,128)(2,1)S(1)} %get-tuple-element.56), channel_id=1, source_target_pairs={{0,1},{8,10},{16,17},{24,26}} | collective-permute-start | bytes 589832 | tf_op jit(solution)/shard_map/ppermute | solution.py:336
  7.0 1.3 %collective-permute-start.4 = (bf16[384,256]{1,0:T(8,128)(2,1)S(1)}, bf16[384,256]{1,0:T(8,128)(2,1)S(1)}, u32[]{:S(2)}, u32[]{:S(2)}) collective-permute-start(bf16[384,256]{1,0:T(8,128)(2,1)S(1)} %get-tuple-element.57), channel_id=1, source_target_pairs={{0,4},{8,9},{16,20},{24,25}} | collective-permute-start | bytes 589832 | tf_op jit(solution)/shard_map/ppermute | solution.py:336
  8.3 1.3 %collective-permute-start.5 = (bf16[384,256]{1,0:T(8,128)(2,1)S(1)}, bf16[384,256]{1,0:T(8,128)(2,1)S(1)}, u32[]{:S(2)}, u32[]{:S(2)}) collective-permute-start(bf16[384,256]{1,0:T(8,128)(2,1)S(1)} %get-tuple-element.58), channel_id=1, source_target_pairs={{0,1},{8,12},{16,17},{24,28}} | collective-permute-start | bytes 589832 | tf_op jit(solution)/shard_map/ppermute | solution.py:336
  9.6 1.7 %collective-permute-start = (bf16[384,256]{1,0:T(8,128)(2,1)S(1)}, bf16[384,256]{1,0:T(8,128)(2,1)S(1)}, u32[]{:S(2)}, u32[]{:S(2)}) collective-permute-start(bf16[384,256]{1,0:T(8,128)(2,1)S(1)} %get-tuple-element.54), channel_id=1, source_target_pairs={{0,7},{8,15},{16,23},{24,31}} | collective-permute-start | bytes 589832 | tf_op jit(solution)/shard_map/ppermute | solution.py:35
  11.4 0.0 collective-permute-done.1
  11.4 1.3 %collective-permute-start.7 = (bf16[384,256]{1,0:T(8,128)(2,1)S(1)}, bf16[384,256]{1,0:T(8,128)(2,1)S(1)}, u32[]{:S(2)}, u32[]{:S(2)}) collective-permute-start(bf16[384,256]{1,0:T(8,128)(2,1)S(1)} %get-tuple-element.59), channel_id=1, source_target_pairs={{0,6},{8,9},{16,22},{24,25}} | collective-permute-start | bytes 589832 | tf_op jit(solution)/shard_map/ppermute | solution.py:336
  12.7 0.0 collective-permute-done.2
  12.7 3.9 %collective-permute-start.8 = (bf16[384,256]{1,0:T(8,128)(2,1)S(1)}, bf16[384,256]{1,0:T(8,128)(2,1)S(1)}, u32[]{:S(2)}, u32[]{:S(2)}) collective-permute-start(bf16[384,256]{1,0:T(8,128)(2,1)S(1)} %get-tuple-element.60), channel_id=1, source_target_pairs={{0,1},{8,14},{16,17},{24,30}} | collective-permute-start | bytes 589832 | tf_op jit(solution)/shard_map/ppermute | solution.py:336
  16.6 0.1 add.67
  16.6 0.0 collective-permute-done.4
  16.7 0.7 collective-permute-start.3
  17.3 0.0 collective-permute-done.5
  17.3 0.1 add.70
  17.4 0.7 collective-permute-start.6
  18.1 1.2 %collective-permute-done = bf16[384,256]{1,0:T(8,128)(2,1)S(1)} collective-permute-done((bf16[384,256]{1,0:T(8,128)(2,1)S(1)}, bf16[384,256]{1,0:T(8,128)(2,1)S(1)}, u32[]{:S(2)}, u32[]{:S(2)}) %collective-permute-start) | collective-permute-done | bytes 196640 | tf_op jit(solution)/shard_map/ppermute | solution.py:35
  19.3 4.3 %collective-permute-done.7 = bf16[384,256]{1,0:T(8,128)(2,1)S(1)} collective-permute-done((bf16[384,256]{1,0:T(8,128)(2,1)S(1)}, bf16[384,256]{1,0:T(8,128)(2,1)S(1)}, u32[]{:S(2)}, u32[]{:S(2)}) %collective-permute-start.7) | collective-permute-done | bytes 196640 | tf_op jit(solution)/shard_map/ppermute | solution.py:336
  23.6 0.0 collective-permute-done.8
  23.6 0.0 collective-permute-done.3
  23.6 0.0 collective-permute-done.6
  23.6 0.1 add_add_fusion.refs_0_
  23.7 0.1 collective-permute-start.9
  23.7 2.0 %collective-permute-start.11 = (bf16[384,256]{1,0:T(8,128)(2,1)S(1)}, bf16[384,256]{1,0:T(8,128)(2,1)S(1)}, u32[]{:S(2)}, u32[]{:S(2)}) collective-permute-start(bf16[384,256]{1,0:T(8,128)(2,1)S(1)} %add_add_fusion.refs_0_), channel_id=1, source_target_pairs={{2,0},{4,2},{6,4},{7,6},{5,7},{3,5},{1,3},{0,1},{10,8},{12,10},{14... | collective-permute-start | bytes 589832 | tf_op jit(solution)/shard_map/ppermute | solution.py:35
  25.8 0.0 copy-done
  25.8 0.0 copy-done.1
  25.8 3.2 %gram.4 = (f32[4,256,512]{2,1,0:T(8,128)S(1)}, f32[256,256]{1,0:T(8,128)S(1)}, bf16[384,2048]{1,0:T(8,128)(2,1)S(1)}, bf16[384,2048]{1,0:T(8,128)(2,1)S(1)}) custom-call(s32[7]{0:T(128)S(1)} %stack.31.place_ref, f32[8,384]{1,0:T(8,128)S(1)} %reshape.6.lower_ref, f32[8,384]{1,0:T(8,128)S(1)} %reshape.7.upper_ref, bf16[3072,2048]{1,0:T(8,128)(2,1)} %basis_ref.9, ...), custom_call_target="tpu_custom_call" | custom-call | flops 402653184 | bytes 5767168 | tf_op jit(solution)/shard_map/gram/pallas_call | solution.py:209
  29.0 1.8 %collective-permute-done.9.refs_0_ = bf16[384,256]{1,0:T(8,128)(2,1)S(1)} collective-permute-done((bf16[384,256]{1,0:T(8,128)(2,1)S(1)}, bf16[384,256]{1,0:T(8,128)(2,1)S(1)}, u32[]{:S(2)}, u32[]{:S(2)}) %collective-permute-start.9) | collective-permute-done | bytes 196640 | tf_op jit(solution)/shard_map/ppermute | solution.py:35
  30.8 0.3 collective-permute-start.10
  31.1 0.0 collective-permute-done.11.refs_1_
  31.1 1.7 %collective-permute-start.13 = (bf16[384,256]{1,0:T(8,128)(2,1)S(1)}, bf16[384,256]{1,0:T(8,128)(2,1)S(1)}, u32[]{:S(2)}, u32[]{:S(2)}) collective-permute-start(bf16[384,256]{1,0:T(8,128)(2,1)S(1)} %collective-permute-done.11.refs_1_), channel_id=1, source_target_pairs={{2,0},{4,2},{6,4},{7,6},{5,7},{3,5},{1,3},{0,1},{10,8},{12,10},{14... | collective-permute-start | bytes 589832 | tf_op jit(solution)/shard_map/ppermute | solution.py:35
  32.9 2.8 %gram.5 = (f32[4,256,512]{2,1,0:T(8,128)S(1)}, f32[256,256]{1,0:T(8,128)S(1)}, bf16[384,2048]{1,0:T(8,128)(2,1)S(1)}, bf16[384,2048]{1,0:T(8,128)(2,1)S(1)}) custom-call(s32[7]{0:T(128)S(1)} %stack.31.place_ref, f32[8,384]{1,0:T(8,128)S(1)} %reshape.6.lower_ref, f32[8,384]{1,0:T(8,128)S(1)} %reshape.7.upper_ref, ...), custom_call_target="tpu_custom_call", output_to_operand_aliasing={{0}: (8, {}), {1}: (9, {})} | custom-call | flops 805306368 | bytes 7340032 | tf_op jit(solution)/shard_map/gram/pallas_call | solution.py:209
  35.6 1.5 %collective-permute-done.10.refs_0_ = bf16[384,256]{1,0:T(8,128)(2,1)S(1)} collective-permute-done((bf16[384,256]{1,0:T(8,128)(2,1)S(1)}, bf16[384,256]{1,0:T(8,128)(2,1)S(1)}, u32[]{:S(2)}, u32[]{:S(2)}) %collective-permute-start.10) | collective-permute-done | bytes 196640 | tf_op jit(solution)/shard_map/ppermute | solution.py:35
  37.1 0.6 collective-permute-start.12
  37.7 0.6 collective-permute-done.13.refs_1_
  38.3 0.8 %collective-permute-start.14 = (bf16[384,256]{1,0:T(8,128)(2,1)S(1)}, bf16[384,256]{1,0:T(8,128)(2,1)S(1)}, u32[]{:S(2)}, u32[]{:S(2)}) collective-permute-start(bf16[384,256]{1,0:T(8,128)(2,1)S(1)} %collective-permute-done.13.refs_1_), channel_id=1, source_target_pairs={{2,0},{4,2},{6,4},{7,6},{5,7},{3,5},{1,3},{0,1},{10,8},{12,10},{14... | collective-permute-start | bytes 589832 | tf_op jit(solution)/shard_map/ppermute | solution.py:35
  39.1 2.8 %gram.6 = (f32[4,256,512]{2,1,0:T(8,128)S(1)}, f32[256,256]{1,0:T(8,128)S(1)}, bf16[384,2048]{1,0:T(8,128)(2,1)S(1)}, bf16[384,2048]{1,0:T(8,128)(2,1)S(1)}) custom-call(s32[7]{0:T(128)S(1)} %stack.31.place_ref, f32[8,384]{1,0:T(8,128)S(1)} %reshape.6.lower_ref, f32[8,384]{1,0:T(8,128)S(1)} %reshape.7.upper_ref, ...), custom_call_target="tpu_custom_call", output_to_operand_aliasing={{0}: (8, {}), {1}: (9, {})} | custom-call | flops 805306368 | bytes 7340032 | tf_op jit(solution)/shard_map/gram/pallas_call | solution.py:209
  41.9 0.9 %collective-permute-done.12.refs_0_ = bf16[384,256]{1,0:T(8,128)(2,1)S(1)} collective-permute-done((bf16[384,256]{1,0:T(8,128)(2,1)S(1)}, bf16[384,256]{1,0:T(8,128)(2,1)S(1)}, u32[]{:S(2)}, u32[]{:S(2)}) %collective-permute-start.12) | collective-permute-done | bytes 196640 | tf_op jit(solution)/shard_map/ppermute | solution.py:35
  42.8 0.7 %collective-permute-start.15 = (bf16[192,256]{1,0:T(8,128)(2,1)S(1)}, bf16[192,256]{1,0:T(8,128)(2,1)S(1)}, u32[]{:S(2)}, u32[]{:S(2)}) collective-permute-start(bf16[192,256]{1,0:T(8,128)(2,1)S(1)} %slice.6), channel_id=1, source_target_pairs={{0,2},{2,4},{4,6},{6,7},{7,5},{5,3},{3,1},{1,0},{8,10},{10,12},{12... | collective-permute-start | bytes 294920 | tf_op jit(solution)/shard_map/ppermute | solution.py:35
  43.5 0.5 collective-permute-done.14.refs_1_
  44.0 1.0 %collective-permute-start.16 = (bf16[192,256]{1,0:T(8,128)(2,1)S(1)}, bf16[192,256]{1,0:T(8,128)(2,1)S(1)}, u32[]{:S(2)}, u32[]{:S(2)}) collective-permute-start(bf16[192,256]{1,0:T(8,128)(2,1)S(1)} %slice.8), channel_id=1, source_target_pairs={{2,0},{4,2},{6,4},{7,6},{5,7},{3,5},{1,3},{0,1},{10,8},{12,10},{14... | collective-permute-start | bytes 294920 | tf_op jit(solution)/shard_map/ppermute | solution.py:35
  44.9 2.8 %gram.7 = (f32[4,256,512]{2,1,0:T(8,128)S(1)}, f32[256,256]{1,0:T(8,128)S(1)}, bf16[384,2048]{1,0:T(8,128)(2,1)S(1)}) custom-call(s32[7]{0:T(128)S(1)} %stack.31.place_ref, f32[8,384]{1,0:T(8,128)S(1)} %reshape.6.lower_ref, f32[8,384]{1,0:T(8,128)S(1)} %reshape.7.upper_ref, ...), custom_call_target="tpu_custom_call", output_to_operand_aliasing={{0}: (8, {}), {1}: (9, {})} | custom-call | flops 805306368 | bytes 7340032 | tf_op jit(solution)/shard_map/gram/pallas_call | solution.py:209
  47.7 0.0 collective-permute-done.15.top_ref
  47.7 0.9 %collective-permute-done.16.bottom_ref = bf16[192,256]{1,0:T(8,128)(2,1)S(1)} collective-permute-done((bf16[192,256]{1,0:T(8,128)(2,1)S(1)}, bf16[192,256]{1,0:T(8,128)(2,1)S(1)}, u32[]{:S(2)}, u32[]{:S(2)}) %collective-permute-start.16) | collective-permute-done | bytes 98336 | tf_op jit(solution)/shard_map/ppermute | solution.py:35
  48.7 1.1 %last.1 = (f32[1,256,512]{2,1,0:T(8,128)S(1)}, f32[1,256,512]{2,1,0:T(8,128)S(1)}, f32[192,128]{1,0:T(8,128)S(1)}, f32[192,128]{1,0:T(8,128)S(1)}, bf16[256,384]{1,0:T(8,128)(2,1)S(1)}) custom-call(s32[7]{0:T(128)S(1)} %stack.31.place_ref, f32[8,384]{1,0:T(8,128)S(1)} %reshape.6.lower_ref, f32[8,384]{1,0:T(8,128)S(1)} %reshape.7.upper_ref, ...), custom_call_target="tpu_custom_call" | custom-call | flops 201326592 | bytes 2097152 | tf_op jit(solution)/shard_map/last/pallas_call | solution.py:269
  49.8 0.1 collective-permute-start.18
  49.9 0.5 collective-permute-start.17
  50.3 1.0 %rest.1 = (f32[1,256,512]{2,1,0:T(8,128)S(1)}, f32[1,256,512]{2,1,0:T(8,128)S(1)}) custom-call(s32[7]{0:T(128)S(1)} %stack.31.place_ref, bf16[256,384]{1,0:T(8,128)(2,1)S(1)} %get-tuple-element.95.weighted_ref, bf16[384,2048]{1,0:T(8,128)(2,1)S(1)} %get-tuple-element.88.tile_ref, f32[4,256,512]{2,1,0:T(8,128)S(1)} %get-tuple-element.89.refs_0_.gram_ref), custom_call_target="tpu_custom_call" | custom-call | flops 201326592 | bytes 2097152 | tf_op jit(solution)/shard_map/rest/pallas_call | solution.py:279
  51.3 0.6 collective-permute-done.17
  51.9 0.0 collective-permute-done.18
  51.9 0.1 add.76
  52.0 1.6 %collective-permute-start.19 = (f32[192,128]{1,0:T(8,128)S(1)}, f32[192,128]{1,0:T(8,128)S(1)}, u32[]{:S(2)}, u32[]{:S(2)}) collective-permute-start(f32[192,128]{1,0:T(8,128)S(1)} %add.75), channel_id=1, source_target_pairs={{0,16},{1,17},{2,18},{3,19},{4,20},{5,21},{6,22},{7,23},{8,24},{9,... | collective-permute-start | bytes 294920 | tf_op jit(solution)/shard_map/ppermute | solution.py:42
  53.6 0.0 collective-permute-start.21
  53.6 0.5 collective-permute-start.22
  54.1 3.0 %collective-permute-done.19 = f32[192,128]{1,0:T(8,128)S(1)} collective-permute-done((f32[192,128]{1,0:T(8,128)S(1)}, f32[192,128]{1,0:T(8,128)S(1)}, u32[]{:S(2)}, u32[]{:S(2)}) %collective-permute-start.19) | collective-permute-done | bytes 98336 | tf_op jit(solution)/shard_map/ppermute | solution.py:42
  57.1 0.1 collective-permute-start.20
  57.2 1.3 %collective-permute-done.20.other_ref = f32[192,128]{1,0:T(8,128)S(1)} collective-permute-done((f32[192,128]{1,0:T(8,128)S(1)}, f32[192,128]{1,0:T(8,128)S(1)}, u32[]{:S(2)}, u32[]{:S(2)}) %collective-permute-start.20) | collective-permute-done | bytes 98336 | tf_op jit(solution)/shard_map/ppermute | solution.py:42
  58.5 9.4 %invert.1.inverse_ref = f32[256,256]{1,0:T(8,128)S(1)} custom-call(s32[7]{0:T(128)S(1)} %stack.31.place_ref, f32[192,128]{1,0:T(8,128)S(1)} %add.77.mine_ref, f32[192,128]{1,0:T(8,128)S(1)} %collective-permute-done.20.other_ref), custom_call_target="tpu_custom_call" | custom-call | flops 4000000000 | bytes 524288 | tf_op jit(solution)/shard_map/invert/pallas_call | solution.py:134
  67.9 0.0 collective-permute-done.21.refs_1_
  67.9 0.3 collective-permute-done.22.refs_2_
  68.1 1.5 %transform.1 = f32[512,256]{1,0:T(8,128)} custom-call(f32[256,256]{1,0:T(8,128)S(1)} %invert.1.inverse_ref, f32[1,256,512]{2,1,0:T(8,128)S(1)} %get-tuple-element.98.refs_0_, f32[1,256,512]{2,1,0:T(8,128)S(1)} %collective-permute-done.21.refs_1_, f32[1,256,512]{2,1,0:T(8,128)S(1)} %collective-permute-done.22.refs_2_), custom_call_target="tpu_custom_call" | custom-call | flops 402653184 | bytes 1572864 | tf_op jit(solution)/shard_map/transform/pallas_call | solution.py:302
  (6 shorter events, 0.0 us)
Async XLA Ops:
  2.2 23.6 %copy-start = (f32[3072]{0:T(1024)S(1)}, f32[3072]{0:T(1024)}, u32[]{:S(2)}) copy-start(f32[3072]{0:T(1024)} %param.4) | copy-start | bytes 36868
  2.2 23.6 %copy-start.1 = (f32[3072]{0:T(1024)S(1)}, f32[3072]{0:T(1024)}, u32[]{:S(2)}) copy-start(f32[3072]{0:T(1024)} %param.5) | copy-start | bytes 36868
  2.2 9.2 %collective-permute-start.1 = (bf16[384,256]{1,0:T(8,128)(2,1)S(1)}, bf16[384,256]{1,0:T(8,128)(2,1)S(1)}, u32[]{:S(2)}, u32[]{:S(2)}) collective-permute-start(bf16[384,256]{1,0:T(8,128)(2,1)S(1)} %get-tuple-element.55), channel_id=1, source_target_pairs={{0,2},{8,9},{16,18},{24,25}} | collective-permute-start | bytes 589832 | tf_op jit(solution)/shard_map/ppermute | solution.py:336
  5.7 7.0 %collective-permute-start.2 = (bf16[384,256]{1,0:T(8,128)(2,1)S(1)}, bf16[384,256]{1,0:T(8,128)(2,1)S(1)}, u32[]{:S(2)}, u32[]{:S(2)}) collective-permute-start(bf16[384,256]{1,0:T(8,128)(2,1)S(1)} %get-tuple-element.56), channel_id=1, source_target_pairs={{0,1},{8,10},{16,17},{24,26}} | collective-permute-start | bytes 589832 | tf_op jit(solution)/shard_map/ppermute | solution.py:336
  7.0 9.6 %collective-permute-start.4 = (bf16[384,256]{1,0:T(8,128)(2,1)S(1)}, bf16[384,256]{1,0:T(8,128)(2,1)S(1)}, u32[]{:S(2)}, u32[]{:S(2)}) collective-permute-start(bf16[384,256]{1,0:T(8,128)(2,1)S(1)} %get-tuple-element.57), channel_id=1, source_target_pairs={{0,4},{8,9},{16,20},{24,25}} | collective-permute-start | bytes 589832 | tf_op jit(solution)/shard_map/ppermute | solution.py:336
  8.3 9.0 %collective-permute-start.5 = (bf16[384,256]{1,0:T(8,128)(2,1)S(1)}, bf16[384,256]{1,0:T(8,128)(2,1)S(1)}, u32[]{:S(2)}, u32[]{:S(2)}) collective-permute-start(bf16[384,256]{1,0:T(8,128)(2,1)S(1)} %get-tuple-element.58), channel_id=1, source_target_pairs={{0,1},{8,12},{16,17},{24,28}} | collective-permute-start | bytes 589832 | tf_op jit(solution)/shard_map/ppermute | solution.py:336
  9.6 9.7 %collective-permute-start = (bf16[384,256]{1,0:T(8,128)(2,1)S(1)}, bf16[384,256]{1,0:T(8,128)(2,1)S(1)}, u32[]{:S(2)}, u32[]{:S(2)}) collective-permute-start(bf16[384,256]{1,0:T(8,128)(2,1)S(1)} %get-tuple-element.54), channel_id=1, source_target_pairs={{0,7},{8,15},{16,23},{24,31}} | collective-permute-start | bytes 589832 | tf_op jit(solution)/shard_map/ppermute | solution.py:35
  11.4 12.2 %collective-permute-start.7 = (bf16[384,256]{1,0:T(8,128)(2,1)S(1)}, bf16[384,256]{1,0:T(8,128)(2,1)S(1)}, u32[]{:S(2)}, u32[]{:S(2)}) collective-permute-start(bf16[384,256]{1,0:T(8,128)(2,1)S(1)} %get-tuple-element.59), channel_id=1, source_target_pairs={{0,6},{8,9},{16,22},{24,25}} | collective-permute-start | bytes 589832 | tf_op jit(solution)/shard_map/ppermute | solution.py:336
  12.7 10.9 %collective-permute-start.8 = (bf16[384,256]{1,0:T(8,128)(2,1)S(1)}, bf16[384,256]{1,0:T(8,128)(2,1)S(1)}, u32[]{:S(2)}, u32[]{:S(2)}) collective-permute-start(bf16[384,256]{1,0:T(8,128)(2,1)S(1)} %get-tuple-element.60), channel_id=1, source_target_pairs={{0,1},{8,14},{16,17},{24,30}} | collective-permute-start | bytes 589832 | tf_op jit(solution)/shard_map/ppermute | solution.py:336
  16.7 6.9 %collective-permute-start.3 = (bf16[384,256]{1,0:T(8,128)(2,1)S(1)}, bf16[384,256]{1,0:T(8,128)(2,1)S(1)}, u32[]{:S(2)}, u32[]{:S(2)}) collective-permute-start(bf16[384,256]{1,0:T(8,128)(2,1)S(1)} %add.67), channel_id=1, source_target_pairs={{1,5},{9,13},{17,21},{25,29}} | collective-permute-start | bytes 589832 | tf_op jit(solution)/shard_map/ppermute | solution.py:35
  17.4 6.2 %collective-permute-start.6 = (bf16[384,256]{1,0:T(8,128)(2,1)S(1)}, bf16[384,256]{1,0:T(8,128)(2,1)S(1)}, u32[]{:S(2)}, u32[]{:S(2)}) collective-permute-start(bf16[384,256]{1,0:T(8,128)(2,1)S(1)} %add.70), channel_id=1, source_target_pairs={{1,3},{9,11},{17,19},{25,27}} | collective-permute-start | bytes 589832 | tf_op jit(solution)/shard_map/ppermute | solution.py:35
  23.7 7.1 %collective-permute-start.9 = (bf16[384,256]{1,0:T(8,128)(2,1)S(1)}, bf16[384,256]{1,0:T(8,128)(2,1)S(1)}, u32[]{:S(2)}, u32[]{:S(2)}) collective-permute-start(bf16[384,256]{1,0:T(8,128)(2,1)S(1)} %add_add_fusion.refs_0_), channel_id=1, source_target_pairs={{0,2},{2,4},{4,6},{6,7},{7,5},{5,3},{3,1},{1,0},{8,10},{10,12},{12... | collective-permute-start | bytes 589832 | tf_op jit(solution)/shard_map/ppermute | solution.py:35
  23.7 7.4 %collective-permute-start.11 = (bf16[384,256]{1,0:T(8,128)(2,1)S(1)}, bf16[384,256]{1,0:T(8,128)(2,1)S(1)}, u32[]{:S(2)}, u32[]{:S(2)}) collective-permute-start(bf16[384,256]{1,0:T(8,128)(2,1)S(1)} %add_add_fusion.refs_0_), channel_id=1, source_target_pairs={{2,0},{4,2},{6,4},{7,6},{5,7},{3,5},{1,3},{0,1},{10,8},{12,10},{14... | collective-permute-start | bytes 589832 | tf_op jit(solution)/shard_map/ppermute | solution.py:35
  30.8 6.3 %collective-permute-start.10 = (bf16[384,256]{1,0:T(8,128)(2,1)S(1)}, bf16[384,256]{1,0:T(8,128)(2,1)S(1)}, u32[]{:S(2)}, u32[]{:S(2)}) collective-permute-start(bf16[384,256]{1,0:T(8,128)(2,1)S(1)} %collective-permute-done.9.refs_0_), channel_id=1, source_target_pairs={{0,2},{2,4},{4,6},{6,7},{7,5},{5,3},{3,1},{1,0},{8,10},{10,12},{12... | collective-permute-start | bytes 589832 | tf_op jit(solution)/shard_map/ppermute | solution.py:35
  31.1 7.2 %collective-permute-start.13 = (bf16[384,256]{1,0:T(8,128)(2,1)S(1)}, bf16[384,256]{1,0:T(8,128)(2,1)S(1)}, u32[]{:S(2)}, u32[]{:S(2)}) collective-permute-start(bf16[384,256]{1,0:T(8,128)(2,1)S(1)} %collective-permute-done.11.refs_1_), channel_id=1, source_target_pairs={{2,0},{4,2},{6,4},{7,6},{5,7},{3,5},{1,3},{0,1},{10,8},{12,10},{14... | collective-permute-start | bytes 589832 | tf_op jit(solution)/shard_map/ppermute | solution.py:35
  37.1 5.7 %collective-permute-start.12 = (bf16[384,256]{1,0:T(8,128)(2,1)S(1)}, bf16[384,256]{1,0:T(8,128)(2,1)S(1)}, u32[]{:S(2)}, u32[]{:S(2)}) collective-permute-start(bf16[384,256]{1,0:T(8,128)(2,1)S(1)} %collective-permute-done.10.refs_0_), channel_id=1, source_target_pairs={{0,2},{2,4},{4,6},{6,7},{7,5},{5,3},{3,1},{1,0},{8,10},{10,12},{12... | collective-permute-start | bytes 589832 | tf_op jit(solution)/shard_map/ppermute | solution.py:35
  38.3 5.7 %collective-permute-start.14 = (bf16[384,256]{1,0:T(8,128)(2,1)S(1)}, bf16[384,256]{1,0:T(8,128)(2,1)S(1)}, u32[]{:S(2)}, u32[]{:S(2)}) collective-permute-start(bf16[384,256]{1,0:T(8,128)(2,1)S(1)} %collective-permute-done.13.refs_1_), channel_id=1, source_target_pairs={{2,0},{4,2},{6,4},{7,6},{5,7},{3,5},{1,3},{0,1},{10,8},{12,10},{14... | collective-permute-start | bytes 589832 | tf_op jit(solution)/shard_map/ppermute | solution.py:35
  42.8 4.9 %collective-permute-start.15 = (bf16[192,256]{1,0:T(8,128)(2,1)S(1)}, bf16[192,256]{1,0:T(8,128)(2,1)S(1)}, u32[]{:S(2)}, u32[]{:S(2)}) collective-permute-start(bf16[192,256]{1,0:T(8,128)(2,1)S(1)} %slice.6), channel_id=1, source_target_pairs={{0,2},{2,4},{4,6},{6,7},{7,5},{5,3},{3,1},{1,0},{8,10},{10,12},{12... | collective-permute-start | bytes 294920 | tf_op jit(solution)/shard_map/ppermute | solution.py:35
  44.0 4.7 %collective-permute-start.16 = (bf16[192,256]{1,0:T(8,128)(2,1)S(1)}, bf16[192,256]{1,0:T(8,128)(2,1)S(1)}, u32[]{:S(2)}, u32[]{:S(2)}) collective-permute-start(bf16[192,256]{1,0:T(8,128)(2,1)S(1)} %slice.8), channel_id=1, source_target_pairs={{2,0},{4,2},{6,4},{7,6},{5,7},{3,5},{1,3},{0,1},{10,8},{12,10},{14... | collective-permute-start | bytes 294920 | tf_op jit(solution)/shard_map/ppermute | solution.py:35
  49.8 2.1 %collective-permute-start.18 = (f32[1,256,512]{2,1,0:T(8,128)S(1)}, f32[1,256,512]{2,1,0:T(8,128)S(1)}, u32[]{:S(2)}, u32[]{:S(2)}) collective-permute-start(f32[1,256,512]{2,1,0:T(8,128)S(1)} %get-tuple-element.94), channel_id=1, source_target_pairs={{0,8},{1,9},{2,10},{3,11},{4,12},{5,13},{6,14},{7,15},{8,0},{9,1},... | collective-permute-start | bytes 1572872 | tf_op jit(solution)/shard_map/ppermute | solution.py:42
  49.9 2.0 %collective-permute-start.17 = (f32[192,128]{1,0:T(8,128)S(1)}, f32[192,128]{1,0:T(8,128)S(1)}, u32[]{:S(2)}, u32[]{:S(2)}) collective-permute-start(f32[192,128]{1,0:T(8,128)S(1)} %get-tuple-element.92), channel_id=1, source_target_pairs={{0,8},{1,9},{2,10},{3,11},{4,12},{5,13},{6,14},{7,15},{8,0},{9,1},... | collective-permute-start | bytes 294920 | tf_op jit(solution)/shard_map/ppermute | solution.py:42
  52.0 5.1 %collective-permute-start.19 = (f32[192,128]{1,0:T(8,128)S(1)}, f32[192,128]{1,0:T(8,128)S(1)}, u32[]{:S(2)}, u32[]{:S(2)}) collective-permute-start(f32[192,128]{1,0:T(8,128)S(1)} %add.75), channel_id=1, source_target_pairs={{0,16},{1,17},{2,18},{3,19},{4,20},{5,21},{6,22},{7,23},{8,24},{9,... | collective-permute-start | bytes 294920 | tf_op jit(solution)/shard_map/ppermute | solution.py:42
  53.6 14.3 %collective-permute-start.21 = (f32[1,256,512]{2,1,0:T(8,128)S(1)}, f32[1,256,512]{2,1,0:T(8,128)S(1)}, u32[]{:S(2)}, u32[]{:S(2)}) collective-permute-start(f32[1,256,512]{2,1,0:T(8,128)S(1)} %get-tuple-element.99), channel_id=1, source_target_pairs={{0,8},{1,9},{2,10},{3,11},{4,12},{5,13},{6,14},{7,15},{8,0},{9,1},... | collective-permute-start | bytes 1572872 | tf_op jit(solution)/shard_map/ppermute | solution.py:42
  53.6 14.5 %collective-permute-start.22 = (f32[1,256,512]{2,1,0:T(8,128)S(1)}, f32[1,256,512]{2,1,0:T(8,128)S(1)}, u32[]{:S(2)}, u32[]{:S(2)}) collective-permute-start(f32[1,256,512]{2,1,0:T(8,128)S(1)} %add.76), channel_id=1, source_target_pairs={{0,16},{1,17},{2,18},{3,19},{4,20},{5,21},{6,22},{7,23},{8,24},{9,... | collective-permute-start | bytes 1572872 | tf_op jit(solution)/shard_map/ppermute | solution.py:42
  57.1 1.4 %collective-permute-start.20 = (f32[192,128]{1,0:T(8,128)S(1)}, f32[192,128]{1,0:T(8,128)S(1)}, u32[]{:S(2)}, u32[]{:S(2)}) collective-permute-start(f32[192,128]{1,0:T(8,128)S(1)} %add.77.mine_ref), channel_id=1, source_target_pairs={{0,8},{1,9},{2,10},{3,11},{4,12},{5,13},{6,14},{7,15},{8,0},{9,1},... | collective-permute-start | bytes 294920 | tf_op jit(solution)/shard_map/ppermute | solution.py:42

commit v4 on v3

--- a/solution.py
+++ b/solution.py
@@ -11,7 +11,7 @@
 HALF = PANEL // 2
 LANES = 128
 BLOCK = 64
-STRIP = 8
+STRIP = 16
 COLUMN, CORE, AT, BLOCKS = 0, 1, 2, 3
 SMEM, VMEM, HBM = (pl.BlockSpec(memory_space=space) for space in (pltpu.SMEM, pltpu.VMEM, pltpu.HBM))
 HIGHEST = lax.Precision.HIGHEST
@@ -138,7 +138,7 @@
         out_specs=VMEM,
         scratch_shapes=[pltpu.VMEM((PANEL, 2 * PANEL), F32), pltpu.VMEM((3 * HALF, HALF), F32)],
         compiler_params=PARAMS,
-        cost_estimate=pl.CostEstimate(flops=4*10**9, bytes_accessed=2**19, transcendentals=0),
+        cost_estimate=pl.CostEstimate(flops=10*10**8, bytes_accessed=2**19, transcendentals=0),
         name="invert",
     )(place, mine, other)
 
@@ -230,7 +230,7 @@
 
 
 def last_kernel(offset, total, place_ref, lower_ref, upper_ref, tile_ref, top_ref, bottom_ref, *refs):
-    gram_ref, diagonal_ref, sent_ref, away_ref, mine_ref, other_ref, weighted_ref, sum_ref = refs
+    gram_ref, diagonal_ref, *outs, mine_ref, other_ref, weighted_ref, sum_ref = refs
     piece = jnp.concatenate([top_ref[...], bottom_ref[...]], 0)
     at = piece_at(place_ref, offset, lower_ref.shape[0])
     weighted_ref[...] = weigh(total, at, lower_ref, upper_ref, piece)
@@ -241,21 +241,22 @@
     core, part = place_ref[CORE], mine_ref.shape[0]
     mine_ref[...] = sum_ref[pl.ds(pl.multiple_of(core * part, part), part), :]
     other_ref[...] = sum_ref[pl.ds(pl.multiple_of((1 - core) * part, part), part), :]
-    add_blocks(place_ref, gram_ref, weighted_ref, tile_ref, [(3, sent_ref), (1, away_ref)])
+    add_blocks(place_ref, gram_ref, weighted_ref, tile_ref, [(3, outs[:2]), (1, outs[2:])])
 
 
 def add_blocks(place_ref, gram_ref, weighted_ref, tile_ref, quarters):
-    for number, out_ref in quarters:
-        count, _, share = out_ref.shape
+    for number, outs in quarters:
+        count, height, share = outs[0].shape
         for j in range(count):
             block = number * count + j
             lanes = block_lanes(place_ref, block, share)
-            term = jnp.dot(weighted_ref[...], tile_ref[:, lanes], preferred_element_type=F32)
-            out_ref[j] = gram_ref[block] + term
+            gram = gram_ref[block] + jnp.dot(weighted_ref[...], tile_ref[:, lanes], preferred_element_type=F32)
+            for i, out_ref in enumerate(outs):
+                out_ref[j] = gram[i * height : (i + 1) * height]
 
 
 def rest_kernel(place_ref, weighted_ref, tile_ref, gram_ref, sent_ref, kept_ref):
-    add_blocks(place_ref, gram_ref, weighted_ref, tile_ref, [(2, sent_ref), (0, kept_ref)])
+    add_blocks(place_ref, gram_ref, weighted_ref, tile_ref, [(2, [sent_ref]), (0, [kept_ref])])
 
 
 def finish_gram(total, shared, sums, tile, top, bottom, offset):
@@ -264,13 +265,14 @@
     shares, _, share = gram.shape
     depth = tile.shape[0]
     quarter = jax.ShapeDtypeStruct((shares // 4, PANEL, share), F32)
+    eighth = jax.ShapeDtypeStruct((shares // 4, HALF, share), F32)
     half = jax.ShapeDtypeStruct((3 * HALF // 2, HALF), F32)
     cost = pl.CostEstimate(flops=depth * PANEL * share * shares, bytes_accessed=2**21, transcendentals=0)
-    third, first, mine, other, weighted = pl.pallas_call(
+    *thirds, first, other_first, mine, other, weighted = pl.pallas_call(
         functools.partial(last_kernel, offset, float(total)),
-        out_shape=[quarter, quarter, half, half, jax.ShapeDtypeStruct((PANEL, depth), jnp.bfloat16)],
+        out_shape=[eighth] * 4 + [half, half, jax.ShapeDtypeStruct((PANEL, depth), jnp.bfloat16)],
         in_specs=[SMEM] + [VMEM] * 7,
-        out_specs=[VMEM] * 5,
+        out_specs=[VMEM] * 7,
         scratch_shapes=[pltpu.VMEM((3 * HALF, HALF), F32)],
         compiler_params=PARAMS,
         cost_estimate=cost,
@@ -285,28 +287,38 @@
         cost_estimate=cost,
         name="rest",
     )(place, weighted, tile, gram)
-    return zeroth, first, second, third, mine, other
-
-
-def transform_kernel(inverse_ref, *refs):
-    gram = refs[0][0]
-    for ref in refs[1:-1]:
-        gram = gram + ref[0]
-    refs[-1][...] = lax.dot_general(
-        gram.T, inverse_ref[...], (((1,), (1,)), ((), ())), precision=HIGHEST, preferred_element_type=F32
+    return zeroth, (first, other_first), second, thirds, mine, other
+
+
+def transform_kernel(part, inverse_ref, *refs):
+    *terms, out_ref = refs
+    rows = slice(part * HALF, (part + 1) * HALF)
+    grams = [ref[0, rows, :] if ref.shape[1] == PANEL else ref[0] for ref in terms[part:]]
+    gram = functools.reduce(lambda a, b: a + b, grams).T
+    product = lax.dot_general(
+        gram,
+        inverse_ref[part * HALF :, rows],
+        (((1,), (1,)), ((), ())),
+        precision=HIGHEST,
+        preferred_element_type=F32,
     )
-
-
-def transform(inverse, terms):
-    share = terms[0].shape[2]
+    if part:
+        out_ref[:, :HALF] = terms[0][:, :HALF]
+        out_ref[:, HALF:] = terms[0][:, HALF:] + product
+    else:
+        out_ref[...] = product
+
+
+def transform(part, inverse, terms):
+    share = terms[-1].shape[2]
     return pl.pallas_call(
-        transform_kernel,
+        functools.partial(transform_kernel, part),
         out_shape=jax.ShapeDtypeStruct((share, PANEL), F32),
         in_specs=[VMEM] * (1 + len(terms)),
         out_specs=VMEM,
         compiler_params=PARAMS,
         cost_estimate=pl.CostEstimate(
-            flops=12 * share * PANEL * PANEL, bytes_accessed=12 * share * PANEL, transcendentals=0
+            flops=6 * share * PANEL * PANEL, bytes_accessed=8 * share * PANEL, transcendentals=0
         ),
         name="transform",
     )(inverse, *terms)
@@ -355,29 +367,33 @@
         ahead, back = to_column(ahead, forward), to_column(back, backward)
         later = [-step, step]
         *sums, left, right = gram(sums, pieces, offsets, tiles, later)
-        ahead, left, right, *sums = lax.optimization_barrier((ahead, left, right, *sums))
+        back, left, right, *sums = lax.optimization_barrier((back, left, right, *sums))
         pieces, offsets, tiles = [ahead, back], later, [left, right]
     cut = rows // columns // 2
     top, bottom = to_column(ahead[:cut], forward), to_column(back[cut:], backward)
     *sums, tile = gram(sums, pieces, offsets, tiles, [middle])
-    zeroth, first, second, third, mine, other = finish_gram(rows * shares, shared, sums, tile, top, bottom, middle)
-
-    mine, third = mine + swap(other, 1), swap(third, 1)
-    mine, away, second = lax.optimization_barrier((mine, first + third, second))
-    part, came, second = swap(mine, 2), swap(away, 2), swap(second, 1)
+    zeroth, first, second, thirds, mine, other = finish_gram(rows * shares, shared, sums, tile, top, bottom, middle)
+
+    mine = mine + swap(other, 1)
+    away = [x + swap(y, 1) for x, y in zip(first, thirds)]
+    mine, second = lax.optimization_barrier((mine, second))
+    part, came, second = swap(mine, 2), [swap(x, 2) for x in away], swap(second, 1)
     mine, bit = mine + part, 4
     while bit < shares:
         mine = mine + swap(mine, bit)
         bit *= 2
-    other = swap(mine, 1)
-    inverse = invert(place, mine, other)
-    terms, bit = [zeroth, second, came], 4
-    while bit < shares:
-        mine = functools.reduce(lambda a, b: a + b, terms)
-        middle = mine.shape[0] // 2
-        terms = [mine[:middle], swap(mine[middle:], bit)]
-        bit *= 2
-    return transform(inverse, terms)
+    inverse = invert(place, mine, swap(mine, 1))
+    out = []
+    for i in range(2):
+        terms, bit = [zeroth, second, came[i]], 4
+        while bit < shares:
+            lane = slice(i * HALF, (i + 1) * HALF)
+            mine = sum(x[:, lane] if x.shape[1] == PANEL else x for x in terms)
+            half = mine.shape[0] // 2
+            terms = [mine[:half], swap(mine[half:], bit)]
+            bit *= 2
+        out = transform(i, inverse, [out, *terms] if i else terms)
+    return out
 
 
 def solution(mesh):

time: 70 us -> 69 us (0.986)
  waiting for transfers between devices: 16.7 us -> 13.4 us
  starting transfers between devices: 25.6 us -> 28.7 us
  Pallas kernels: 26.6 us -> 25.8 us
    ppermute x6 -> x8, starting transfers between devices: 2.73 us -> 4.92 us  [swap(): return lax.ppermute(value, ('rxn', 'col'), pairs)]
    ppermute x6 -> x8, waiting for transfers between devices: 5.13 us -> 3.29 us  [swap(): return lax.ppermute(value, ('rxn', 'col'), pairs)]
    ppermute x11, waiting for transfers between devices: 7.34 us -> 5.9 us  [to_column(): return lax.ppermute(value, 'col', pairs)]
    pallas_call x1, Pallas kernels: 9.36 us -> 8.17 us  [invert(): pl.pallas_call(invert_kernel, out_shape=jax.ShapeDtypeStruct((PANEL, PANE...]
    ppermute x11, starting transfers between devices: 10.3 us -> 11.3 us  [to_column(): return lax.ppermute(value, 'col', pairs)]
    pallas_call x1 -> x2, Pallas kernels: 1.51 us -> 1.84 us  [transform(): pl.pallas_call(functools.partial(transform_kernel, part), out_shape=jax.S...]
  transfers between devices with their start and end apart: 23 -> 25, of which waited for: 12 -> 9; matrix products, arithmetic and copies ran while one was open for 0% -> 0% of each run, Pallas kernels for 31% -> 31%
where the time goes in v4:
time: 69 us; the launch traced here: 68.6 us
  starting transfers between devices  28.7 us (42%)
  Pallas kernels  25.8 us (37%)
  waiting for transfers between devices  13.4 us (19%)
    ppermute x6, starting transfers between devices, on_device(): lax.ppermute(pieces[2 * i + k], ('rxn', 'col'), [(r * columns, r * column...  12.6 us
    pallas_call x4, Pallas kernels, add_gram(): pl.pallas_call(functools.partial(gram_kernel, offsets, later, float(total...  11.5 us
    ppermute x11, starting transfers between devices, to_column(): return lax.ppermute(value, 'col', pairs)  11.3 us
    pallas_call x1, Pallas kernels, invert(): pl.pallas_call(invert_kernel, out_shape=jax.ShapeDtypeStruct((PANEL, PANE...  8.17 us
    ppermute x11, waiting for transfers between devices, to_column(): return lax.ppermute(value, 'col', pairs)  5.9 us
    ppermute x8, starting transfers between devices, swap(): return lax.ppermute(value, ('rxn', 'col'), pairs)  4.92 us
    ppermute x6, waiting for transfers between devices, on_device(): lax.ppermute(pieces[2 * i + k], ('rxn', 'col'), [(r * columns, r * column...  4.23 us
    ppermute x8, waiting for transfers between devices, swap(): return lax.ppermute(value, ('rxn', 'col'), pairs)  3.29 us
  transfers between devices with their start and end apart: 25, of which 9 were waited for; matrix products, arithmetic and copies ran while one was open for 0% of the time, Pallas kernels for 31%

profile of v4, /device:TPU:0, one launch (start us, length us, event | category | flops | bytes accessed | tf_op | source)
XLA Modules:
  0.0 68.6 jit_solution(10960937111969602485)
XLA Ops:
  0.0 0.1 stack.31.place_ref
  0.1 2.1 %cut_panel.1 = (bf16[384,256]{1,0:T(8,128)(2,1)S(1)}, bf16[384,256]{1,0:T(8,128)(2,1)S(1)}, bf16[384,256]{1,0:T(8,128)(2,1)S(1)}, bf16[384,256]{1,0:T(8,128)(2,1...) custom-call(s32[7]{0:T(128)S(1)} %stack.31.place_ref, ...), custom_call_target="tpu_custom_call" | custom-call | tf_op jit(solution)/shard_map/cut_panel/pallas_call | solution.py:66
  2.2 0.0 copy-start
  2.2 0.0 copy-start.1
  2.2 3.5 %collective-permute-start.1 = (bf16[384,256]{1,0:T(8,128)(2,1)S(1)}, bf16[384,256]{1,0:T(8,128)(2,1)S(1)}, u32[]{:S(2)}, u32[]{:S(2)}) collective-permute-start(bf16[384,256]{1,0:T(8,128)(2,1)S(1)} %get-tuple-element.56), channel_id=1, source_target_pairs={{0,2},{8,9},{16,18},{24,25}} | collective-permute-start | bytes 589832 | tf_op jit(solution)/shard_map/ppermute | solution.py:348
  5.7 1.3 %collective-permute-start.2 = (bf16[384,256]{1,0:T(8,128)(2,1)S(1)}, bf16[384,256]{1,0:T(8,128)(2,1)S(1)}, u32[]{:S(2)}, u32[]{:S(2)}) collective-permute-start(bf16[384,256]{1,0:T(8,128)(2,1)S(1)} %get-tuple-element.57), channel_id=1, source_target_pairs={{0,1},{8,10},{16,17},{24,26}} | collective-permute-start | bytes 589832 | tf_op jit(solution)/shard_map/ppermute | solution.py:348
  7.0 1.3 %collective-permute-start.4 = (bf16[384,256]{1,0:T(8,128)(2,1)S(1)}, bf16[384,256]{1,0:T(8,128)(2,1)S(1)}, u32[]{:S(2)}, u32[]{:S(2)}) collective-permute-start(bf16[384,256]{1,0:T(8,128)(2,1)S(1)} %get-tuple-element.58), channel_id=1, source_target_pairs={{0,4},{8,9},{16,20},{24,25}} | collective-permute-start | bytes 589832 | tf_op jit(solution)/shard_map/ppermute | solution.py:348
  8.3 1.3 %collective-permute-start.5 = (bf16[384,256]{1,0:T(8,128)(2,1)S(1)}, bf16[384,256]{1,0:T(8,128)(2,1)S(1)}, u32[]{:S(2)}, u32[]{:S(2)}) collective-permute-start(bf16[384,256]{1,0:T(8,128)(2,1)S(1)} %get-tuple-element.59), channel_id=1, source_target_pairs={{0,1},{8,12},{16,17},{24,28}} | collective-permute-start | bytes 589832 | tf_op jit(solution)/shard_map/ppermute | solution.py:348
  9.6 1.7 %collective-permute-start = (bf16[384,256]{1,0:T(8,128)(2,1)S(1)}, bf16[384,256]{1,0:T(8,128)(2,1)S(1)}, u32[]{:S(2)}, u32[]{:S(2)}) collective-permute-start(bf16[384,256]{1,0:T(8,128)(2,1)S(1)} %get-tuple-element.55), channel_id=1, source_target_pairs={{0,7},{8,15},{16,23},{24,31}} | collective-permute-start | bytes 589832 | tf_op jit(solution)/shard_map/ppermute | solution.py:35
  11.4 0.0 collective-permute-done.1
  11.4 1.3 %collective-permute-start.7 = (bf16[384,256]{1,0:T(8,128)(2,1)S(1)}, bf16[384,256]{1,0:T(8,128)(2,1)S(1)}, u32[]{:S(2)}, u32[]{:S(2)}) collective-permute-start(bf16[384,256]{1,0:T(8,128)(2,1)S(1)} %get-tuple-element.60), channel_id=1, source_target_pairs={{0,6},{8,9},{16,22},{24,25}} | collective-permute-start | bytes 589832 | tf_op jit(solution)/shard_map/ppermute | solution.py:348
  12.7 0.0 collective-permute-done.2
  12.7 3.9 %collective-permute-start.8 = (bf16[384,256]{1,0:T(8,128)(2,1)S(1)}, bf16[384,256]{1,0:T(8,128)(2,1)S(1)}, u32[]{:S(2)}, u32[]{:S(2)}) collective-permute-start(bf16[384,256]{1,0:T(8,128)(2,1)S(1)} %get-tuple-element.61), channel_id=1, source_target_pairs={{0,1},{8,14},{16,17},{24,30}} | collective-permute-start | bytes 589832 | tf_op jit(solution)/shard_map/ppermute | solution.py:348
  16.6 0.1 add.70
  16.6 0.0 collective-permute-done.4
  16.7 0.7 collective-permute-start.3
  17.3 0.0 collective-permute-done.5
  17.3 0.1 add.73
  17.4 0.7 collective-permute-start.6
  18.1 1.2 %collective-permute-done = bf16[384,256]{1,0:T(8,128)(2,1)S(1)} collective-permute-done((bf16[384,256]{1,0:T(8,128)(2,1)S(1)}, bf16[384,256]{1,0:T(8,128)(2,1)S(1)}, u32[]{:S(2)}, u32[]{:S(2)}) %collective-permute-start) | collective-permute-done | bytes 196640 | tf_op jit(solution)/shard_map/ppermute | solution.py:35
  19.3 4.2 %collective-permute-done.7 = bf16[384,256]{1,0:T(8,128)(2,1)S(1)} collective-permute-done((bf16[384,256]{1,0:T(8,128)(2,1)S(1)}, bf16[384,256]{1,0:T(8,128)(2,1)S(1)}, u32[]{:S(2)}, u32[]{:S(2)}) %collective-permute-start.7) | collective-permute-done | bytes 196640 | tf_op jit(solution)/shard_map/ppermute | solution.py:348
  23.5 0.0 collective-permute-done.8
  23.5 0.0 collective-permute-done.3
  23.5 0.0 collective-permute-done.6
  23.5 0.1 add_add_fusion.refs_0_
  23.6 1.6 %collective-permute-start.12 = (bf16[384,256]{1,0:T(8,128)(2,1)S(1)}, bf16[384,256]{1,0:T(8,128)(2,1)S(1)}, u32[]{:S(2)}, u32[]{:S(2)}) collective-permute-start(bf16[384,256]{1,0:T(8,128)(2,1)S(1)} %add_add_fusion.refs_0_), channel_id=1, source_target_pairs={{2,0},{4,2},{6,4},{7,6},{5,7},{3,5},{1,3},{0,1},{10,8},{12,10},{14... | collective-permute-start | bytes 589832 | tf_op jit(solution)/shard_map/ppermute | solution.py:35
  25.2 0.5 collective-permute-start.9
  25.7 3.2 %gram.4 = (f32[4,256,512]{2,1,0:T(8,128)S(1)}, f32[256,256]{1,0:T(8,128)S(1)}, bf16[384,2048]{1,0:T(8,128)(2,1)S(1)}, bf16[384,2048]{1,0:T(8,128)(2,1)S(1)}) custom-call(s32[7]{0:T(128)S(1)} %stack.31.place_ref, f32[8,384]{1,0:T(8,128)S(1)} %reshape.6.lower_ref, f32[8,384]{1,0:T(8,128)S(1)} %reshape.7.upper_ref, bf16[3072,2048]{1,0:T(8,128)(2,1)} %basis_ref.9, ...), custom_call_target="tpu_custom_call" | custom-call | flops 402653184 | bytes 5767168 | tf_op jit(solution)/shard_map/gram/pallas_call | solution.py:209
  29.0 1.8 %collective-permute-done.12.refs_1_ = bf16[384,256]{1,0:T(8,128)(2,1)S(1)} collective-permute-done((bf16[384,256]{1,0:T(8,128)(2,1)S(1)}, bf16[384,256]{1,0:T(8,128)(2,1)S(1)}, u32[]{:S(2)}, u32[]{:S(2)}) %collective-permute-start.12) | collective-permute-done | bytes 196640 | tf_op jit(solution)/shard_map/ppermute | solution.py:35
  30.8 0.3 collective-permute-start.13
  31.1 0.3 collective-permute-done.9.refs_0_
  31.3 1.5 %collective-permute-start.10 = (bf16[384,256]{1,0:T(8,128)(2,1)S(1)}, bf16[384,256]{1,0:T(8,128)(2,1)S(1)}, u32[]{:S(2)}, u32[]{:S(2)}) collective-permute-start(bf16[384,256]{1,0:T(8,128)(2,1)S(1)} %collective-permute-done.9.refs_0_), channel_id=1, source_target_pairs={{0,2},{2,4},{4,6},{6,7},{7,5},{5,3},{3,1},{1,0},{8,10},{10,12},{12... | collective-permute-start | bytes 589832 | tf_op jit(solution)/shard_map/ppermute | solution.py:35
  32.8 2.8 %gram.5 = (f32[4,256,512]{2,1,0:T(8,128)S(1)}, f32[256,256]{1,0:T(8,128)S(1)}, bf16[384,2048]{1,0:T(8,128)(2,1)S(1)}, bf16[384,2048]{1,0:T(8,128)(2,1)S(1)}) custom-call(s32[7]{0:T(128)S(1)} %stack.31.place_ref, f32[8,384]{1,0:T(8,128)S(1)} %reshape.6.lower_ref, f32[8,384]{1,0:T(8,128)S(1)} %reshape.7.upper_ref, ...), custom_call_target="tpu_custom_call", output_to_operand_aliasing={{0}: (8, {}), {1}: (9, {})} | custom-call | flops 805306368 | bytes 7340032 | tf_op jit(solution)/shard_map/gram/pallas_call | solution.py:209
  35.6 1.5 %collective-permute-done.13.refs_1_ = bf16[384,256]{1,0:T(8,128)(2,1)S(1)} collective-permute-done((bf16[384,256]{1,0:T(8,128)(2,1)S(1)}, bf16[384,256]{1,0:T(8,128)(2,1)S(1)}, u32[]{:S(2)}, u32[]{:S(2)}) %collective-permute-start.13) | collective-permute-done | bytes 196640 | tf_op jit(solution)/shard_map/ppermute | solution.py:35
  37.1 0.3 collective-permute-start.14
  37.4 0.0 collective-permute-done.10.refs_0_
  37.4 1.7 %collective-permute-start.11 = (bf16[384,256]{1,0:T(8,128)(2,1)S(1)}, bf16[384,256]{1,0:T(8,128)(2,1)S(1)}, u32[]{:S(2)}, u32[]{:S(2)}) collective-permute-start(bf16[384,256]{1,0:T(8,128)(2,1)S(1)} %collective-permute-done.10.refs_0_), channel_id=1, source_target_pairs={{0,2},{2,4},{4,6},{6,7},{7,5},{5,3},{3,1},{1,0},{8,10},{10,12},{12... | collective-permute-start | bytes 589832 | tf_op jit(solution)/shard_map/ppermute | solution.py:35
  39.1 2.8 %gram.6 = (f32[4,256,512]{2,1,0:T(8,128)S(1)}, f32[256,256]{1,0:T(8,128)S(1)}, bf16[384,2048]{1,0:T(8,128)(2,1)S(1)}, bf16[384,2048]{1,0:T(8,128)(2,1)S(1)}) custom-call(s32[7]{0:T(128)S(1)} %stack.31.place_ref, f32[8,384]{1,0:T(8,128)S(1)} %reshape.6.lower_ref, f32[8,384]{1,0:T(8,128)S(1)} %reshape.7.upper_ref, ...), custom_call_target="tpu_custom_call", output_to_operand_aliasing={{0}: (8, {}), {1}: (9, {})} | custom-call | flops 805306368 | bytes 7340032 | tf_op jit(solution)/shard_map/gram/pallas_call | solution.py:209
  41.9 1.1 %collective-permute-done.14.refs_1_ = bf16[384,256]{1,0:T(8,128)(2,1)S(1)} collective-permute-done((bf16[384,256]{1,0:T(8,128)(2,1)S(1)}, bf16[384,256]{1,0:T(8,128)(2,1)S(1)}, u32[]{:S(2)}, u32[]{:S(2)}) %collective-permute-start.14) | collective-permute-done | bytes 196640 | tf_op jit(solution)/shard_map/ppermute | solution.py:35
  43.0 0.1 collective-permute-start.16
  43.1 0.0 collective-permute-done.11.refs_0_
  43.1 2.2 %collective-permute-start.15 = (bf16[192,256]{1,0:T(8,128)(2,1)S(1)}, bf16[192,256]{1,0:T(8,128)(2,1)S(1)}, u32[]{:S(2)}, u32[]{:S(2)}) collective-permute-start(bf16[192,256]{1,0:T(8,128)(2,1)S(1)} %slice.8), channel_id=1, source_target_pairs={{0,2},{2,4},{4,6},{6,7},{7,5},{5,3},{3,1},{1,0},{8,10},{10,12},{12... | collective-permute-start | bytes 294920 | tf_op jit(solution)/shard_map/ppermute | solution.py:35
  45.3 2.8 %gram.7 = (f32[4,256,512]{2,1,0:T(8,128)S(1)}, f32[256,256]{1,0:T(8,128)S(1)}, bf16[384,2048]{1,0:T(8,128)(2,1)S(1)}) custom-call(s32[7]{0:T(128)S(1)} %stack.31.place_ref, f32[8,384]{1,0:T(8,128)S(1)} %reshape.6.lower_ref, f32[8,384]{1,0:T(8,128)S(1)} %reshape.7.upper_ref, ...), custom_call_target="tpu_custom_call", output_to_operand_aliasing={{0}: (8, {}), {1}: (9, {})} | custom-call | flops 805306368 | bytes 7340032 | tf_op jit(solution)/shard_map/gram/pallas_call | solution.py:209
  48.1 0.0 collective-permute-done.16.bottom_ref
  48.1 0.0 collective-permute-done.15.top_ref
  48.1 1.1 %last.1 = (f32[1,128,512]{2,1,0:T(8,128)S(1)}, f32[1,128,512]{2,1,0:T(8,128)S(1)}, f32[1,128,512]{2,1,0:T(8,128)S(1)}, f32[1,128,512]{2,1,0:T(8,128)S(1)}, f32[1...) custom-call(s32[7]{0:T(128)S(1)} %stack.31.place_ref, f32[8,384]{1,0:T(8,128)S(1)} %reshape.6.lower_ref, ...), custom_call_target="tpu_custom_call" | custom-call | flops 201326592 | bytes 2097152 | tf_op jit(solution)/shard_map/last/pallas_call | solution.py:271
  49.2 0.1 collective-permute-start.17
  49.3 0.5 collective-permute-start.21
  49.8 1.0 %rest.1 = (f32[1,256,512]{2,1,0:T(8,128)S(1)}, f32[1,256,512]{2,1,0:T(8,128)S(1)}) custom-call(s32[7]{0:T(128)S(1)} %stack.31.place_ref, bf16[256,384]{1,0:T(8,128)(2,1)S(1)} %get-tuple-element.94.weighted_ref, bf16[384,2048]{1,0:T(8,128)(2,1)S(1)} %get-tuple-element.89.tile_ref, f32[4,256,512]{2,1,0:T(8,128)S(1)} %get-tuple-element.90.refs_0_.gram_ref), custom_call_target="tpu_custom_call" | custom-call | flops 201326592 | bytes 2097152 | tf_op jit(solution)/shard_map/rest/pallas_call | solution.py:281
  50.8 0.0 collective-permute-done.17
  50.8 0.1 collective-permute-start.20
  51.0 0.4 collective-permute-start.23
  51.4 1.5 %collective-permute-start.18 = (f32[192,128]{1,0:T(8,128)S(1)}, f32[192,128]{1,0:T(8,128)S(1)}, u32[]{:S(2)}, u32[]{:S(2)}) collective-permute-start(f32[192,128]{1,0:T(8,128)S(1)} %add.78), channel_id=1, source_target_pairs={{0,16},{1,17},{2,18},{3,19},{4,20},{5,21},{6,22},{7,23},{8,24},{9,... | collective-permute-start | bytes 294920 | tf_op jit(solution)/shard_map/ppermute | solution.py:42
  52.9 0.0 collective-permute-done.21
  53.0 0.6 collective-permute-start.22
  53.6 1.6 %collective-permute-start.24 = (f32[1,128,512]{2,1,0:T(8,128)S(1)}, f32[1,128,512]{2,1,0:T(8,128)S(1)}, u32[]{:S(2)}, u32[]{:S(2)}) collective-permute-start(f32[1,128,512]{2,1,0:T(8,128)S(1)} %add.81), channel_id=1, source_target_pairs={{0,16},{1,17},{2,18},{3,19},{4,20},{5,21},{6,22},{7,23},{8,24},{9,... | collective-permute-start | bytes 786440 | tf_op jit(solution)/shard_map/ppermute | solution.py:42
  55.2 1.7 %collective-permute-done.18 = f32[192,128]{1,0:T(8,128)S(1)} collective-permute-done((f32[192,128]{1,0:T(8,128)S(1)}, f32[192,128]{1,0:T(8,128)S(1)}, u32[]{:S(2)}, u32[]{:S(2)}) %collective-permute-start.18) | collective-permute-done | bytes 98336 | tf_op jit(solution)/shard_map/ppermute | solution.py:42
  57.0 0.1 collective-permute-start.19
  57.0 1.3 %collective-permute-done.19.other_ref = f32[192,128]{1,0:T(8,128)S(1)} collective-permute-done((f32[192,128]{1,0:T(8,128)S(1)}, f32[192,128]{1,0:T(8,128)S(1)}, u32[]{:S(2)}, u32[]{:S(2)}) %collective-permute-start.19) | collective-permute-done | bytes 98336 | tf_op jit(solution)/shard_map/ppermute | solution.py:42
  58.3 8.2 %invert.1.inverse_ref = f32[256,256]{1,0:T(8,128)S(1)} custom-call(s32[7]{0:T(128)S(1)} %stack.31.place_ref, f32[192,128]{1,0:T(8,128)S(1)} %add.79.mine_ref, f32[192,128]{1,0:T(8,128)S(1)} %collective-permute-done.19.other_ref), custom_call_target="tpu_custom_call" | custom-call | flops 1000000000 | bytes 524288 | tf_op jit(solution)/shard_map/invert/pallas_call | solution.py:134
  66.5 0.0 collective-permute-done.20.refs_1_.refs_2_
  66.5 0.6 transform.2.refs_0_
  67.2 0.3 collective-permute-done.24.refs_3_
  67.4 1.2 %transform.3 = f32[512,256]{1,0:T(8,128)} custom-call(f32[256,256]{1,0:T(8,128)S(1)} %invert.1.inverse_ref, f32[512,256]{1,0:T(8,128)S(1)} %transform.2.refs_0_, f32[1,256,512]{2,1,0:T(8,128)S(1)} %get-tuple-element.97.refs_0_.refs_1_, f32[1,256,512]{2,1,0:T(8,128)S(1)} %collective-permute-done.20.refs_1_.refs_2_, ...), custom_call_target="tpu_custom_call" | custom-call | flops 201326592 | bytes 1048576 | tf_op jit(solution)/shard_map/transform/pallas_call | solution.py:314
  (12 shorter events, 0.1 us)
Async XLA Ops:
  2.2 23.5 %copy-start = (f32[3072]{0:T(1024)S(1)}, f32[3072]{0:T(1024)}, u32[]{:S(2)}) copy-start(f32[3072]{0:T(1024)} %param.4) | copy-start | bytes 36868
  2.2 23.5 %copy-start.1 = (f32[3072]{0:T(1024)S(1)}, f32[3072]{0:T(1024)}, u32[]{:S(2)}) copy-start(f32[3072]{0:T(1024)} %param.5) | copy-start | bytes 36868
  2.2 9.2 %collective-permute-start.1 = (bf16[384,256]{1,0:T(8,128)(2,1)S(1)}, bf16[384,256]{1,0:T(8,128)(2,1)S(1)}, u32[]{:S(2)}, u32[]{:S(2)}) collective-permute-start(bf16[384,256]{1,0:T(8,128)(2,1)S(1)} %get-tuple-element.56), channel_id=1, source_target_pairs={{0,2},{8,9},{16,18},{24,25}} | collective-permute-start | bytes 589832 | tf_op jit(solution)/shard_map/ppermute | solution.py:348
  5.7 7.0 %collective-permute-start.2 = (bf16[384,256]{1,0:T(8,128)(2,1)S(1)}, bf16[384,256]{1,0:T(8,128)(2,1)S(1)}, u32[]{:S(2)}, u32[]{:S(2)}) collective-permute-start(bf16[384,256]{1,0:T(8,128)(2,1)S(1)} %get-tuple-element.57), channel_id=1, source_target_pairs={{0,1},{8,10},{16,17},{24,26}} | collective-permute-start | bytes 589832 | tf_op jit(solution)/shard_map/ppermute | solution.py:348
  7.0 9.6 %collective-permute-start.4 = (bf16[384,256]{1,0:T(8,128)(2,1)S(1)}, bf16[384,256]{1,0:T(8,128)(2,1)S(1)}, u32[]{:S(2)}, u32[]{:S(2)}) collective-permute-start(bf16[384,256]{1,0:T(8,128)(2,1)S(1)} %get-tuple-element.58), channel_id=1, source_target_pairs={{0,4},{8,9},{16,20},{24,25}} | collective-permute-start | bytes 589832 | tf_op jit(solution)/shard_map/ppermute | solution.py:348
  8.3 9.0 %collective-permute-start.5 = (bf16[384,256]{1,0:T(8,128)(2,1)S(1)}, bf16[384,256]{1,0:T(8,128)(2,1)S(1)}, u32[]{:S(2)}, u32[]{:S(2)}) collective-permute-start(bf16[384,256]{1,0:T(8,128)(2,1)S(1)} %get-tuple-element.59), channel_id=1, source_target_pairs={{0,1},{8,12},{16,17},{24,28}} | collective-permute-start | bytes 589832 | tf_op jit(solution)/shard_map/ppermute | solution.py:348
  9.6 9.7 %collective-permute-start = (bf16[384,256]{1,0:T(8,128)(2,1)S(1)}, bf16[384,256]{1,0:T(8,128)(2,1)S(1)}, u32[]{:S(2)}, u32[]{:S(2)}) collective-permute-start(bf16[384,256]{1,0:T(8,128)(2,1)S(1)} %get-tuple-element.55), channel_id=1, source_target_pairs={{0,7},{8,15},{16,23},{24,31}} | collective-permute-start | bytes 589832 | tf_op jit(solution)/shard_map/ppermute | solution.py:35
  11.4 12.1 %collective-permute-start.7 = (bf16[384,256]{1,0:T(8,128)(2,1)S(1)}, bf16[384,256]{1,0:T(8,128)(2,1)S(1)}, u32[]{:S(2)}, u32[]{:S(2)}) collective-permute-start(bf16[384,256]{1,0:T(8,128)(2,1)S(1)} %get-tuple-element.60), channel_id=1, source_target_pairs={{0,6},{8,9},{16,22},{24,25}} | collective-permute-start | bytes 589832 | tf_op jit(solution)/shard_map/ppermute | solution.py:348
  12.7 10.8 %collective-permute-start.8 = (bf16[384,256]{1,0:T(8,128)(2,1)S(1)}, bf16[384,256]{1,0:T(8,128)(2,1)S(1)}, u32[]{:S(2)}, u32[]{:S(2)}) collective-permute-start(bf16[384,256]{1,0:T(8,128)(2,1)S(1)} %get-tuple-element.61), channel_id=1, source_target_pairs={{0,1},{8,14},{16,17},{24,30}} | collective-permute-start | bytes 589832 | tf_op jit(solution)/shard_map/ppermute | solution.py:348
  16.7 6.9 %collective-permute-start.3 = (bf16[384,256]{1,0:T(8,128)(2,1)S(1)}, bf16[384,256]{1,0:T(8,128)(2,1)S(1)}, u32[]{:S(2)}, u32[]{:S(2)}) collective-permute-start(bf16[384,256]{1,0:T(8,128)(2,1)S(1)} %add.70), channel_id=1, source_target_pairs={{1,5},{9,13},{17,21},{25,29}} | collective-permute-start | bytes 589832 | tf_op jit(solution)/shard_map/ppermute | solution.py:35
  17.4 6.1 %collective-permute-start.6 = (bf16[384,256]{1,0:T(8,128)(2,1)S(1)}, bf16[384,256]{1,0:T(8,128)(2,1)S(1)}, u32[]{:S(2)}, u32[]{:S(2)}) collective-permute-start(bf16[384,256]{1,0:T(8,128)(2,1)S(1)} %add.73), channel_id=1, source_target_pairs={{1,3},{9,11},{17,19},{25,27}} | collective-permute-start | bytes 589832 | tf_op jit(solution)/shard_map/ppermute | solution.py:35
  23.6 7.1 %collective-permute-start.12 = (bf16[384,256]{1,0:T(8,128)(2,1)S(1)}, bf16[384,256]{1,0:T(8,128)(2,1)S(1)}, u32[]{:S(2)}, u32[]{:S(2)}) collective-permute-start(bf16[384,256]{1,0:T(8,128)(2,1)S(1)} %add_add_fusion.refs_0_), channel_id=1, source_target_pairs={{2,0},{4,2},{6,4},{7,6},{5,7},{3,5},{1,3},{0,1},{10,8},{12,10},{14... | collective-permute-start | bytes 589832 | tf_op jit(solution)/shard_map/ppermute | solution.py:35
  25.2 6.1 %collective-permute-start.9 = (bf16[384,256]{1,0:T(8,128)(2,1)S(1)}, bf16[384,256]{1,0:T(8,128)(2,1)S(1)}, u32[]{:S(2)}, u32[]{:S(2)}) collective-permute-start(bf16[384,256]{1,0:T(8,128)(2,1)S(1)} %add_add_fusion.refs_0_), channel_id=1, source_target_pairs={{0,2},{2,4},{4,6},{6,7},{7,5},{5,3},{3,1},{1,0},{8,10},{10,12},{12... | collective-permute-start | bytes 589832 | tf_op jit(solution)/shard_map/ppermute | solution.py:35
  30.8 6.3 %collective-permute-start.13 = (bf16[384,256]{1,0:T(8,128)(2,1)S(1)}, bf16[384,256]{1,0:T(8,128)(2,1)S(1)}, u32[]{:S(2)}, u32[]{:S(2)}) collective-permute-start(bf16[384,256]{1,0:T(8,128)(2,1)S(1)} %collective-permute-done.12.refs_1_), channel_id=1, source_target_pairs={{2,0},{4,2},{6,4},{7,6},{5,7},{3,5},{1,3},{0,1},{10,8},{12,10},{14... | collective-permute-start | bytes 589832 | tf_op jit(solution)/shard_map/ppermute | solution.py:35
  31.3 6.0 %collective-permute-start.10 = (bf16[384,256]{1,0:T(8,128)(2,1)S(1)}, bf16[384,256]{1,0:T(8,128)(2,1)S(1)}, u32[]{:S(2)}, u32[]{:S(2)}) collective-permute-start(bf16[384,256]{1,0:T(8,128)(2,1)S(1)} %collective-permute-done.9.refs_0_), channel_id=1, source_target_pairs={{0,2},{2,4},{4,6},{6,7},{7,5},{5,3},{3,1},{1,0},{8,10},{10,12},{12... | collective-permute-start | bytes 589832 | tf_op jit(solution)/shard_map/ppermute | solution.py:35
  37.1 5.9 %collective-permute-start.14 = (bf16[384,256]{1,0:T(8,128)(2,1)S(1)}, bf16[384,256]{1,0:T(8,128)(2,1)S(1)}, u32[]{:S(2)}, u32[]{:S(2)}) collective-permute-start(bf16[384,256]{1,0:T(8,128)(2,1)S(1)} %collective-permute-done.13.refs_1_), channel_id=1, source_target_pairs={{2,0},{4,2},{6,4},{7,6},{5,7},{3,5},{1,3},{0,1},{10,8},{12,10},{14... | collective-permute-start | bytes 589832 | tf_op jit(solution)/shard_map/ppermute | solution.py:35
  37.4 5.7 %collective-permute-start.11 = (bf16[384,256]{1,0:T(8,128)(2,1)S(1)}, bf16[384,256]{1,0:T(8,128)(2,1)S(1)}, u32[]{:S(2)}, u32[]{:S(2)}) collective-permute-start(bf16[384,256]{1,0:T(8,128)(2,1)S(1)} %collective-permute-done.10.refs_0_), channel_id=1, source_target_pairs={{0,2},{2,4},{4,6},{6,7},{7,5},{5,3},{3,1},{1,0},{8,10},{10,12},{12... | collective-permute-start | bytes 589832 | tf_op jit(solution)/shard_map/ppermute | solution.py:35
  43.0 5.1 %collective-permute-start.16 = (bf16[192,256]{1,0:T(8,128)(2,1)S(1)}, bf16[192,256]{1,0:T(8,128)(2,1)S(1)}, u32[]{:S(2)}, u32[]{:S(2)}) collective-permute-start(bf16[192,256]{1,0:T(8,128)(2,1)S(1)} %slice.7), channel_id=1, source_target_pairs={{2,0},{4,2},{6,4},{7,6},{5,7},{3,5},{1,3},{0,1},{10,8},{12,10},{14... | collective-permute-start | bytes 294920 | tf_op jit(solution)/shard_map/ppermute | solution.py:35
  43.1 5.0 %collective-permute-start.15 = (bf16[192,256]{1,0:T(8,128)(2,1)S(1)}, bf16[192,256]{1,0:T(8,128)(2,1)S(1)}, u32[]{:S(2)}, u32[]{:S(2)}) collective-permute-start(bf16[192,256]{1,0:T(8,128)(2,1)S(1)} %slice.8), channel_id=1, source_target_pairs={{0,2},{2,4},{4,6},{6,7},{7,5},{5,3},{3,1},{1,0},{8,10},{10,12},{12... | collective-permute-start | bytes 294920 | tf_op jit(solution)/shard_map/ppermute | solution.py:35
  49.2 1.6 %collective-permute-start.17 = (f32[192,128]{1,0:T(8,128)S(1)}, f32[192,128]{1,0:T(8,128)S(1)}, u32[]{:S(2)}, u32[]{:S(2)}) collective-permute-start(f32[192,128]{1,0:T(8,128)S(1)} %get-tuple-element.93), channel_id=1, source_target_pairs={{0,8},{1,9},{2,10},{3,11},{4,12},{5,13},{6,14},{7,15},{8,0},{9,1},... | collective-permute-start | bytes 294920 | tf_op jit(solution)/shard_map/ppermute | solution.py:42
  49.3 3.6 %collective-permute-start.21 = (f32[1,128,512]{2,1,0:T(8,128)S(1)}, f32[1,128,512]{2,1,0:T(8,128)S(1)}, u32[]{:S(2)}, u32[]{:S(2)}) collective-permute-start(f32[1,128,512]{2,1,0:T(8,128)S(1)} %get-tuple-element.100), channel_id=1, source_target_pairs={{0,8},{1,9},{2,10},{3,11},{4,12},{5,13},{6,14},{7,15},{8,0},{9,1},... | collective-permute-start | bytes 786440 | tf_op jit(solution)/shard_map/ppermute | solution.py:42
  50.8 15.7 %collective-permute-start.20 = (f32[1,256,512]{2,1,0:T(8,128)S(1)}, f32[1,256,512]{2,1,0:T(8,128)S(1)}, u32[]{:S(2)}, u32[]{:S(2)}) collective-permute-start(f32[1,256,512]{2,1,0:T(8,128)S(1)} %get-tuple-element.98), channel_id=1, source_target_pairs={{0,8},{1,9},{2,10},{3,11},{4,12},{5,13},{6,14},{7,15},{8,0},{9,1},... | collective-permute-start | bytes 1572872 | tf_op jit(solution)/shard_map/ppermute | solution.py:42
  51.0 2.6 %collective-permute-start.23 = (f32[1,128,512]{2,1,0:T(8,128)S(1)}, f32[1,128,512]{2,1,0:T(8,128)S(1)}, u32[]{:S(2)}, u32[]{:S(2)}) collective-permute-start(f32[1,128,512]{2,1,0:T(8,128)S(1)} %get-tuple-element.102), channel_id=1, source_target_pairs={{0,8},{1,9},{2,10},{3,11},{4,12},{5,13},{6,14},{7,15},{8,0},{9,1},... | collective-permute-start | bytes 786440 | tf_op jit(solution)/shard_map/ppermute | solution.py:42
  51.4 5.5 %collective-permute-start.18 = (f32[192,128]{1,0:T(8,128)S(1)}, f32[192,128]{1,0:T(8,128)S(1)}, u32[]{:S(2)}, u32[]{:S(2)}) collective-permute-start(f32[192,128]{1,0:T(8,128)S(1)} %add.78), channel_id=1, source_target_pairs={{0,16},{1,17},{2,18},{3,19},{4,20},{5,21},{6,22},{7,23},{8,24},{9,... | collective-permute-start | bytes 294920 | tf_op jit(solution)/shard_map/ppermute | solution.py:42
  53.0 13.5 %collective-permute-start.22 = (f32[1,128,512]{2,1,0:T(8,128)S(1)}, f32[1,128,512]{2,1,0:T(8,128)S(1)}, u32[]{:S(2)}, u32[]{:S(2)}) collective-permute-start(f32[1,128,512]{2,1,0:T(8,128)S(1)} %add.80), channel_id=1, source_target_pairs={{0,16},{1,17},{2,18},{3,19},{4,20},{5,21},{6,22},{7,23},{8,24},{9,... | collective-permute-start | bytes 786440 | tf_op jit(solution)/shard_map/ppermute | solution.py:42
  53.6 13.8 %collective-permute-start.24 = (f32[1,128,512]{2,1,0:T(8,128)S(1)}, f32[1,128,512]{2,1,0:T(8,128)S(1)}, u32[]{:S(2)}, u32[]{:S(2)}) collective-permute-start(f32[1,128,512]{2,1,0:T(8,128)S(1)} %add.81), channel_id=1, source_target_pairs={{0,16},{1,17},{2,18},{3,19},{4,20},{5,21},{6,22},{7,23},{8,24},{9,... | collective-permute-start | bytes 786440 | tf_op jit(solution)/shard_map/ppermute | solution.py:42
  57.0 1.4 %collective-permute-start.19 = (f32[192,128]{1,0:T(8,128)S(1)}, f32[192,128]{1,0:T(8,128)S(1)}, u32[]{:S(2)}, u32[]{:S(2)}) collective-permute-start(f32[192,128]{1,0:T(8,128)S(1)} %add.79.mine_ref), channel_id=1, source_target_pairs={{0,8},{1,9},{2,10},{3,11},{4,12},{5,13},{6,14},{7,15},{8,0},{9,1},... | collective-permute-start | bytes 294920 | tf_op jit(solution)/shard_map/ppermute | solution.py:42

commit v5 on v4

--- a/solution.py
+++ b/solution.py
@@ -377,7 +377,9 @@
     mine = mine + swap(other, 1)
     away = [x + swap(y, 1) for x, y in zip(first, thirds)]
     mine, second = lax.optimization_barrier((mine, second))
-    part, came, second = swap(mine, 2), [swap(x, 2) for x in away], swap(second, 1)
+    part, away_last = swap(mine, 2), away.pop()
+    away_last, second = lax.optimization_barrier((away_last, second))
+    came, second = [swap(x, 2) for x in (*away, away_last)], swap(second, 1)
     mine, bit = mine + part, 4
     while bit < shares:
         mine = mine + swap(mine, bit)

time: 69 us -> 69.1 us (level)
  transfers between devices with their start and end apart: 25 -> 25, of which waited for: 9 -> 10; matrix products, arithmetic and copies ran while one was open for 0% -> 0% of each run, Pallas kernels for 31% -> 31%
where the time goes in v5:
time: 69.1 us; the launch traced here: 68.8 us
  starting transfers between devices  28.6 us (41%)
  Pallas kernels  25.7 us (37%)
  waiting for transfers between devices  13.7 us (20%)
    ppermute x6, starting transfers between devices, on_device(): lax.ppermute(pieces[2 * i + k], ('rxn', 'col'), [(r * columns, r * column...  12.6 us
    pallas_call x4, Pallas kernels, add_gram(): pl.pallas_call(functools.partial(gram_kernel, offsets, later, float(total...  11.5 us
    ppermute x11, starting transfers between devices, to_column(): return lax.ppermute(value, 'col', pairs)  11.3 us
    pallas_call x1, Pallas kernels, invert(): pl.pallas_call(invert_kernel, out_shape=jax.ShapeDtypeStruct((PANEL, PANE...  8.17 us
    ppermute x11, waiting for transfers between devices, to_column(): return lax.ppermute(value, 'col', pairs)  5.9 us
    ppermute x8, starting transfers between devices, swap(): return lax.ppermute(value, ('rxn', 'col'), pairs)  4.74 us
    ppermute x6, waiting for transfers between devices, on_device(): lax.ppermute(pieces[2 * i + k], ('rxn', 'col'), [(r * columns, r * column...  4.23 us
    ppermute x8, waiting for transfers between devices, swap(): return lax.ppermute(value, ('rxn', 'col'), pairs)  3.62 us
  transfers between devices with their start and end apart: 25, of which 10 were waited for; matrix products, arithmetic and copies ran while one was open for 0% of the time, Pallas kernels for 31%

profile of v5, /device:TPU:0, one launch (start us, length us, event | category | flops | bytes accessed | tf_op | source)
XLA Modules:
  0.0 68.8 jit_solution(7146981200593706698)
XLA Ops:
  0.0 0.1 stack.31.place_ref
  0.1 2.1 %cut_panel.1 = (bf16[384,256]{1,0:T(8,128)(2,1)S(1)}, bf16[384,256]{1,0:T(8,128)(2,1)S(1)}, bf16[384,256]{1,0:T(8,128)(2,1)S(1)}, bf16[384,256]{1,0:T(8,128)(2,1...) custom-call(s32[7]{0:T(128)S(1)} %stack.31.place_ref, ...), custom_call_target="tpu_custom_call" | custom-call | tf_op jit(solution)/shard_map/cut_panel/pallas_call | solution.py:66
  2.2 0.0 copy-start
  2.2 0.0 copy-start.1
  2.2 3.5 %collective-permute-start.1 = (bf16[384,256]{1,0:T(8,128)(2,1)S(1)}, bf16[384,256]{1,0:T(8,128)(2,1)S(1)}, u32[]{:S(2)}, u32[]{:S(2)}) collective-permute-start(bf16[384,256]{1,0:T(8,128)(2,1)S(1)} %get-tuple-element.58), channel_id=1, source_target_pairs={{0,2},{8,9},{16,18},{24,25}} | collective-permute-start | bytes 589832 | tf_op jit(solution)/shard_map/ppermute | solution.py:348
  5.7 1.3 %collective-permute-start.2 = (bf16[384,256]{1,0:T(8,128)(2,1)S(1)}, bf16[384,256]{1,0:T(8,128)(2,1)S(1)}, u32[]{:S(2)}, u32[]{:S(2)}) collective-permute-start(bf16[384,256]{1,0:T(8,128)(2,1)S(1)} %get-tuple-element.59), channel_id=1, source_target_pairs={{0,1},{8,10},{16,17},{24,26}} | collective-permute-start | bytes 589832 | tf_op jit(solution)/shard_map/ppermute | solution.py:348
  7.0 1.3 %collective-permute-start.4 = (bf16[384,256]{1,0:T(8,128)(2,1)S(1)}, bf16[384,256]{1,0:T(8,128)(2,1)S(1)}, u32[]{:S(2)}, u32[]{:S(2)}) collective-permute-start(bf16[384,256]{1,0:T(8,128)(2,1)S(1)} %get-tuple-element.60), channel_id=1, source_target_pairs={{0,4},{8,9},{16,20},{24,25}} | collective-permute-start | bytes 589832 | tf_op jit(solution)/shard_map/ppermute | solution.py:348
  8.3 1.3 %collective-permute-start.5 = (bf16[384,256]{1,0:T(8,128)(2,1)S(1)}, bf16[384,256]{1,0:T(8,128)(2,1)S(1)}, u32[]{:S(2)}, u32[]{:S(2)}) collective-permute-start(bf16[384,256]{1,0:T(8,128)(2,1)S(1)} %get-tuple-element.61), channel_id=1, source_target_pairs={{0,1},{8,12},{16,17},{24,28}} | collective-permute-start | bytes 589832 | tf_op jit(solution)/shard_map/ppermute | solution.py:348
  9.6 1.7 %collective-permute-start = (bf16[384,256]{1,0:T(8,128)(2,1)S(1)}, bf16[384,256]{1,0:T(8,128)(2,1)S(1)}, u32[]{:S(2)}, u32[]{:S(2)}) collective-permute-start(bf16[384,256]{1,0:T(8,128)(2,1)S(1)} %get-tuple-element.57), channel_id=1, source_target_pairs={{0,7},{8,15},{16,23},{24,31}} | collective-permute-start | bytes 589832 | tf_op jit(solution)/shard_map/ppermute | solution.py:35
  11.4 0.0 collective-permute-done.1
  11.4 1.3 %collective-permute-start.7 = (bf16[384,256]{1,0:T(8,128)(2,1)S(1)}, bf16[384,256]{1,0:T(8,128)(2,1)S(1)}, u32[]{:S(2)}, u32[]{:S(2)}) collective-permute-start(bf16[384,256]{1,0:T(8,128)(2,1)S(1)} %get-tuple-element.62), channel_id=1, source_target_pairs={{0,6},{8,9},{16,22},{24,25}} | collective-permute-start | bytes 589832 | tf_op jit(solution)/shard_map/ppermute | solution.py:348
  12.7 0.0 collective-permute-done.2
  12.7 3.9 %collective-permute-start.8 = (bf16[384,256]{1,0:T(8,128)(2,1)S(1)}, bf16[384,256]{1,0:T(8,128)(2,1)S(1)}, u32[]{:S(2)}, u32[]{:S(2)}) collective-permute-start(bf16[384,256]{1,0:T(8,128)(2,1)S(1)} %get-tuple-element.63), channel_id=1, source_target_pairs={{0,1},{8,14},{16,17},{24,30}} | collective-permute-start | bytes 589832 | tf_op jit(solution)/shard_map/ppermute | solution.py:348
  16.6 0.1 add.70
  16.6 0.0 collective-permute-done.4
  16.7 0.7 collective-permute-start.3
  17.3 0.0 collective-permute-done.5
  17.3 0.1 add.73
  17.4 0.7 collective-permute-start.6
  18.1 1.2 %collective-permute-done = bf16[384,256]{1,0:T(8,128)(2,1)S(1)} collective-permute-done((bf16[384,256]{1,0:T(8,128)(2,1)S(1)}, bf16[384,256]{1,0:T(8,128)(2,1)S(1)}, u32[]{:S(2)}, u32[]{:S(2)}) %collective-permute-start) | collective-permute-done | bytes 196640 | tf_op jit(solution)/shard_map/ppermute | solution.py:35
  19.3 4.2 %collective-permute-done.7 = bf16[384,256]{1,0:T(8,128)(2,1)S(1)} collective-permute-done((bf16[384,256]{1,0:T(8,128)(2,1)S(1)}, bf16[384,256]{1,0:T(8,128)(2,1)S(1)}, u32[]{:S(2)}, u32[]{:S(2)}) %collective-permute-start.7) | collective-permute-done | bytes 196640 | tf_op jit(solution)/shard_map/ppermute | solution.py:348
  23.5 0.0 collective-permute-done.8
  23.5 0.0 collective-permute-done.3
  23.5 0.0 collective-permute-done.6
  23.5 0.1 add_add_fusion.refs_0_
  23.6 1.6 %collective-permute-start.12 = (bf16[384,256]{1,0:T(8,128)(2,1)S(1)}, bf16[384,256]{1,0:T(8,128)(2,1)S(1)}, u32[]{:S(2)}, u32[]{:S(2)}) collective-permute-start(bf16[384,256]{1,0:T(8,128)(2,1)S(1)} %add_add_fusion.refs_0_), channel_id=1, source_target_pairs={{2,0},{4,2},{6,4},{7,6},{5,7},{3,5},{1,3},{0,1},{10,8},{12,10},{14... | collective-permute-start | bytes 589832 | tf_op jit(solution)/shard_map/ppermute | solution.py:35
  25.2 0.5 collective-permute-start.9
  25.7 3.2 %gram.4 = (f32[4,256,512]{2,1,0:T(8,128)S(1)}, f32[256,256]{1,0:T(8,128)S(1)}, bf16[384,2048]{1,0:T(8,128)(2,1)S(1)}, bf16[384,2048]{1,0:T(8,128)(2,1)S(1)}) custom-call(s32[7]{0:T(128)S(1)} %stack.31.place_ref, f32[8,384]{1,0:T(8,128)S(1)} %reshape.6.lower_ref, f32[8,384]{1,0:T(8,128)S(1)} %reshape.7.upper_ref, bf16[3072,2048]{1,0:T(8,128)(2,1)} %basis_ref.9, ...), custom_call_target="tpu_custom_call" | custom-call | flops 402653184 | bytes 5767168 | tf_op jit(solution)/shard_map/gram/pallas_call | solution.py:209
  29.0 1.8 %collective-permute-done.12.refs_1_ = bf16[384,256]{1,0:T(8,128)(2,1)S(1)} collective-permute-done((bf16[384,256]{1,0:T(8,128)(2,1)S(1)}, bf16[384,256]{1,0:T(8,128)(2,1)S(1)}, u32[]{:S(2)}, u32[]{:S(2)}) %collective-permute-start.12) | collective-permute-done | bytes 196640 | tf_op jit(solution)/shard_map/ppermute | solution.py:35
  30.8 0.3 collective-permute-start.13
  31.1 0.3 collective-permute-done.9.refs_0_
  31.3 1.5 %collective-permute-start.10 = (bf16[384,256]{1,0:T(8,128)(2,1)S(1)}, bf16[384,256]{1,0:T(8,128)(2,1)S(1)}, u32[]{:S(2)}, u32[]{:S(2)}) collective-permute-start(bf16[384,256]{1,0:T(8,128)(2,1)S(1)} %collective-permute-done.9.refs_0_), channel_id=1, source_target_pairs={{0,2},{2,4},{4,6},{6,7},{7,5},{5,3},{3,1},{1,0},{8,10},{10,12},{12... | collective-permute-start | bytes 589832 | tf_op jit(solution)/shard_map/ppermute | solution.py:35
  32.8 2.8 %gram.5 = (f32[4,256,512]{2,1,0:T(8,128)S(1)}, f32[256,256]{1,0:T(8,128)S(1)}, bf16[384,2048]{1,0:T(8,128)(2,1)S(1)}, bf16[384,2048]{1,0:T(8,128)(2,1)S(1)}) custom-call(s32[7]{0:T(128)S(1)} %stack.31.place_ref, f32[8,384]{1,0:T(8,128)S(1)} %reshape.6.lower_ref, f32[8,384]{1,0:T(8,128)S(1)} %reshape.7.upper_ref, ...), custom_call_target="tpu_custom_call", output_to_operand_aliasing={{0}: (8, {}), {1}: (9, {})} | custom-call | flops 805306368 | bytes 7340032 | tf_op jit(solution)/shard_map/gram/pallas_call | solution.py:209
  35.6 1.5 %collective-permute-done.13.refs_1_ = bf16[384,256]{1,0:T(8,128)(2,1)S(1)} collective-permute-done((bf16[384,256]{1,0:T(8,128)(2,1)S(1)}, bf16[384,256]{1,0:T(8,128)(2,1)S(1)}, u32[]{:S(2)}, u32[]{:S(2)}) %collective-permute-start.13) | collective-permute-done | bytes 196640 | tf_op jit(solution)/shard_map/ppermute | solution.py:35
  37.1 0.3 collective-permute-start.14
  37.4 0.0 collective-permute-done.10.refs_0_
  37.4 1.7 %collective-permute-start.11 = (bf16[384,256]{1,0:T(8,128)(2,1)S(1)}, bf16[384,256]{1,0:T(8,128)(2,1)S(1)}, u32[]{:S(2)}, u32[]{:S(2)}) collective-permute-start(bf16[384,256]{1,0:T(8,128)(2,1)S(1)} %collective-permute-done.10.refs_0_), channel_id=1, source_target_pairs={{0,2},{2,4},{4,6},{6,7},{7,5},{5,3},{3,1},{1,0},{8,10},{10,12},{12... | collective-permute-start | bytes 589832 | tf_op jit(solution)/shard_map/ppermute | solution.py:35
  39.1 2.8 %gram.6 = (f32[4,256,512]{2,1,0:T(8,128)S(1)}, f32[256,256]{1,0:T(8,128)S(1)}, bf16[384,2048]{1,0:T(8,128)(2,1)S(1)}, bf16[384,2048]{1,0:T(8,128)(2,1)S(1)}) custom-call(s32[7]{0:T(128)S(1)} %stack.31.place_ref, f32[8,384]{1,0:T(8,128)S(1)} %reshape.6.lower_ref, f32[8,384]{1,0:T(8,128)S(1)} %reshape.7.upper_ref, ...), custom_call_target="tpu_custom_call", output_to_operand_aliasing={{0}: (8, {}), {1}: (9, {})} | custom-call | flops 805306368 | bytes 7340032 | tf_op jit(solution)/shard_map/gram/pallas_call | solution.py:209
  41.9 1.1 %collective-permute-done.14.refs_1_ = bf16[384,256]{1,0:T(8,128)(2,1)S(1)} collective-permute-done((bf16[384,256]{1,0:T(8,128)(2,1)S(1)}, bf16[384,256]{1,0:T(8,128)(2,1)S(1)}, u32[]{:S(2)}, u32[]{:S(2)}) %collective-permute-start.14) | collective-permute-done | bytes 196640 | tf_op jit(solution)/shard_map/ppermute | solution.py:35
  43.0 0.1 collective-permute-start.16
  43.1 0.0 collective-permute-done.11.refs_0_
  43.1 2.2 %collective-permute-start.15 = (bf16[192,256]{1,0:T(8,128)(2,1)S(1)}, bf16[192,256]{1,0:T(8,128)(2,1)S(1)}, u32[]{:S(2)}, u32[]{:S(2)}) collective-permute-start(bf16[192,256]{1,0:T(8,128)(2,1)S(1)} %slice.8), channel_id=1, source_target_pairs={{0,2},{2,4},{4,6},{6,7},{7,5},{5,3},{3,1},{1,0},{8,10},{10,12},{12... | collective-permute-start | bytes 294920 | tf_op jit(solution)/shard_map/ppermute | solution.py:35
  45.3 2.8 %gram.7 = (f32[4,256,512]{2,1,0:T(8,128)S(1)}, f32[256,256]{1,0:T(8,128)S(1)}, bf16[384,2048]{1,0:T(8,128)(2,1)S(1)}) custom-call(s32[7]{0:T(128)S(1)} %stack.31.place_ref, f32[8,384]{1,0:T(8,128)S(1)} %reshape.6.lower_ref, f32[8,384]{1,0:T(8,128)S(1)} %reshape.7.upper_ref, ...), custom_call_target="tpu_custom_call", output_to_operand_aliasing={{0}: (8, {}), {1}: (9, {})} | custom-call | flops 805306368 | bytes 7340032 | tf_op jit(solution)/shard_map/gram/pallas_call | solution.py:209
  48.1 0.0 collective-permute-done.16.bottom_ref
  48.1 0.0 collective-permute-done.15.top_ref
  48.1 1.1 %last.1 = (f32[1,128,512]{2,1,0:T(8,128)S(1)}, f32[1,128,512]{2,1,0:T(8,128)S(1)}, f32[1,128,512]{2,1,0:T(8,128)S(1)}, f32[1,128,512]{2,1,0:T(8,128)S(1)}, f32[1...) custom-call(s32[7]{0:T(128)S(1)} %stack.31.place_ref, f32[8,384]{1,0:T(8,128)S(1)} %reshape.6.lower_ref, ...), custom_call_target="tpu_custom_call" | custom-call | flops 201326592 | bytes 2097152 | tf_op jit(solution)/shard_map/last/pallas_call | solution.py:271
  49.2 0.1 collective-permute-start.20
  49.3 0.5 collective-permute-start.17
  49.8 0.1 collective-permute-start.22
  49.9 1.0 %rest.1 = (f32[1,256,512]{2,1,0:T(8,128)S(1)}, f32[1,256,512]{2,1,0:T(8,128)S(1)}) custom-call(s32[7]{0:T(128)S(1)} %stack.31.place_ref, bf16[256,384]{1,0:T(8,128)(2,1)S(1)} %get-tuple-element.96.weighted_ref, bf16[384,2048]{1,0:T(8,128)(2,1)S(1)} %get-tuple-element.91.tile_ref, f32[4,256,512]{2,1,0:T(8,128)S(1)} %get-tuple-element.92.refs_0_.gram_ref), custom_call_target="tpu_custom_call" | custom-call | flops 201326592 | bytes 2097152 | tf_op jit(solution)/shard_map/rest/pallas_call | solution.py:281
  50.9 0.1 collective-permute-done.17
  51.1 0.4 collective-permute-start.21
  51.5 1.5 %collective-permute-start.18 = (f32[192,128]{1,0:T(8,128)S(1)}, f32[192,128]{1,0:T(8,128)S(1)}, u32[]{:S(2)}, u32[]{:S(2)}) collective-permute-start(f32[192,128]{1,0:T(8,128)S(1)} %add.78), channel_id=1, source_target_pairs={{0,16},{1,17},{2,18},{3,19},{4,20},{5,21},{6,22},{7,23},{8,24},{9,... | collective-permute-start | bytes 294920 | tf_op jit(solution)/shard_map/ppermute | solution.py:42
  53.0 0.0 collective-permute-done.22
  53.0 0.6 collective-permute-start.23
  53.6 1.5 %collective-permute-start.24 = (f32[1,128,512]{2,1,0:T(8,128)S(1)}, f32[1,128,512]{2,1,0:T(8,128)S(1)}, u32[]{:S(2)}, u32[]{:S(2)}) collective-permute-start(f32[1,128,512]{2,1,0:T(8,128)S(1)} %add.80), channel_id=1, source_target_pairs={{0,16},{1,17},{2,18},{3,19},{4,20},{5,21},{6,22},{7,23},{8,24},{9,... | collective-permute-start | bytes 786440 | tf_op jit(solution)/shard_map/ppermute | solution.py:42
  55.1 1.9 %collective-permute-done.18 = f32[192,128]{1,0:T(8,128)S(1)} collective-permute-done((f32[192,128]{1,0:T(8,128)S(1)}, f32[192,128]{1,0:T(8,128)S(1)}, u32[]{:S(2)}, u32[]{:S(2)}) %collective-permute-start.18) | collective-permute-done | bytes 98336 | tf_op jit(solution)/shard_map/ppermute | solution.py:42
  57.1 0.1 collective-permute-start.19
  57.2 1.3 %collective-permute-done.19.other_ref = f32[192,128]{1,0:T(8,128)S(1)} collective-permute-done((f32[192,128]{1,0:T(8,128)S(1)}, f32[192,128]{1,0:T(8,128)S(1)}, u32[]{:S(2)}, u32[]{:S(2)}) %collective-permute-start.19) | collective-permute-done | bytes 98336 | tf_op jit(solution)/shard_map/ppermute | solution.py:42
  58.5 8.2 %invert.1.inverse_ref = f32[256,256]{1,0:T(8,128)S(1)} custom-call(s32[7]{0:T(128)S(1)} %stack.31.place_ref, f32[192,128]{1,0:T(8,128)S(1)} %add.79.mine_ref, f32[192,128]{1,0:T(8,128)S(1)} %collective-permute-done.19.other_ref), custom_call_target="tpu_custom_call" | custom-call | flops 1000000000 | bytes 524288 | tf_op jit(solution)/shard_map/invert/pallas_call | solution.py:134
  66.7 0.0 collective-permute-done.21.refs_1_.refs_2_
  66.7 0.6 transform.2.refs_0_
  67.3 0.3 collective-permute-done.24.refs_3_
  67.6 1.2 %transform.3 = f32[512,256]{1,0:T(8,128)} custom-call(f32[256,256]{1,0:T(8,128)S(1)} %invert.1.inverse_ref, f32[512,256]{1,0:T(8,128)S(1)} %transform.2.refs_0_, f32[1,256,512]{2,1,0:T(8,128)S(1)} %get-tuple-element.99.refs_0_.refs_1_, f32[1,256,512]{2,1,0:T(8,128)S(1)} %collective-permute-done.21.refs_1_.refs_2_, ...), custom_call_target="tpu_custom_call" | custom-call | flops 201326592 | bytes 1048576 | tf_op jit(solution)/shard_map/transform/pallas_call | solution.py:314
  (12 shorter events, 0.1 us)
Async XLA Ops:
  2.2 23.5 %copy-start = (f32[3072]{0:T(1024)S(1)}, f32[3072]{0:T(1024)}, u32[]{:S(2)}) copy-start(f32[3072]{0:T(1024)} %param.4) | copy-start | bytes 36868
  2.2 23.5 %copy-start.1 = (f32[3072]{0:T(1024)S(1)}, f32[3072]{0:T(1024)}, u32[]{:S(2)}) copy-start(f32[3072]{0:T(1024)} %param.5) | copy-start | bytes 36868
  2.2 9.2 %collective-permute-start.1 = (bf16[384,256]{1,0:T(8,128)(2,1)S(1)}, bf16[384,256]{1,0:T(8,128)(2,1)S(1)}, u32[]{:S(2)}, u32[]{:S(2)}) collective-permute-start(bf16[384,256]{1,0:T(8,128)(2,1)S(1)} %get-tuple-element.58), channel_id=1, source_target_pairs={{0,2},{8,9},{16,18},{24,25}} | collective-permute-start | bytes 589832 | tf_op jit(solution)/shard_map/ppermute | solution.py:348
  5.7 7.0 %collective-permute-start.2 = (bf16[384,256]{1,0:T(8,128)(2,1)S(1)}, bf16[384,256]{1,0:T(8,128)(2,1)S(1)}, u32[]{:S(2)}, u32[]{:S(2)}) collective-permute-start(bf16[384,256]{1,0:T(8,128)(2,1)S(1)} %get-tuple-element.59), channel_id=1, source_target_pairs={{0,1},{8,10},{16,17},{24,26}} | collective-permute-start | bytes 589832 | tf_op jit(solution)/shard_map/ppermute | solution.py:348
  7.0 9.6 %collective-permute-start.4 = (bf16[384,256]{1,0:T(8,128)(2,1)S(1)}, bf16[384,256]{1,0:T(8,128)(2,1)S(1)}, u32[]{:S(2)}, u32[]{:S(2)}) collective-permute-start(bf16[384,256]{1,0:T(8,128)(2,1)S(1)} %get-tuple-element.60), channel_id=1, source_target_pairs={{0,4},{8,9},{16,20},{24,25}} | collective-permute-start | bytes 589832 | tf_op jit(solution)/shard_map/ppermute | solution.py:348
  8.3 9.0 %collective-permute-start.5 = (bf16[384,256]{1,0:T(8,128)(2,1)S(1)}, bf16[384,256]{1,0:T(8,128)(2,1)S(1)}, u32[]{:S(2)}, u32[]{:S(2)}) collective-permute-start(bf16[384,256]{1,0:T(8,128)(2,1)S(1)} %get-tuple-element.61), channel_id=1, source_target_pairs={{0,1},{8,12},{16,17},{24,28}} | collective-permute-start | bytes 589832 | tf_op jit(solution)/shard_map/ppermute | solution.py:348
  9.6 9.7 %collective-permute-start = (bf16[384,256]{1,0:T(8,128)(2,1)S(1)}, bf16[384,256]{1,0:T(8,128)(2,1)S(1)}, u32[]{:S(2)}, u32[]{:S(2)}) collective-permute-start(bf16[384,256]{1,0:T(8,128)(2,1)S(1)} %get-tuple-element.57), channel_id=1, source_target_pairs={{0,7},{8,15},{16,23},{24,31}} | collective-permute-start | bytes 589832 | tf_op jit(solution)/shard_map/ppermute | solution.py:35
  11.4 12.1 %collective-permute-start.7 = (bf16[384,256]{1,0:T(8,128)(2,1)S(1)}, bf16[384,256]{1,0:T(8,128)(2,1)S(1)}, u32[]{:S(2)}, u32[]{:S(2)}) collective-permute-start(bf16[384,256]{1,0:T(8,128)(2,1)S(1)} %get-tuple-element.62), channel_id=1, source_target_pairs={{0,6},{8,9},{16,22},{24,25}} | collective-permute-start | bytes 589832 | tf_op jit(solution)/shard_map/ppermute | solution.py:348
  12.7 10.8 %collective-permute-start.8 = (bf16[384,256]{1,0:T(8,128)(2,1)S(1)}, bf16[384,256]{1,0:T(8,128)(2,1)S(1)}, u32[]{:S(2)}, u32[]{:S(2)}) collective-permute-start(bf16[384,256]{1,0:T(8,128)(2,1)S(1)} %get-tuple-element.63), channel_id=1, source_target_pairs={{0,1},{8,14},{16,17},{24,30}} | collective-permute-start | bytes 589832 | tf_op jit(solution)/shard_map/ppermute | solution.py:348
  16.7 6.9 %collective-permute-start.3 = (bf16[384,256]{1,0:T(8,128)(2,1)S(1)}, bf16[384,256]{1,0:T(8,128)(2,1)S(1)}, u32[]{:S(2)}, u32[]{:S(2)}) collective-permute-start(bf16[384,256]{1,0:T(8,128)(2,1)S(1)} %add.70), channel_id=1, source_target_pairs={{1,5},{9,13},{17,21},{25,29}} | collective-permute-start | bytes 589832 | tf_op jit(solution)/shard_map/ppermute | solution.py:35
  17.4 6.1 %collective-permute-start.6 = (bf16[384,256]{1,0:T(8,128)(2,1)S(1)}, bf16[384,256]{1,0:T(8,128)(2,1)S(1)}, u32[]{:S(2)}, u32[]{:S(2)}) collective-permute-start(bf16[384,256]{1,0:T(8,128)(2,1)S(1)} %add.73), channel_id=1, source_target_pairs={{1,3},{9,11},{17,19},{25,27}} | collective-permute-start | bytes 589832 | tf_op jit(solution)/shard_map/ppermute | solution.py:35
  23.6 7.1 %collective-permute-start.12 = (bf16[384,256]{1,0:T(8,128)(2,1)S(1)}, bf16[384,256]{1,0:T(8,128)(2,1)S(1)}, u32[]{:S(2)}, u32[]{:S(2)}) collective-permute-start(bf16[384,256]{1,0:T(8,128)(2,1)S(1)} %add_add_fusion.refs_0_), channel_id=1, source_target_pairs={{2,0},{4,2},{6,4},{7,6},{5,7},{3,5},{1,3},{0,1},{10,8},{12,10},{14... | collective-permute-start | bytes 589832 | tf_op jit(solution)/shard_map/ppermute | solution.py:35
  25.2 6.1 %collective-permute-start.9 = (bf16[384,256]{1,0:T(8,128)(2,1)S(1)}, bf16[384,256]{1,0:T(8,128)(2,1)S(1)}, u32[]{:S(2)}, u32[]{:S(2)}) collective-permute-start(bf16[384,256]{1,0:T(8,128)(2,1)S(1)} %add_add_fusion.refs_0_), channel_id=1, source_target_pairs={{0,2},{2,4},{4,6},{6,7},{7,5},{5,3},{3,1},{1,0},{8,10},{10,12},{12... | collective-permute-start | bytes 589832 | tf_op jit(solution)/shard_map/ppermute | solution.py:35
  30.8 6.3 %collective-permute-start.13 = (bf16[384,256]{1,0:T(8,128)(2,1)S(1)}, bf16[384,256]{1,0:T(8,128)(2,1)S(1)}, u32[]{:S(2)}, u32[]{:S(2)}) collective-permute-start(bf16[384,256]{1,0:T(8,128)(2,1)S(1)} %collective-permute-done.12.refs_1_), channel_id=1, source_target_pairs={{2,0},{4,2},{6,4},{7,6},{5,7},{3,5},{1,3},{0,1},{10,8},{12,10},{14... | collective-permute-start | bytes 589832 | tf_op jit(solution)/shard_map/ppermute | solution.py:35
  31.3 6.0 %collective-permute-start.10 = (bf16[384,256]{1,0:T(8,128)(2,1)S(1)}, bf16[384,256]{1,0:T(8,128)(2,1)S(1)}, u32[]{:S(2)}, u32[]{:S(2)}) collective-permute-start(bf16[384,256]{1,0:T(8,128)(2,1)S(1)} %collective-permute-done.9.refs_0_), channel_id=1, source_target_pairs={{0,2},{2,4},{4,6},{6,7},{7,5},{5,3},{3,1},{1,0},{8,10},{10,12},{12... | collective-permute-start | bytes 589832 | tf_op jit(solution)/shard_map/ppermute | solution.py:35
  37.1 5.9 %collective-permute-start.14 = (bf16[384,256]{1,0:T(8,128)(2,1)S(1)}, bf16[384,256]{1,0:T(8,128)(2,1)S(1)}, u32[]{:S(2)}, u32[]{:S(2)}) collective-permute-start(bf16[384,256]{1,0:T(8,128)(2,1)S(1)} %collective-permute-done.13.refs_1_), channel_id=1, source_target_pairs={{2,0},{4,2},{6,4},{7,6},{5,7},{3,5},{1,3},{0,1},{10,8},{12,10},{14... | collective-permute-start | bytes 589832 | tf_op jit(solution)/shard_map/ppermute | solution.py:35
  37.4 5.7 %collective-permute-start.11 = (bf16[384,256]{1,0:T(8,128)(2,1)S(1)}, bf16[384,256]{1,0:T(8,128)(2,1)S(1)}, u32[]{:S(2)}, u32[]{:S(2)}) collective-permute-start(bf16[384,256]{1,0:T(8,128)(2,1)S(1)} %collective-permute-done.10.refs_0_), channel_id=1, source_target_pairs={{0,2},{2,4},{4,6},{6,7},{7,5},{5,3},{3,1},{1,0},{8,10},{10,12},{12... | collective-permute-start | bytes 589832 | tf_op jit(solution)/shard_map/ppermute | solution.py:35
  43.0 5.1 %collective-permute-start.16 = (bf16[192,256]{1,0:T(8,128)(2,1)S(1)}, bf16[192,256]{1,0:T(8,128)(2,1)S(1)}, u32[]{:S(2)}, u32[]{:S(2)}) collective-permute-start(bf16[192,256]{1,0:T(8,128)(2,1)S(1)} %slice.7), channel_id=1, source_target_pairs={{2,0},{4,2},{6,4},{7,6},{5,7},{3,5},{1,3},{0,1},{10,8},{12,10},{14... | collective-permute-start | bytes 294920 | tf_op jit(solution)/shard_map/ppermute | solution.py:35
  43.1 5.0 %collective-permute-start.15 = (bf16[192,256]{1,0:T(8,128)(2,1)S(1)}, bf16[192,256]{1,0:T(8,128)(2,1)S(1)}, u32[]{:S(2)}, u32[]{:S(2)}) collective-permute-start(bf16[192,256]{1,0:T(8,128)(2,1)S(1)} %slice.8), channel_id=1, source_target_pairs={{0,2},{2,4},{4,6},{6,7},{7,5},{5,3},{3,1},{1,0},{8,10},{10,12},{12... | collective-permute-start | bytes 294920 | tf_op jit(solution)/shard_map/ppermute | solution.py:35
  49.2 1.8 %collective-permute-start.20 = (f32[1,128,512]{2,1,0:T(8,128)S(1)}, f32[1,128,512]{2,1,0:T(8,128)S(1)}, u32[]{:S(2)}, u32[]{:S(2)}) collective-permute-start(f32[1,128,512]{2,1,0:T(8,128)S(1)} %get-tuple-element.101), channel_id=1, source_target_pairs={{0,8},{1,9},{2,10},{3,11},{4,12},{5,13},{6,14},{7,15},{8,0},{9,1},... | collective-permute-start | bytes 786440 | tf_op jit(solution)/shard_map/ppermute | solution.py:42
  49.3 1.7 %collective-permute-start.17 = (f32[192,128]{1,0:T(8,128)S(1)}, f32[192,128]{1,0:T(8,128)S(1)}, u32[]{:S(2)}, u32[]{:S(2)}) collective-permute-start(f32[192,128]{1,0:T(8,128)S(1)} %get-tuple-element.95), channel_id=1, source_target_pairs={{0,8},{1,9},{2,10},{3,11},{4,12},{5,13},{6,14},{7,15},{8,0},{9,1},... | collective-permute-start | bytes 294920 | tf_op jit(solution)/shard_map/ppermute | solution.py:42
  49.8 3.2 %collective-permute-start.22 = (f32[1,128,512]{2,1,0:T(8,128)S(1)}, f32[1,128,512]{2,1,0:T(8,128)S(1)}, u32[]{:S(2)}, u32[]{:S(2)}) collective-permute-start(f32[1,128,512]{2,1,0:T(8,128)S(1)} %get-tuple-element.105), channel_id=1, source_target_pairs={{0,8},{1,9},{2,10},{3,11},{4,12},{5,13},{6,14},{7,15},{8,0},{9,1},... | collective-permute-start | bytes 786440 | tf_op jit(solution)/shard_map/ppermute | solution.py:42
  51.1 15.6 %collective-permute-start.21 = (f32[1,256,512]{2,1,0:T(8,128)S(1)}, f32[1,256,512]{2,1,0:T(8,128)S(1)}, u32[]{:S(2)}, u32[]{:S(2)}) collective-permute-start(f32[1,256,512]{2,1,0:T(8,128)S(1)} %get-tuple-element.103), channel_id=1, source_target_pairs={{0,8},{1,9},{2,10},{3,11},{4,12},{5,13},{6,14},{7,15},{8,0},{9,1},... | collective-permute-start | bytes 1572872 | tf_op jit(solution)/shard_map/ppermute | solution.py:42
  51.5 5.6 %collective-permute-start.18 = (f32[192,128]{1,0:T(8,128)S(1)}, f32[192,128]{1,0:T(8,128)S(1)}, u32[]{:S(2)}, u32[]{:S(2)}) collective-permute-start(f32[192,128]{1,0:T(8,128)S(1)} %add.78), channel_id=1, source_target_pairs={{0,16},{1,17},{2,18},{3,19},{4,20},{5,21},{6,22},{7,23},{8,24},{9,... | collective-permute-start | bytes 294920 | tf_op jit(solution)/shard_map/ppermute | solution.py:42
  53.0 13.6 %collective-permute-start.23 = (f32[1,128,512]{2,1,0:T(8,128)S(1)}, f32[1,128,512]{2,1,0:T(8,128)S(1)}, u32[]{:S(2)}, u32[]{:S(2)}) collective-permute-start(f32[1,128,512]{2,1,0:T(8,128)S(1)} %add.81), channel_id=1, source_target_pairs={{0,16},{1,17},{2,18},{3,19},{4,20},{5,21},{6,22},{7,23},{8,24},{9,... | collective-permute-start | bytes 786440 | tf_op jit(solution)/shard_map/ppermute | solution.py:42
  53.6 14.0 %collective-permute-start.24 = (f32[1,128,512]{2,1,0:T(8,128)S(1)}, f32[1,128,512]{2,1,0:T(8,128)S(1)}, u32[]{:S(2)}, u32[]{:S(2)}) collective-permute-start(f32[1,128,512]{2,1,0:T(8,128)S(1)} %add.80), channel_id=1, source_target_pairs={{0,16},{1,17},{2,18},{3,19},{4,20},{5,21},{6,22},{7,23},{8,24},{9,... | collective-permute-start | bytes 786440 | tf_op jit(solution)/shard_map/ppermute | solution.py:42
  57.1 1.4 %collective-permute-start.19 = (f32[192,128]{1,0:T(8,128)S(1)}, f32[192,128]{1,0:T(8,128)S(1)}, u32[]{:S(2)}, u32[]{:S(2)}) collective-permute-start(f32[192,128]{1,0:T(8,128)S(1)} %add.79.mine_ref), channel_id=1, source_target_pairs={{0,8},{1,9},{2,10},{3,11},{4,12},{5,13},{6,14},{7,15},{8,0},{9,1},... | collective-permute-start | bytes 294920 | tf_op jit(solution)/shard_map/ppermute | solution.py:42
